TPU v7x, 32 devices: a whole 2x2x4 slice. The times are simulated.
32 devices in a mesh: row: 4 (over x, core), col: 8 (over z, y).
Axes of the slice: x: 2, y: 2, z: 4, core: 2. Of those that a mesh axis runs over, the one named last changes fastest.
Arguments:
- hamiltonian: float32 [64, 4, 128, 128], P(('row', 'col')), may hold values from -20 to 20
- block_lists: int32 [64, 4], replicated, may hold values from -1 to 63, as said below
Outputs:
- density: float32 [64, 4, 128, 128], P(('row', 'col'))
Inputs may be any that keep to these rules, and one draw needn't show every extreme that they name: `block_lists`: block column j = (r * 8 + c) * 2 + s sits on grid row r, grid column c, slot s. Entry 0 is j. Entry 1 is the column of the same r and s at grid column c - 1 (cyclically), entry 2 the one at c + 1, each either present or -1, present for both ends of a link or for neither. Entry 3 is never -1: the column of the same c and s on grid row r with one bit flipped, the same bit for all rows of one grid column and slot. Some columns have all four entries, some only entries 0 and 3.
All inputs are finite; a program needn't handle non-finite values.
Results may differ from a plain program's by a relative error of at most 0.0001.
Values sent between devices are 32-bit elements; how exact they have to be, the bound alone decides.
No kernel may reach another device: no remote copies, remote signals or barrier semaphores. Data moves between devices by JAX's collectives and lax.ppermute only.
A program may use at most 64 MiB of HBM per device.

v0:
```python
import functools
import jax
import jax.numpy as jnp
from jax import lax
from jax.experimental import pallas as pl
from jax.experimental.pallas import tpu as pltpu
from jax.sharding import PartitionSpec as P

ITERS = 6
STEPS = 2
SIDE = 128
HALF = SIDE // 2
PACKED = HALF + 8

epsilon = 1e-06
f32 = jnp.float32
bf16 = jnp.bfloat16


def turned(block):
    return jnp.swapaxes(block, -1, -2)


def symmetric(block):
    return 0.5 * (block + turned(block))


def split(values):
    high = values.astype(bf16)
    return high, (values - high.astype(f32)).astype(bf16)


def dot(left, right):
    return lax.dot_general(left, right, (((1,), (0,)), ((), ())), preferred_element_type=f32)


def product(left, right, rows, cols):
    left_high, left_low = left[0][rows, :], left[1][rows, :]
    right_high, right_low = right[0][:, cols], right[1][:, cols]
    return dot(
        jnp.concatenate([left_high, left_low, left_high], 1),
        jnp.concatenate([right_high, right_high, right_low], 0),
    )


def upper_tiles(order):
    tile = order // 2
    for row, col in ((0, 0), (0, 1), (1, 1)):
        yield pl.ds(row * tile, tile), pl.ds(col * tile, tile), row != col


def lanes(shape):
    return lax.broadcasted_iota(jnp.int32, shape, 1)


def rows_of(shape):
    return lax.broadcasted_iota(jnp.int32, shape, 0)


def pack(block):
    shape = (HALF, SIDE)
    lower = pltpu.roll(block[HALF:, :], HALF, 1)
    body = jnp.where(lanes(shape) < rows_of(shape), lower, block[:HALF, :])
    whole = block.shape
    diagonal = jnp.sum(jnp.where(lanes(whole) == rows_of(whole), block, 0.0), 0, keepdims=True)
    return body, jnp.broadcast_to(diagonal, (PACKED - HALF, SIDE))


def unpack(body, diagonal):
    shape = (HALF, SIDE)
    lane, row = lanes(shape), rows_of(shape)
    top = jnp.where(lane == row, 0.5 * body, jnp.where(lane < row, 0.0, body))
    rolled = pltpu.roll(body, HALF, 1)
    at = lane - HALF
    bottom = jnp.where(at == row, 0.5 * diagonal, jnp.where((at >= 0) & (at < row), rolled, 0.0))
    folded = jnp.concatenate([top, bottom], 0)
    return folded + turned(folded)


def fill(target, slot, face, packed):
    target[slot, pl.ds(0, SIDE), :] = face
    if packed is not None:
        target[slot, pl.ds(SIDE, HALF), :] = packed[0]
        target[slot, pl.ds(SIDE + HALF, PACKED - HALF), :] = packed[1]


def pack_kernel(own, to_right, to_left, to_partner):
    for slot in range(own.shape[0]):
        packed = pack(symmetric(own[slot, 0]))
        fill(to_right, slot, own[slot, 2], packed)
        fill(to_left, slot, own[slot, 1], packed)
        fill(to_partner, slot, own[slot, 3], packed)


def my_links(lists, cols, slots):
    my_row = lax.axis_index("row")
    device = my_row * cols + lax.axis_index("col")
    links = []
    for slot in range(slots):
        column = device * slots + slot
        present = [jnp.where(lists[column, k] >= 0, 1.0, 0.0).astype(f32) for k in range(4)]
        partner_row = lists[column, 3] // (slots * cols)
        links.append((present, jnp.bitwise_xor(my_row, partner_row)))
    return links


def neighbour_parts(slot, bit, received, with_diagonals):
    from_left, from_right = received[:2]
    from_rows = received[2:]

    def read(first, count):
        span = pl.ds(first, count)
        partner = from_rows[0][slot, span, :]
        for place in range(1, len(from_rows)):
            partner = jnp.where(bit == (1 << place), from_rows[place][slot, span, :], partner)
        return from_left[slot, span, :], from_right[slot, span, :], partner

    faces = read(0, SIDE)
    if not with_diagonals:
        return faces, None
    bodies = read(SIDE, HALF)
    diagonals = read(SIDE + HALF, PACKED - HALF)
    return faces, [unpack(b, d[0:1, :]) for b, d in zip(bodies, diagonals)]


def assemble_kernel(cols, members, has_base, *refs):
    lists, own = refs[:2]
    base = refs[2] if has_base else None
    received = refs[2 + has_base : -7]
    blocks, cube, norms, s_high, s_low, q_high, q_low = refs[-7:]
    slots = own.shape[0]
    order = members * SIDE
    top = None
    links = my_links(lists, cols, slots)
    for slot in range(slots):
        present, bit = links[slot]
        faces, diagonals = neighbour_parts(slot, bit, received, True)

        def place(row, col, value):
            high, low = split(value)
            at = (slot, pl.ds(row * SIDE, SIDE), pl.ds(col * SIDE, SIDE))
            s_high[at] = high
            s_low[at] = low

        centre = symmetric(own[slot, 0])
        if has_base:
            centre = centre + base[slot, 0]
        blocks[slot, 0] = centre
        place(0, 0, centre)
        empty = jnp.zeros((SIDE, SIDE), bf16)
        for k in range(1, members):
            column = present[k] * (0.5 * (own[slot, k] + turned(faces[k - 1])))
            block = present[k] * diagonals[k - 1]
            if has_base:
                column = column + base[slot, k]
                block = block + base[slot, members - 1 + k]
            blocks[slot, k] = column
            blocks[slot, members - 1 + k] = block
            place(k, 0, column)
            place(0, k, turned(column))
            place(k, k, block)
            for other in range(1, members):
                if other != k:
                    at = (slot, pl.ds(k * SIDE, SIDE), pl.ds(other * SIDE, SIDE))
                    s_high[at] = empty
                    s_low[at] = empty
    for slot in range(slots):
        matrix = (s_high.at[slot], s_low.at[slot])
        total = None
        for rows, columns, off in upper_tiles(order):
            tile = product(matrix, matrix, rows, columns)
            part = jnp.sum(tile * tile, axis=0, keepdims=True)
            part = 2.0 * part if off else part
            total = part if total is None else total + part
            high, low = split(tile)
            q_high[slot, rows, columns] = high
            q_low[slot, rows, columns] = low
            if off:
                high, low = split(turned(tile))
                q_high[slot, columns, rows] = high
                q_low[slot, columns, rows] = low
        total = jnp.sum(total, axis=1, keepdims=True)
        top = total if top is None else jnp.maximum(top, total)
    norms[...] = jnp.broadcast_to(top.reshape(1, 1, 1), norms.shape)
    for slot in range(slots):
        matrix = (s_high.at[slot], s_low.at[slot])
        square = (q_high.at[slot], q_low.at[slot])
        for rows, columns, off in upper_tiles(order):
            cube[slot, rows, columns] = product(matrix, square, rows, columns)


def sign_kernel(members, last, norms, blocks, cube, own, to_right, to_left, to_partner, x, xh, xl, yh, yl):
    slots = blocks.shape[0]
    order = members * SIDE
    largest = jnp.max(jnp.max(norms[...], axis=0), axis=(0, 1), keepdims=True)
    scaling = 1.5 / jnp.sqrt(jnp.sqrt(largest + epsilon))
    linear = 1.5 * scaling
    cubic = -0.5 * (scaling * scaling * scaling)

    def keep(now, slot, rows, columns, value, mirror):
        high, low = split(value)
        x[slot, rows, columns] = value
        xh[now, slot, rows, columns] = high
        xl[now, slot, rows, columns] = low
        if mirror:
            high, low = split(turned(value))
            xh[now, slot, columns, rows] = high
            xl[now, slot, columns, rows] = low

    for slot in range(slots):
        for i in range(members):
            for j in range(i, members):
                rows, columns = pl.ds(i * SIDE, SIDE), pl.ds(j * SIDE, SIDE)
                value = cubic * cube[slot, rows, columns]
                if i == 0 and j > 0:
                    value = value + linear * turned(blocks[slot, j])
                elif i == j:
                    value = value + linear * blocks[slot, members - 1 + i if i else 0]
                keep(0, slot, rows, columns, value, i != j)
                if i != j and i // 2 == j // 2:
                    x[slot, columns, rows] = turned(value)
    now = 0
    for repeat in range(1, ITERS - 1):
        for slot in range(slots):
            iterate = (xh.at[now, slot], xl.at[now, slot])
            for rows, columns, off in upper_tiles(order):
                tile = product(iterate, iterate, rows, columns)
                high, low = split(tile)
                yh[slot, rows, columns] = high
                yl[slot, rows, columns] = low
                if off:
                    high, low = split(turned(tile))
                    yh[slot, columns, rows] = high
                    yl[slot, columns, rows] = low
        for slot in range(slots):
            iterate = (xh.at[now, slot], xl.at[now, slot])
            square = (yh.at[slot], yl.at[slot])
            for rows, columns, off in upper_tiles(order):
                tile = product(iterate, square, rows, columns)
                value = 1.5 * x[slot, rows, columns] - 0.5 * tile
                keep(1 - now, slot, rows, columns, value, off)
                if off and repeat == ITERS - 2:
                    x[slot, columns, rows] = turned(value)
        now = 1 - now
    first = pl.ds(0, SIDE)

    def thin(slot, high, low):
        left_high, left_low = xh[now, slot], xl[now, slot]
        both = dot(left_high, jnp.concatenate([high, low], 1))
        return both[:, :SIDE] + both[:, SIDE:] + dot(left_low, high)

    middle = [thin(slot, xh[now, slot, :, first], xl[now, slot, :, first]) for slot in range(slots)]
    outer = [thin(slot, *split(middle[slot])) for slot in range(slots)]
    square = (SIDE, SIDE)
    eye = jnp.where(lanes(square) == rows_of(square), 0.5, 0.0)
    for slot in range(slots):
        central = 0.25 * outer[slot] - 0.75 * x[slot, :, first]
        parts = [central[k * SIDE : (k + 1) * SIDE] for k in range(members)]
        parts[0] = parts[0] + eye
        for k in range(members):
            own[slot, k] = parts[k]
        packed = None if last else pack(symmetric(parts[0]))
        fill(to_right, slot, parts[2], packed)
        fill(to_left, slot, parts[1], packed)
        fill(to_partner, slot, parts[3], packed)


def density_kernel(cols, members, *refs):
    lists, own = refs[:2]
    received = refs[2:-1]
    out = refs[-1]
    links = my_links(lists, cols, own.shape[0])
    for slot in range(own.shape[0]):
        present, bit = links[slot]
        faces, _ = neighbour_parts(slot, bit, received, False)
        out[slot, 0] = symmetric(own[slot, 0])
        for k in range(1, members):
            out[slot, k] = present[k] * (0.5 * (own[slot, k] + turned(faces[k - 1])))


def from_behind(block, axis, distance):
    devices = range(lax.axis_size(axis))
    return lax.ppermute(block, axis, [((i - distance) % len(devices), i) for i in devices])


def exchange(to_right, to_left, to_partner):
    received = [from_behind(to_right, "col", 1), from_behind(to_left, "col", -1)]
    rows = range(lax.axis_size("row"))
    place = 1
    while place < len(rows):
        received.append(lax.ppermute(to_partner, "row", [(i, i ^ place) for i in rows]))
        place *= 2
    return received


def vmem():
    return pl.BlockSpec(memory_space=pltpu.VMEM)


def smem():
    return pl.BlockSpec(memory_space=pltpu.SMEM)


def shape(*dims, dtype=f32):
    return jax.ShapeDtypeStruct(dims, dtype)


params = pltpu.CompilerParams(vmem_limit_bytes=48 * 1024 * 1024)


def per_device(hamiltonian, block_lists):
    slots, members = hamiltonian.shape[:2]
    order = members * SIDE
    cols = lax.axis_size("col")
    devices = lax.axis_size("row") * cols
    face = shape(slots, SIDE, SIDE)
    full = shape(slots, SIDE + PACKED, SIDE)

    sent = pl.pallas_call(
        pack_kernel,
        out_shape=[full] * 3,
        in_specs=[vmem()],
        out_specs=[vmem()] * 3,
        compiler_params=params,
        name="pack",
    )(hamiltonian)
    own = hamiltonian
    base = []
    for step in range(STEPS):
        last = step == STEPS - 1
        received = exchange(*sent)
        operands = [own, *base, *received]
        blocks, cube, norms = pl.pallas_call(
            functools.partial(assemble_kernel, cols, members, len(base)),
            out_shape=[
                shape(slots, 2 * members - 1, SIDE, SIDE),
                shape(slots, order, order),
                shape(devices, 8, SIDE),
            ],
            in_specs=[smem()] + [vmem()] * len(operands),
            out_specs=[vmem()] * 3,
            scratch_shapes=[pltpu.VMEM((slots, order, order), bf16)] * 4,
            compiler_params=params,
            name="assemble",
        )(block_lists, *operands)
        norms = lax.all_to_all(norms, ("row", "col"), 0, 0, tiled=True)
        own, *sent = pl.pallas_call(
            functools.partial(sign_kernel, members, last),
            out_shape=[shape(slots, members, SIDE, SIDE)] + [face if last else full] * 3,
            in_specs=[vmem()] * 3,
            out_specs=[vmem()] * 4,
            scratch_shapes=[pltpu.VMEM((slots, order, order), f32)]
            + [pltpu.VMEM((2, slots, order, order), bf16)] * 2
            + [pltpu.VMEM((slots, order, order), bf16)] * 2,
            compiler_params=params,
            name="sign",
        )(norms, blocks, cube)
        base = [blocks]
    received = exchange(*sent)
    return pl.pallas_call(
        functools.partial(density_kernel, cols, members),
        out_shape=shape(*hamiltonian.shape),
        in_specs=[smem()] + [vmem()] * (1 + len(received)),
        out_specs=vmem(),
        compiler_params=params,
        name="density",
    )(block_lists, own, *received)


def solution(mesh):
    return jax.shard_map(
        per_device,
        mesh=mesh,
        in_specs=(P(("row", "col"), None, None, None), P()),
        out_specs=P(("row", "col"), None, None, None),
        check_vma=False,
    )
```

profile of v0, /device:TPU:0, one launch (start us, length us, event | category | flops | bytes accessed | tf_op | source)
XLA Modules:
  0.0 94.0 jit_solution(14198494470257767890)
XLA Ops:
  0.0 1.0 %copy-done = f32[2,4,128,128]{3,2,1,0:T(8,128)S(1)} copy-done((f32[2,4,128,128]{3,2,1,0:T(8,128)S(1)}, f32[2,4,128,128]{3,2,1,0:T(8,128)}, u32[]{:S(2)}) %copy-start) | copy-done | bytes 524312
  1.0 0.2 pack.1
  1.2 3.0 %collective-permute-start = (f32[2,200,128]{2,1,0:T(8,128)S(1)}, f32[2,200,128]{2,1,0:T(8,128)S(1)}, u32[]{:S(2)}, u32[]{:S(2)}) collective-permute-start(f32[2,200,128]{2,1,0:T(8,128)S(1)} %get-tuple-element.22), channel_id=1, source_target_pairs={{7,0},{0,1},{1,2},{2,3},{3,4},{4,5},{5,6},{6,7},{15,8},{8,9},{9,10... | collective-permute-start | bytes 614408 | tf_op jit(solution)/shard_map/ppermute | solution.py:283
  4.2 3.1 %collective-permute-start.1 = (f32[2,200,128]{2,1,0:T(8,128)S(1)}, f32[2,200,128]{2,1,0:T(8,128)S(1)}, u32[]{:S(2)}, u32[]{:S(2)}) collective-permute-start(f32[2,200,128]{2,1,0:T(8,128)S(1)} %get-tuple-element.23), channel_id=1, source_target_pairs={{1,0},{2,1},{3,2},{4,3},{5,4},{6,5},{7,6},{0,7},{9,8},{10,9},{11,1... | collective-permute-start | bytes 614408 | tf_op jit(solution)/shard_map/ppermute | solution.py:283
  7.3 1.6 %collective-permute-start.3 = (f32[2,200,128]{2,1,0:T(8,128)S(1)}, f32[2,200,128]{2,1,0:T(8,128)S(1)}, u32[]{:S(2)}, u32[]{:S(2)}) collective-permute-start(f32[2,200,128]{2,1,0:T(8,128)S(1)} %get-tuple-element.24), channel_id=1, source_target_pairs={{0,16},{8,24},{16,0},{24,8},{1,17},{9,25},{17,1},{25,9},{2,18},{10... | collective-permute-start | bytes 614408 | tf_op jit(solution)/shard_map/ppermute | solution.py:291
  8.9 0.0 collective-permute-start.2
  8.9 0.8 copy.5.refs_0_
  9.7 3.3 %collective-permute-done.refs_2_ = f32[2,200,128]{2,1,0:T(8,128)S(1)} collective-permute-done((f32[2,200,128]{2,1,0:T(8,128)S(1)}, f32[2,200,128]{2,1,0:T(8,128)S(1)}, u32[]{:S(2)}, u32[]{:S(2)}) %collective-permute-start) | collective-permute-done | bytes 204832 | tf_op jit(solution)/shard_map/ppermute | solution.py:283
  13.0 2.2 %collective-permute-done.1.refs_3_ = f32[2,200,128]{2,1,0:T(8,128)S(1)} collective-permute-done((f32[2,200,128]{2,1,0:T(8,128)S(1)}, f32[2,200,128]{2,1,0:T(8,128)S(1)}, u32[]{:S(2)}, u32[]{:S(2)}) %collective-permute-start.1) | collective-permute-done | bytes 204832 | tf_op jit(solution)/shard_map/ppermute | solution.py:283
  15.2 0.0 collective-permute-done.3.refs_5_
  15.2 0.0 collective-permute-done.2.refs_4_
  15.2 1.0 %copy-done.1 = f32[2,4,128,128]{3,2,1,0:T(8,128)S(1)} copy-done((f32[2,4,128,128]{3,2,1,0:T(8,128)S(1)}, f32[2,4,128,128]{3,2,1,0:T(8,128)}, u32[]{:S(2)}) %copy-start.1) | copy-done | bytes 524312
  16.2 4.0 %assemble.2 = (f32[2,7,128,128]{3,2,1,0:T(8,128)S(1)}, f32[2,512,512]{2,1,0:T(8,128)S(1)}, f32[32,8,128]{2,1,0:T(8,128)S(1)}) custom-call(s32[64,4]{1,0:T(8,128)S(1)} %copy.5.refs_0_, f32[2,4,128,128]{3,2,1,0:T(8,128)S(1)} %copy-done.1, f32[2,200,128]{2,1,0:T(8,128)S(1)} %collective-permute-done.refs_2_, f32[2,200,128]{2,1,0:T(8,128)S(1)} %collective-permute-done.1.refs_3_, ...), custom_call_target="tpu_custom_call" | custom-call | tf_op jit(solution)/shard_map/assemble/pallas_call | solution.py:333
  20.2 12.2 %all_to_all.10.norms = f32[32,8,128]{2,1,0:T(8,128)S(1)} all-to-all(f32[32,8,128]{2,1,0:T(8,128)S(1)} %get-tuple-element.25), channel_id=1, replica_groups=mesh['row'=4,'col'=8] {'row','col'}, dimensions={0} | all-to-all | bytes 262144 | tf_op jit(solution)/shard_map/all_to_all | solution.py:346
  32.4 11.7 %sign.2 = (f32[2,4,128,128]{3,2,1,0:T(8,128)S(1)}, f32[2,200,128]{2,1,0:T(8,128)S(1)}, f32[2,200,128]{2,1,0:T(8,128)S(1)}, f32[2,200,128]{2,1,0:T(8,128)S(1)}) custom-call(f32[32,8,128]{2,1,0:T(8,128)S(1)} %all_to_all.10.norms, f32[2,7,128,128]{3,2,1,0:T(8,128)S(1)} %get-tuple-element.26.blocks.refs_2_, f32[2,512,512]{2,1,0:T(8,128)S(1)} %get-tuple-element.27.cube), custom_call_target="tpu_custom_call" | custom-call | tf_op jit(solution)/shard_map/sign/pallas_call | solution.py:347
  44.2 1.3 %collective-permute-start.4 = (f32[2,200,128]{2,1,0:T(8,128)S(1)}, f32[2,200,128]{2,1,0:T(8,128)S(1)}, u32[]{:S(2)}, u32[]{:S(2)}) collective-permute-start(f32[2,200,128]{2,1,0:T(8,128)S(1)} %get-tuple-element.29), channel_id=1, source_target_pairs={{7,0},{0,1},{1,2},{2,3},{3,4},{4,5},{5,6},{6,7},{15,8},{8,9},{9,10... | collective-permute-start | bytes 614408 | tf_op jit(solution)/shard_map/ppermute | solution.py:283
  45.4 3.5 %collective-permute-start.5 = (f32[2,200,128]{2,1,0:T(8,128)S(1)}, f32[2,200,128]{2,1,0:T(8,128)S(1)}, u32[]{:S(2)}, u32[]{:S(2)}) collective-permute-start(f32[2,200,128]{2,1,0:T(8,128)S(1)} %get-tuple-element.30), channel_id=1, source_target_pairs={{1,0},{2,1},{3,2},{4,3},{5,4},{6,5},{7,6},{0,7},{9,8},{10,9},{11,1... | collective-permute-start | bytes 614408 | tf_op jit(solution)/shard_map/ppermute | solution.py:283
  48.9 1.1 %collective-permute-start.7 = (f32[2,200,128]{2,1,0:T(8,128)S(1)}, f32[2,200,128]{2,1,0:T(8,128)S(1)}, u32[]{:S(2)}, u32[]{:S(2)}) collective-permute-start(f32[2,200,128]{2,1,0:T(8,128)S(1)} %get-tuple-element.31), channel_id=1, source_target_pairs={{0,16},{8,24},{16,0},{24,8},{1,17},{9,25},{17,1},{25,9},{2,18},{10... | collective-permute-start | bytes 614408 | tf_op jit(solution)/shard_map/ppermute | solution.py:291
  50.0 0.0 collective-permute-start.6
  50.0 4.4 %collective-permute-done.4.refs_3_ = f32[2,200,128]{2,1,0:T(8,128)S(1)} collective-permute-done((f32[2,200,128]{2,1,0:T(8,128)S(1)}, f32[2,200,128]{2,1,0:T(8,128)S(1)}, u32[]{:S(2)}, u32[]{:S(2)}) %collective-permute-start.4) | collective-permute-done | bytes 204832 | tf_op jit(solution)/shard_map/ppermute | solution.py:283
  54.4 2.2 %collective-permute-done.5.refs_4_ = f32[2,200,128]{2,1,0:T(8,128)S(1)} collective-permute-done((f32[2,200,128]{2,1,0:T(8,128)S(1)}, f32[2,200,128]{2,1,0:T(8,128)S(1)}, u32[]{:S(2)}, u32[]{:S(2)}) %collective-permute-start.5) | collective-permute-done | bytes 204832 | tf_op jit(solution)/shard_map/ppermute | solution.py:283
  56.6 4.0 %assemble.3 = (f32[2,7,128,128]{3,2,1,0:T(8,128)S(1)}, f32[2,512,512]{2,1,0:T(8,128)S(1)}, f32[32,8,128]{2,1,0:T(8,128)S(1)}) custom-call(s32[64,4]{1,0:T(8,128)S(1)} %copy.5.refs_0_, f32[2,4,128,128]{3,2,1,0:T(8,128)S(1)} %get-tuple-element.28.refs_1_, f32[2,7,128,128]{3,2,1,0:T(8,128)S(1)} %get-tuple-element.26.blocks.refs_2_, ...), custom_call_target="tpu_custom_call" | custom-call | tf_op jit(solution)/shard_map/assemble/pallas_call | solution.py:333
  60.7 9.8 %all_to_all.11.norms = f32[32,8,128]{2,1,0:T(8,128)S(1)} all-to-all(f32[32,8,128]{2,1,0:T(8,128)S(1)} %get-tuple-element.32), channel_id=1, replica_groups=mesh['row'=4,'col'=8] {'row','col'}, dimensions={0} | all-to-all | bytes 262144 | tf_op jit(solution)/shard_map/all_to_all | solution.py:346
  70.5 11.7 %sign.3 = (f32[2,4,128,128]{3,2,1,0:T(8,128)S(1)}, f32[2,128,128]{2,1,0:T(8,128)S(1)}, f32[2,128,128]{2,1,0:T(8,128)S(1)}, f32[2,128,128]{2,1,0:T(8,128)S(1)}) custom-call(f32[32,8,128]{2,1,0:T(8,128)S(1)} %all_to_all.11.norms, f32[2,7,128,128]{3,2,1,0:T(8,128)S(1)} %get-tuple-element.33.blocks, f32[2,512,512]{2,1,0:T(8,128)S(1)} %get-tuple-element.34.cube), custom_call_target="tpu_custom_call" | custom-call | tf_op jit(solution)/shard_map/sign/pallas_call | solution.py:347
  82.2 1.3 %collective-permute-start.8 = (f32[2,128,128]{2,1,0:T(8,128)S(1)}, f32[2,128,128]{2,1,0:T(8,128)S(1)}, u32[]{:S(2)}, u32[]{:S(2)}) collective-permute-start(f32[2,128,128]{2,1,0:T(8,128)S(1)} %get-tuple-element.36), channel_id=1, source_target_pairs={{7,0},{0,1},{1,2},{2,3},{3,4},{4,5},{5,6},{6,7},{15,8},{8,9},{9,10... | collective-permute-start | bytes 393224 | tf_op jit(solution)/shard_map/ppermute | solution.py:283
  83.5 3.5 %collective-permute-start.9 = (f32[2,128,128]{2,1,0:T(8,128)S(1)}, f32[2,128,128]{2,1,0:T(8,128)S(1)}, u32[]{:S(2)}, u32[]{:S(2)}) collective-permute-start(f32[2,128,128]{2,1,0:T(8,128)S(1)} %get-tuple-element.37), channel_id=1, source_target_pairs={{1,0},{2,1},{3,2},{4,3},{5,4},{6,5},{7,6},{0,7},{9,8},{10,9},{11,1... | collective-permute-start | bytes 393224 | tf_op jit(solution)/shard_map/ppermute | solution.py:283
  87.0 1.1 %collective-permute-start.11 = (f32[2,128,128]{2,1,0:T(8,128)S(1)}, f32[2,128,128]{2,1,0:T(8,128)S(1)}, u32[]{:S(2)}, u32[]{:S(2)}) collective-permute-start(f32[2,128,128]{2,1,0:T(8,128)S(1)} %get-tuple-element.38), channel_id=1, source_target_pairs={{0,16},{8,24},{16,0},{24,8},{1,17},{9,25},{17,1},{25,9},{2,18},{10... | collective-permute-start | bytes 393224 | tf_op jit(solution)/shard_map/ppermute | solution.py:291
  88.0 2.5 %collective-permute-done.8.refs_2_ = f32[2,128,128]{2,1,0:T(8,128)S(1)} collective-permute-done((f32[2,128,128]{2,1,0:T(8,128)S(1)}, f32[2,128,128]{2,1,0:T(8,128)S(1)}, u32[]{:S(2)}, u32[]{:S(2)}) %collective-permute-start.8) | collective-permute-done | bytes 131104 | tf_op jit(solution)/shard_map/ppermute | solution.py:283
  90.5 1.0 %collective-permute-done.9.refs_3_ = f32[2,128,128]{2,1,0:T(8,128)S(1)} collective-permute-done((f32[2,128,128]{2,1,0:T(8,128)S(1)}, f32[2,128,128]{2,1,0:T(8,128)S(1)}, u32[]{:S(2)}, u32[]{:S(2)}) %collective-permute-start.9) | collective-permute-done | bytes 131104 | tf_op jit(solution)/shard_map/ppermute | solution.py:283
  91.5 0.4 collective-permute-done.11.refs_5_
  91.9 0.0 collective-permute-done.10.refs_4_
  91.9 2.1 %density.1 = f32[2,4,128,128]{3,2,1,0:T(8,128)} custom-call(s32[64,4]{1,0:T(8,128)S(1)} %copy.5.refs_0_, f32[2,4,128,128]{3,2,1,0:T(8,128)S(1)} %get-tuple-element.35.refs_1_, f32[2,128,128]{2,1,0:T(8,128)S(1)} %collective-permute-done.8.refs_2_, f32[2,128,128]{2,1,0:T(8,128)S(1)} %collective-permute-done.9.refs_3_, ...), custom_call_target="tpu_custom_call" | custom-call | tf_op jit(solution)/shard_map/density/pallas_call | solution.py:360
  (5 shorter events, 0.0 us)
Async XLA Ops:
  0.0 1.0 %copy-start = (f32[2,4,128,128]{3,2,1,0:T(8,128)S(1)}, f32[2,4,128,128]{3,2,1,0:T(8,128)}, u32[]{:S(2)}) copy-start(f32[2,4,128,128]{3,2,1,0:T(8,128)} %refs_1_.1) | copy-start | bytes 1572868
  1.2 11.7 %collective-permute-start = (f32[2,200,128]{2,1,0:T(8,128)S(1)}, f32[2,200,128]{2,1,0:T(8,128)S(1)}, u32[]{:S(2)}, u32[]{:S(2)}) collective-permute-start(f32[2,200,128]{2,1,0:T(8,128)S(1)} %get-tuple-element.22), channel_id=1, source_target_pairs={{7,0},{0,1},{1,2},{2,3},{3,4},{4,5},{5,6},{6,7},{15,8},{8,9},{9,10... | collective-permute-start | bytes 614408 | tf_op jit(solution)/shard_map/ppermute | solution.py:283
  4.2 10.9 %collective-permute-start.1 = (f32[2,200,128]{2,1,0:T(8,128)S(1)}, f32[2,200,128]{2,1,0:T(8,128)S(1)}, u32[]{:S(2)}, u32[]{:S(2)}) collective-permute-start(f32[2,200,128]{2,1,0:T(8,128)S(1)} %get-tuple-element.23), channel_id=1, source_target_pairs={{1,0},{2,1},{3,2},{4,3},{5,4},{6,5},{7,6},{0,7},{9,8},{10,9},{11,1... | collective-permute-start | bytes 614408 | tf_op jit(solution)/shard_map/ppermute | solution.py:283
  7.3 7.8 %collective-permute-start.3 = (f32[2,200,128]{2,1,0:T(8,128)S(1)}, f32[2,200,128]{2,1,0:T(8,128)S(1)}, u32[]{:S(2)}, u32[]{:S(2)}) collective-permute-start(f32[2,200,128]{2,1,0:T(8,128)S(1)} %get-tuple-element.24), channel_id=1, source_target_pairs={{0,16},{8,24},{16,0},{24,8},{1,17},{9,25},{17,1},{25,9},{2,18},{10... | collective-permute-start | bytes 614408 | tf_op jit(solution)/shard_map/ppermute | solution.py:291
  8.9 6.2 %collective-permute-start.2 = (f32[2,200,128]{2,1,0:T(8,128)S(1)}, f32[2,200,128]{2,1,0:T(8,128)S(1)}, u32[]{:S(2)}, u32[]{:S(2)}) collective-permute-start(f32[2,200,128]{2,1,0:T(8,128)S(1)} %get-tuple-element.24), channel_id=1, source_target_pairs={{0,8},{8,0},{16,24},{24,16},{1,9},{9,1},{17,25},{25,17},{2,10},{10... | collective-permute-start | bytes 614408 | tf_op jit(solution)/shard_map/ppermute | solution.py:291
  15.2 1.0 %copy-start.1 = (f32[2,4,128,128]{3,2,1,0:T(8,128)S(1)}, f32[2,4,128,128]{3,2,1,0:T(8,128)}, u32[]{:S(2)}) copy-start(f32[2,4,128,128]{3,2,1,0:T(8,128)} %refs_1_.1) | copy-start | bytes 1572868
  44.2 10.3 %collective-permute-start.4 = (f32[2,200,128]{2,1,0:T(8,128)S(1)}, f32[2,200,128]{2,1,0:T(8,128)S(1)}, u32[]{:S(2)}, u32[]{:S(2)}) collective-permute-start(f32[2,200,128]{2,1,0:T(8,128)S(1)} %get-tuple-element.29), channel_id=1, source_target_pairs={{7,0},{0,1},{1,2},{2,3},{3,4},{4,5},{5,6},{6,7},{15,8},{8,9},{9,10... | collective-permute-start | bytes 614408 | tf_op jit(solution)/shard_map/ppermute | solution.py:283
  45.4 11.2 %collective-permute-start.5 = (f32[2,200,128]{2,1,0:T(8,128)S(1)}, f32[2,200,128]{2,1,0:T(8,128)S(1)}, u32[]{:S(2)}, u32[]{:S(2)}) collective-permute-start(f32[2,200,128]{2,1,0:T(8,128)S(1)} %get-tuple-element.30), channel_id=1, source_target_pairs={{1,0},{2,1},{3,2},{4,3},{5,4},{6,5},{7,6},{0,7},{9,8},{10,9},{11,1... | collective-permute-start | bytes 614408 | tf_op jit(solution)/shard_map/ppermute | solution.py:283
  48.9 7.7 %collective-permute-start.7 = (f32[2,200,128]{2,1,0:T(8,128)S(1)}, f32[2,200,128]{2,1,0:T(8,128)S(1)}, u32[]{:S(2)}, u32[]{:S(2)}) collective-permute-start(f32[2,200,128]{2,1,0:T(8,128)S(1)} %get-tuple-element.31), channel_id=1, source_target_pairs={{0,16},{8,24},{16,0},{24,8},{1,17},{9,25},{17,1},{25,9},{2,18},{10... | collective-permute-start | bytes 614408 | tf_op jit(solution)/shard_map/ppermute | solution.py:291
  50.0 6.7 %collective-permute-start.6 = (f32[2,200,128]{2,1,0:T(8,128)S(1)}, f32[2,200,128]{2,1,0:T(8,128)S(1)}, u32[]{:S(2)}, u32[]{:S(2)}) collective-permute-start(f32[2,200,128]{2,1,0:T(8,128)S(1)} %get-tuple-element.31), channel_id=1, source_target_pairs={{0,8},{8,0},{16,24},{24,16},{1,9},{9,1},{17,25},{25,17},{2,10},{10... | collective-permute-start | bytes 614408 | tf_op jit(solution)/shard_map/ppermute | solution.py:291
  82.2 8.4 %collective-permute-start.8 = (f32[2,128,128]{2,1,0:T(8,128)S(1)}, f32[2,128,128]{2,1,0:T(8,128)S(1)}, u32[]{:S(2)}, u32[]{:S(2)}) collective-permute-start(f32[2,128,128]{2,1,0:T(8,128)S(1)} %get-tuple-element.36), channel_id=1, source_target_pairs={{7,0},{0,1},{1,2},{2,3},{3,4},{4,5},{5,6},{6,7},{15,8},{8,9},{9,10... | collective-permute-start | bytes 393224 | tf_op jit(solution)/shard_map/ppermute | solution.py:283
  83.5 8.0 %collective-permute-start.9 = (f32[2,128,128]{2,1,0:T(8,128)S(1)}, f32[2,128,128]{2,1,0:T(8,128)S(1)}, u32[]{:S(2)}, u32[]{:S(2)}) collective-permute-start(f32[2,128,128]{2,1,0:T(8,128)S(1)} %get-tuple-element.37), channel_id=1, source_target_pairs={{1,0},{2,1},{3,2},{4,3},{5,4},{6,5},{7,6},{0,7},{9,8},{10,9},{11,1... | collective-permute-start | bytes 393224 | tf_op jit(solution)/shard_map/ppermute | solution.py:283
  87.0 5.0 %collective-permute-start.11 = (f32[2,128,128]{2,1,0:T(8,128)S(1)}, f32[2,128,128]{2,1,0:T(8,128)S(1)}, u32[]{:S(2)}, u32[]{:S(2)}) collective-permute-start(f32[2,128,128]{2,1,0:T(8,128)S(1)} %get-tuple-element.38), channel_id=1, source_target_pairs={{0,16},{8,24},{16,0},{24,8},{1,17},{9,25},{17,1},{25,9},{2,18},{10... | collective-permute-start | bytes 393224 | tf_op jit(solution)/shard_map/ppermute | solution.py:291
  88.0 3.9 %collective-permute-start.10 = (f32[2,128,128]{2,1,0:T(8,128)S(1)}, f32[2,128,128]{2,1,0:T(8,128)S(1)}, u32[]{:S(2)}, u32[]{:S(2)}) collective-permute-start(f32[2,128,128]{2,1,0:T(8,128)S(1)} %get-tuple-element.38), channel_id=1, source_target_pairs={{0,8},{8,0},{16,24},{24,16},{1,9},{9,1},{17,25},{25,17},{2,10},{10... | collective-permute-start | bytes 393224 | tf_op jit(solution)/shard_map/ppermute | solution.py:291
where the time goes:
time: 94.3 us; the launch traced here: 94 us
  Pallas kernels  33.7 us (36%)
  blocking collectives  22 us (23%)
  starting transfers between devices  19.4 us (21%)
  waiting for transfers between devices  16 us (17%)
  local copies, waits for them, and re-layouts  2.85 us (3%)
    pallas_call x2, Pallas kernels, per_device(): pl.pallas_call(functools.partial(sign_kernel, members, last), out_shape=[...  23.4 us
    all_to_all x2, blocking collectives, per_device(): norms = lax.all_to_all(norms, ('row', 'col'), 0, 0, tiled=True)  22 us
    ppermute x6, starting transfers between devices, from_behind(): lax.ppermute(block, axis, [((i - distance) % len(devices), i) for i in de...  15.7 us
    ppermute x6, waiting for transfers between devices, from_behind(): lax.ppermute(block, axis, [((i - distance) % len(devices), i) for i in de...  15.6 us
    pallas_call x2, Pallas kernels, per_device(): pl.pallas_call(functools.partial(assemble_kernel, cols, members, len(base...  8.05 us
    ppermute x6, starting transfers between devices, exchange(): lax.ppermute(to_partner, 'row', [(i, i ^ place) for i in rows])  3.71 us
    unnamed x5, local copies, waits for them, and re-layouts  2.85 us
    pallas_call x1, Pallas kernels, per_device(): pl.pallas_call(functools.partial(density_kernel, cols, members), out_shap...  2.07 us
  transfers between devices with their start and end apart: 12, of which 7 were waited for; matrix products, arithmetic and copies ran while one was open for 1% of the time, Pallas kernels for 0%

commit v1 on v0

v1 whole, which is shorter than its diff:
```python
import functools
import jax
import jax.numpy as jnp
from jax import lax
from jax.experimental import pallas as pl
from jax.experimental.pallas import tpu as pltpu
from jax.sharding import PartitionSpec as P

ITERS = 6
STEPS = 2
SIDE = 128
HALF = SIDE // 2
PACKED = HALF + 8

epsilon = 1e-06
f32 = jnp.float32
bf16 = jnp.bfloat16


def turned(block):
    return jnp.swapaxes(block, -1, -2)


def symmetric(block):
    return 0.5 * (block + turned(block))


def split(values):
    high = values.astype(bf16)
    return high, (values - high.astype(f32)).astype(bf16)


def dot(left, right):
    return lax.dot_general(left, right, (((1,), (0,)), ((), ())), preferred_element_type=f32)


def product(left, right, rows, cols):
    left_high, left_low = left[0][rows, :], left[1][rows, :]
    right_high, right_low = right[0][:, cols], right[1][:, cols]
    return dot(
        jnp.concatenate([left_high, left_low, left_high], 1),
        jnp.concatenate([right_high, right_high, right_low], 0),
    )


def upper_tiles(order):
    tile = order // 2
    for place, (row, col) in enumerate(((0, 0), (0, 1), (1, 1))):
        yield place, pl.ds(row * tile, tile), pl.ds(col * tile, tile), row != col


def store_split(target, slot, rows, columns, value, mirror):
    high, low = split(value)
    target[0][slot, rows, columns] = high
    target[1][slot, rows, columns] = low
    if mirror:
        high, low = split(turned(value))
        target[0][slot, columns, rows] = high
        target[1][slot, columns, rows] = low


def lanes(shape):
    return lax.broadcasted_iota(jnp.int32, shape, 1)


def rows_of(shape):
    return lax.broadcasted_iota(jnp.int32, shape, 0)


def pack(block):
    shape = (HALF, SIDE)
    lower = pltpu.roll(block[HALF:, :], HALF, 1)
    body = jnp.where(lanes(shape) < rows_of(shape), lower, block[:HALF, :])
    whole = block.shape
    diagonal = jnp.sum(jnp.where(lanes(whole) == rows_of(whole), block, 0.0), 0, keepdims=True)
    return body, jnp.broadcast_to(diagonal, (PACKED - HALF, SIDE))


def unpack(body, diagonal):
    shape = (HALF, SIDE)
    lane, row = lanes(shape), rows_of(shape)
    top = jnp.where(lane == row, 0.5 * body, jnp.where(lane < row, 0.0, body))
    rolled = pltpu.roll(body, HALF, 1)
    at = lane - HALF
    bottom = jnp.where(at == row, 0.5 * diagonal, jnp.where((at >= 0) & (at < row), rolled, 0.0))
    folded = jnp.concatenate([top, bottom], 0)
    return folded + turned(folded)


def fill(target, slot, face, packed):
    target[slot, pl.ds(0, SIDE), :] = face
    if packed is not None:
        target[slot, pl.ds(SIDE, HALF), :] = packed[0]
        target[slot, pl.ds(SIDE + HALF, PACKED - HALF), :] = packed[1]


def pack_kernel(own, half, to_right, to_left, to_partner):
    for slot in range(own.shape[0]):
        centre = symmetric(own[slot, 0])
        packed = pack(centre)
        half[slot, 0] = centre
        for k in range(1, own.shape[1]):
            half[slot, k] = 0.5 * own[slot, k]
        fill(to_right, slot, own[slot, 2], packed)
        fill(to_left, slot, own[slot, 1], packed)
        fill(to_partner, slot, own[slot, 3], packed)


def my_links(lists, cols, slots):
    my_row = lax.axis_index("row")
    device = my_row * cols + lax.axis_index("col")
    links = []
    for slot in range(slots):
        column = device * slots + slot
        present = [jnp.where(lists[column, k] >= 0, 1.0, 0.0).astype(f32) for k in range(4)]
        partner_row = lists[column, 3] // (slots * cols)
        links.append((present, jnp.bitwise_xor(my_row, partner_row)))
    return links


def neighbour_parts(slot, bit, received, with_diagonals):
    from_left, from_right = received[:2]
    from_rows = received[2:]

    def read(first, count):
        span = pl.ds(first, count)
        partner = from_rows[0][slot, span, :]
        for place in range(1, len(from_rows)):
            partner = jnp.where(bit == (1 << place), from_rows[place][slot, span, :], partner)
        return from_left[slot, span, :], from_right[slot, span, :], partner

    faces = read(0, SIDE)
    if not with_diagonals:
        return faces, None
    bodies = read(SIDE, HALF)
    diagonals = read(SIDE + HALF, PACKED - HALF)
    return faces, [unpack(b, d[0:1, :]) for b, d in zip(bodies, diagonals)]


def assemble_kernel(cols, members, has_base, last, *refs):
    lists, half = refs[:2]
    base = refs[2] if has_base else None
    outputs = 6 + (not last)
    received = refs[2 + has_base : -outputs]
    norms, dense, s_high, s_low, q_high, q_low = refs[-outputs:][:6]
    blocks = None if last else refs[-1]
    slots = half.shape[0]
    order = members * SIDE
    top = None
    links = my_links(lists, cols, slots)
    for slot in range(slots):
        present, bit = links[slot]
        faces, diagonals = neighbour_parts(slot, bit, received, True)

        def place(row, col, value):
            high, low = split(value)
            at = (slot, pl.ds(row * SIDE, SIDE), pl.ds(col * SIDE, SIDE))
            s_high[at] = high
            s_low[at] = low
            if row // 2 <= col // 2:
                inner = (pl.ds(row % 2 * SIDE, SIDE), pl.ds(col % 2 * SIDE, SIDE))
                dense[(slot, row // 2 + col // 2, *inner)] = value

        centre = half[slot, 0]
        if has_base:
            centre = centre + base[slot, 0]
        if not last:
            blocks[slot, 0] = centre
        place(0, 0, centre)
        empty = jnp.zeros((SIDE, SIDE), f32)
        for k in range(1, members):
            column = present[k] * (half[slot, k] + 0.5 * turned(faces[k - 1]))
            block = present[k] * diagonals[k - 1]
            if has_base:
                column = column + base[slot, k]
                block = block + base[slot, members - 1 + k]
            if not last:
                blocks[slot, k] = column
                blocks[slot, members - 1 + k] = block
            place(k, 0, column)
            place(0, k, turned(column))
            place(k, k, block)
            for other in range(1, members):
                if other != k:
                    place(k, other, empty)
    for slot in range(slots):
        matrix = (s_high.at[slot], s_low.at[slot])
        total = None
        for _, rows, columns, off in upper_tiles(order):
            tile = product(matrix, matrix, rows, columns)
            part = jnp.sum(tile * tile, axis=0, keepdims=True)
            part = 2.0 * part if off else part
            total = part if total is None else total + part
            store_split((q_high, q_low), slot, rows, columns, tile, off)
        total = jnp.sum(total, axis=1, keepdims=True)
        top = total if top is None else jnp.maximum(top, total)
    norms[...] = jnp.broadcast_to(top.reshape(1, 1, 1), norms.shape)


def powers_kernel(s_high, s_low, q_high, q_low, powers, p_high, p_low):
    slots, count = powers.shape[:2]
    order = s_high.shape[1]
    for power in range(count):
        for slot in range(slots):
            square = (q_high.at[slot], q_low.at[slot])
            if power == 0:
                lower = (s_high.at[slot], s_low.at[slot])
            else:
                lower = (p_high.at[power % 2, slot], p_low.at[power % 2, slot])
            target = (p_high.at[1 - power % 2], p_low.at[1 - power % 2])
            for place, rows, columns, off in upper_tiles(order):
                tile = product(lower, square, rows, columns)
                powers[slot, power, place] = tile
                if power + 1 < count:
                    store_split(target, slot, rows, columns, tile, off)


def two_steps():
    once = {1: 1.5, 3: -0.5}
    cube = {0: 1.0}
    for _ in range(3):
        grown = {}
        for i, a in cube.items():
            for j, b in once.items():
                grown[i + j] = grown.get(i + j, 0.0) + a * b
        cube = grown
    return [1.5 * once.get(i, 0.0) - 0.5 * cube.get(i, 0.0) for i in range(1, 10, 2)]


def sign_kernel(members, last, norms, dense, powers, own, to_right, to_left, to_partner, x, xh, xl, yh, yl):
    slots = dense.shape[0]
    order = members * SIDE
    largest = jnp.max(jnp.max(norms[...], axis=0), axis=(0, 1), keepdims=True)
    scaling = 1.5 / jnp.sqrt(jnp.sqrt(largest + epsilon))
    factors, power = [], scaling
    for coefficient in two_steps():
        factors.append(coefficient * power)
        power = power * (scaling * scaling)
    for slot in range(slots):
        for place, rows, columns, off in upper_tiles(order):
            value = factors[0] * dense[slot, place]
            for k in range(1, len(factors)):
                value = value + factors[k] * powers[slot, k - 1, place]
            x[slot, rows, columns] = value
            store_split((xh.at[0], xl.at[0]), slot, rows, columns, value, off)
    now = 0
    for repeat in range(2, ITERS - 1):
        for slot in range(slots):
            iterate = (xh.at[now, slot], xl.at[now, slot])
            for _, rows, columns, off in upper_tiles(order):
                tile = product(iterate, iterate, rows, columns)
                store_split((yh, yl), slot, rows, columns, tile, off)
        for slot in range(slots):
            iterate = (xh.at[now, slot], xl.at[now, slot])
            square = (yh.at[slot], yl.at[slot])
            target = (xh.at[1 - now], xl.at[1 - now])
            for _, rows, columns, off in upper_tiles(order):
                tile = product(iterate, square, rows, columns)
                value = 1.5 * x[slot, rows, columns] - 0.5 * tile
                x[slot, rows, columns] = value
                store_split(target, slot, rows, columns, value, off)
                if off and repeat == ITERS - 2:
                    x[slot, columns, rows] = turned(value)
        now = 1 - now
    first = pl.ds(0, SIDE)

    def thin(slot, high, low):
        left_high, left_low = xh[now, slot], xl[now, slot]
        both = dot(left_high, jnp.concatenate([high, low], 1))
        return both[:, :SIDE] + both[:, SIDE:] + dot(left_low, high)

    middle = [thin(slot, xh[now, slot, :, first], xl[now, slot, :, first]) for slot in range(slots)]
    outer = [thin(slot, *split(middle[slot])) for slot in range(slots)]
    square = (SIDE, SIDE)
    eye = jnp.where(lanes(square) == rows_of(square), 0.5, 0.0)
    for slot in range(slots):
        central = 0.25 * outer[slot] - 0.75 * x[slot, :, first]
        parts = [central[k * SIDE : (k + 1) * SIDE] for k in range(members)]
        parts[0] = symmetric(parts[0]) + eye
        packed = None if last else pack(parts[0])
        fill(to_right, slot, parts[2], packed)
        fill(to_left, slot, parts[1], packed)
        fill(to_partner, slot, parts[3], packed)
        own[slot, 0] = parts[0]
        for k in range(1, members):
            own[slot, k] = 0.5 * parts[k]


def density_kernel(cols, members, *refs):
    lists, half = refs[:2]
    received = refs[2:-1]
    out = refs[-1]
    links = my_links(lists, cols, half.shape[0])
    for slot in range(half.shape[0]):
        present, bit = links[slot]
        faces, _ = neighbour_parts(slot, bit, received, False)
        out[slot, 0] = half[slot, 0]
        for k in range(1, members):
            out[slot, k] = present[k] * (half[slot, k] + 0.5 * turned(faces[k - 1]))


def from_behind(block, axis, distance):
    devices = range(lax.axis_size(axis))
    return lax.ppermute(block, axis, [((i - distance) % len(devices), i) for i in devices])


def exchange(to_right, to_left, to_partner):
    received = [from_behind(to_right, "col", 1), from_behind(to_left, "col", -1)]
    rows = range(lax.axis_size("row"))
    place = 1
    while place < len(rows):
        received.append(lax.ppermute(to_partner, "row", [(i, i ^ place) for i in rows]))
        place *= 2
    return received


def vmem():
    return pl.BlockSpec(memory_space=pltpu.VMEM)


def shape(*dims, dtype=f32):
    return jax.ShapeDtypeStruct(dims, dtype)


def call(kernel, name, operands, outputs, scratch=(), flops=0, smem_first=False):
    moved = sum(4 * a.size for a in (*operands, *outputs))
    specs = [vmem()] * len(operands)
    if smem_first:
        specs[0] = pl.BlockSpec(memory_space=pltpu.SMEM)
    return pl.pallas_call(
        kernel,
        out_shape=list(outputs),
        in_specs=specs,
        out_specs=[vmem()] * len(outputs),
        scratch_shapes=list(scratch),
        compiler_params=pltpu.CompilerParams(vmem_limit_bytes=24 * 1024 * 1024),
        cost_estimate=pl.CostEstimate(flops=flops, bytes_accessed=moved, transcendentals=0),
        name=name,
    )(*operands)


def per_device(hamiltonian, block_lists):
    slots, members = hamiltonian.shape[:2]
    order = members * SIDE
    tile = order // 2
    cols = lax.axis_size("col")
    devices = lax.axis_size("row") * cols
    face = shape(slots, SIDE, SIDE)
    full = shape(slots, SIDE + PACKED, SIDE)
    own = shape(slots, members, SIDE, SIDE)
    part = shape(slots, order, order, dtype=bf16)
    part_scratch = pltpu.VMEM((slots, order, order), bf16)
    both_scratch = pltpu.VMEM((2, slots, order, order), bf16)
    multiply = slots * 3 * 3 * order * order * order // 2
    count = len(two_steps()) - 1

    half, *sent = call(pack_kernel, "pack", [hamiltonian], [own] + [full] * 3)
    base = []
    for step in range(STEPS):
        last = step == STEPS - 1
        received = exchange(*sent)
        norms, dense, *parts = call(
            functools.partial(assemble_kernel, cols, members, len(base), last),
            "assemble",
            [block_lists, half, *base, *received],
            [shape(devices, 8, SIDE), shape(slots, 3, tile, tile)]
            + [part] * 4
            + ([] if last else [shape(slots, 2 * members - 1, SIDE, SIDE)]),
            flops=multiply,
            smem_first=True,
        )
        base = parts[4:]
        norms = lax.all_to_all(norms, ("row", "col"), 0, 0, tiled=True)
        (powers,) = call(
            powers_kernel,
            "powers",
            parts[:4],
            [shape(slots, count, 3, tile, tile)],
            [both_scratch] * 2,
            flops=count * multiply,
        )
        half, *sent = call(
            functools.partial(sign_kernel, members, last),
            "sign",
            [norms, dense, powers],
            [own] + [face if last else full] * 3,
            [pltpu.VMEM((slots, order, order), f32)] + [both_scratch] * 2 + [part_scratch] * 2,
            flops=7 * multiply,
        )
    received = exchange(*sent)
    (density,) = call(
        functools.partial(density_kernel, cols, members),
        "density",
        [block_lists, half, *received],
        [own],
        smem_first=True,
    )
    return density


def solution(mesh):
    return jax.shard_map(
        per_device,
        mesh=mesh,
        in_specs=(P(("row", "col"), None, None, None), P()),
        out_specs=P(("row", "col"), None, None, None),
        check_vma=False,
    )
```

time: 94.3 us -> 114 us (1.21)
  local copies, waits for them, and re-layouts: 2.85 us -> 29 us
  blocking collectives: 22 us -> 0 us
  starting transfers between devices: 19.4 us -> 30 us
  Pallas kernels: 33.7 us -> 38.6 us
    unnamed x5 -> x43, local copies, waits for them, and re-layouts: 2.85 us -> 29 us
    all_to_all x2 -> x0, blocking collectives: 22 us -> none  [per_device(): norms = lax.all_to_all(norms, ('row', 'col'), 0, 0, tiled=True)]
    all_to_all x0 -> x2, starting transfers between devices: none -> 9.15 us  [per_device(): norms = lax.all_to_all(norms, ('row', 'col'), 0, 0, tiled=True)]
    pallas_call x6 -> x8, Pallas kernels: 33.7 us -> 38.6 us  [call(): pl.pallas_call(kernel, out_shape=list(outputs), in_specs=specs, out_specs...]
    ppermute x6, starting transfers between devices: 3.71 us -> 5.13 us  [exchange(): lax.ppermute(to_partner, 'row', [(i, i ^ place) for i in rows])]
  transfers between devices with their start and end apart: 12 -> 14, of which waited for: 7 -> 6; matrix products, arithmetic and copies ran while one was open for 1% -> 1% of each run, Pallas kernels for 0% -> 9%
where the time goes in v1:
time: 114 us; the launch traced here: 113 us
  Pallas kernels  38.6 us (34%)
  starting transfers between devices  30 us (26%)
  local copies, waits for them, and re-layouts  29 us (25%)
  waiting for transfers between devices  15.4 us (14%)
    pallas_call x8, Pallas kernels, call(): pl.pallas_call(kernel, out_shape=list(outputs), in_specs=specs, out_specs...  38.6 us
    unnamed x43, local copies, waits for them, and re-layouts  29 us
    ppermute x6, starting transfers between devices, from_behind(): lax.ppermute(block, axis, [((i - distance) % len(devices), i) for i in de...  15.7 us
    ppermute x6, waiting for transfers between devices, from_behind(): lax.ppermute(block, axis, [((i - distance) % len(devices), i) for i in de...  15.3 us
    all_to_all x2, starting transfers between devices, per_device(): norms = lax.all_to_all(norms, ('row', 'col'), 0, 0, tiled=True)  9.15 us
    ppermute x6, starting transfers between devices, exchange(): lax.ppermute(to_partner, 'row', [(i, i ^ place) for i in rows])  5.13 us
  transfers between devices with their start and end apart: 14, of which 6 were waited for; matrix products, arithmetic and copies ran while one was open for 1% of the time, Pallas kernels for 9%

profile of v1, /device:TPU:0, one launch (start us, length us, event | category | flops | bytes accessed | tf_op | source)
XLA Modules:
  0.0 113.0 jit_solution(14867435017197724982)
XLA Ops:
  1.2 3.0 %collective-permute-start = (f32[2,200,128]{2,1,0:T(8,128)S(1)}, f32[2,200,128]{2,1,0:T(8,128)S(1)}, u32[]{:S(2)}, u32[]{:S(2)}) collective-permute-start(f32[2,200,128]{2,1,0:T(8,128)S(1)} %get-tuple-element.31), channel_id=1, source_target_pairs={{7,0},{0,1},{1,2},{2,3},{3,4},{4,5},{5,6},{6,7},{15,8},{8,9},{9,10... | collective-permute-start | bytes 614408 | tf_op jit(solution)/shard_map/ppermute | solution.py:304
  4.2 3.1 %collective-permute-start.1 = (f32[2,200,128]{2,1,0:T(8,128)S(1)}, f32[2,200,128]{2,1,0:T(8,128)S(1)}, u32[]{:S(2)}, u32[]{:S(2)}) collective-permute-start(f32[2,200,128]{2,1,0:T(8,128)S(1)} %get-tuple-element.32), channel_id=1, source_target_pairs={{1,0},{2,1},{3,2},{4,3},{5,4},{6,5},{7,6},{0,7},{9,8},{10,9},{11,1... | collective-permute-start | bytes 614408 | tf_op jit(solution)/shard_map/ppermute | solution.py:304
  7.3 1.6 %collective-permute-start.3 = (f32[2,200,128]{2,1,0:T(8,128)S(1)}, f32[2,200,128]{2,1,0:T(8,128)S(1)}, u32[]{:S(2)}, u32[]{:S(2)}) collective-permute-start(f32[2,200,128]{2,1,0:T(8,128)S(1)} %get-tuple-element.33), channel_id=1, source_target_pairs={{0,16},{8,24},{16,0},{24,8},{1,17},{9,25},{17,1},{25,9},{2,18},{10... | collective-permute-start | bytes 614408 | tf_op jit(solution)/shard_map/ppermute | solution.py:312
  9.7 3.3 %collective-permute-done.refs_2_ = f32[2,200,128]{2,1,0:T(8,128)S(1)} collective-permute-done((f32[2,200,128]{2,1,0:T(8,128)S(1)}, f32[2,200,128]{2,1,0:T(8,128)S(1)}, u32[]{:S(2)}, u32[]{:S(2)}) %collective-permute-start) | collective-permute-done | bytes 204832 | tf_op jit(solution)/shard_map/ppermute | solution.py:304
  13.0 2.2 %collective-permute-done.1.refs_3_ = f32[2,200,128]{2,1,0:T(8,128)S(1)} collective-permute-done((f32[2,200,128]{2,1,0:T(8,128)S(1)}, f32[2,200,128]{2,1,0:T(8,128)S(1)}, u32[]{:S(2)}, u32[]{:S(2)}) %collective-permute-start.1) | collective-permute-done | bytes 204832 | tf_op jit(solution)/shard_map/ppermute | solution.py:304
  15.2 3.6 %assemble.2 = (f32[32,8,128]{2,1,0:T(8,128)}, f32[2,3,256,256]{3,2,1,0:T(8,128)S(1)}, bf16[2,512,512]{2,1,0:T(8,128)(2,1)S(1)}, bf16[2,512,512]{2,1,0:T(8,128)(2...) custom-call(s32[64,4]{1,0:T(8,128)S(1)} %copy.5.refs_0_, ...), custom_call_target="tpu_custom_call" | custom-call | flops 1207959552 | bytes 12354560 | tf_op jit(solution)/shard_map/assemble/pallas_call | solution.py:330
  23.7 4.8 %all-to-all-start = ((f32[32,8,128]{2,1,0:T(8,128)}), f32[32,8,128]{2,1,0:T(8,128)S(1)}, u32[]{:S(2)}, u32[]{:S(2)}) async-start(f32[32,8,128]{2,1,0:T(8,128)} %get-tuple-element.34), calls=%async_computation | async-start | bytes 262144 | tf_op jit(solution)/shard_map/all_to_all | solution.py:373
  29.7 1.2 %copy-done.16 = bf16[2,512,512]{2,1,0:T(8,128)(2,1)S(1)} copy-done((bf16[2,512,512]{2,1,0:T(8,128)(2,1)S(1)}, bf16[2,512,512]{2,1,0:T(8,128)(2,1)}, u32[]{:S(2)}) %copy-start.16) | copy-done | bytes 1048600
  30.9 1.2 %copy-done.18 = bf16[2,512,512]{2,1,0:T(8,128)(2,1)S(1)} copy-done((bf16[2,512,512]{2,1,0:T(8,128)(2,1)S(1)}, bf16[2,512,512]{2,1,0:T(8,128)(2,1)}, u32[]{:S(2)}) %copy-start.18) | copy-done | bytes 1048600
  32.1 1.2 %copy-done.20 = bf16[2,512,512]{2,1,0:T(8,128)(2,1)S(1)} copy-done((bf16[2,512,512]{2,1,0:T(8,128)(2,1)S(1)}, bf16[2,512,512]{2,1,0:T(8,128)(2,1)}, u32[]{:S(2)}) %copy-start.20) | copy-done | bytes 1048600
  33.4 5.1 %powers.2 = f32[2,4,3,256,256]{4,3,2,1,0:T(8,128)S(1)} custom-call(bf16[2,512,512]{2,1,0:T(8,128)(2,1)S(1)} %copy-done.14, bf16[2,512,512]{2,1,0:T(8,128)(2,1)S(1)} %copy-done.16, bf16[2,512,512]{2,1,0:T(8,128)(2,1)S(1)} %copy-done.18, bf16[2,512,512]{2,1,0:T(8,128)(2,1)S(1)} %copy-done.20), custom_call_target="tpu_custom_call" | custom-call | flops 4831838208 | bytes 14680064 | tf_op jit(solution)/shard_map/powers/pallas_call | solution.py:330
  38.5 2.6 %copy-done.11 = f32[2,4,3,256,256]{4,3,2,1,0:T(8,128)} copy-done((f32[2,4,3,256,256]{4,3,2,1,0:T(8,128)}, f32[2,4,3,256,256]{4,3,2,1,0:T(8,128)S(1)}, u32[]{:S(2)}) %copy-start.11) | copy-done | bytes 6291480
  41.1 2.8 %copy-done.12 = f32[2,4,3,256,256]{4,3,2,1,0:T(8,128)S(1)} copy-done((f32[2,4,3,256,256]{4,3,2,1,0:T(8,128)S(1)}, f32[2,4,3,256,256]{4,3,2,1,0:T(8,128)}, u32[]{:S(2)}) %copy-start.12) | copy-done | bytes 6291480
  43.9 9.7 %sign.2 = (f32[2,4,128,128]{3,2,1,0:T(8,128)S(1)}, f32[2,200,128]{2,1,0:T(8,128)S(1)}, f32[2,200,128]{2,1,0:T(8,128)S(1)}, f32[2,200,128]{2,1,0:T(8,128)S(1)}) custom-call(f32[32,8,128]{2,1,0:T(8,128)S(1)} %all-to-all-done.norms, f32[2,3,256,256]{3,2,1,0:T(8,128)S(1)} %get-tuple-element.35.dense, f32[2,4,3,256,256]{4,3,2,1,0:T(8,128)S(1)} %copy-done.12), custom_call_target="tpu_custom_call" | custom-call | flops 8455716864 | bytes 9134080 | tf_op jit(solution)/shard_map/sign/pallas_call | solution.py:330
  53.5 1.8 %collective-permute-start.4 = (f32[2,200,128]{2,1,0:T(8,128)S(1)}, f32[2,200,128]{2,1,0:T(8,128)S(1)}, u32[]{:S(2)}, u32[]{:S(2)}) collective-permute-start(f32[2,200,128]{2,1,0:T(8,128)S(1)} %get-tuple-element.42), channel_id=1, source_target_pairs={{7,0},{0,1},{1,2},{2,3},{3,4},{4,5},{5,6},{6,7},{15,8},{8,9},{9,10... | collective-permute-start | bytes 614408 | tf_op jit(solution)/shard_map/ppermute | solution.py:304
  55.4 3.0 %collective-permute-start.5 = (f32[2,200,128]{2,1,0:T(8,128)S(1)}, f32[2,200,128]{2,1,0:T(8,128)S(1)}, u32[]{:S(2)}, u32[]{:S(2)}) collective-permute-start(f32[2,200,128]{2,1,0:T(8,128)S(1)} %get-tuple-element.43), channel_id=1, source_target_pairs={{1,0},{2,1},{3,2},{4,3},{5,4},{6,5},{7,6},{0,7},{9,8},{10,9},{11,1... | collective-permute-start | bytes 614408 | tf_op jit(solution)/shard_map/ppermute | solution.py:304
  58.3 1.8 %collective-permute-start.7 = (f32[2,200,128]{2,1,0:T(8,128)S(1)}, f32[2,200,128]{2,1,0:T(8,128)S(1)}, u32[]{:S(2)}, u32[]{:S(2)}) collective-permute-start(f32[2,200,128]{2,1,0:T(8,128)S(1)} %get-tuple-element.44), channel_id=1, source_target_pairs={{0,16},{8,24},{16,0},{24,8},{1,17},{9,25},{17,1},{25,9},{2,18},{10... | collective-permute-start | bytes 614408 | tf_op jit(solution)/shard_map/ppermute | solution.py:312
  60.1 4.3 %collective-permute-done.4.refs_3_ = f32[2,200,128]{2,1,0:T(8,128)S(1)} collective-permute-done((f32[2,200,128]{2,1,0:T(8,128)S(1)}, f32[2,200,128]{2,1,0:T(8,128)S(1)}, u32[]{:S(2)}, u32[]{:S(2)}) %collective-permute-start.4) | collective-permute-done | bytes 204832 | tf_op jit(solution)/shard_map/ppermute | solution.py:304
  64.4 2.2 %collective-permute-done.5.refs_4_ = f32[2,200,128]{2,1,0:T(8,128)S(1)} collective-permute-done((f32[2,200,128]{2,1,0:T(8,128)S(1)}, f32[2,200,128]{2,1,0:T(8,128)S(1)}, u32[]{:S(2)}, u32[]{:S(2)}) %collective-permute-start.5) | collective-permute-done | bytes 204832 | tf_op jit(solution)/shard_map/ppermute | solution.py:304
  66.6 3.6 %assemble.3 = (f32[32,8,128]{2,1,0:T(8,128)}, f32[2,3,256,256]{3,2,1,0:T(8,128)S(1)}, bf16[2,512,512]{2,1,0:T(8,128)(2,1)S(1)}, bf16[2,512,512]{2,1,0:T(8,128)(2...) custom-call(s32[64,4]{1,0:T(8,128)S(1)} %copy.5.refs_0_, ...), custom_call_target="tpu_custom_call" | custom-call | flops 1207959552 | bytes 12354560 | tf_op jit(solution)/shard_map/assemble/pallas_call | solution.py:330
  73.2 4.4 %all-to-all-start.1 = ((f32[32,8,128]{2,1,0:T(8,128)}), f32[32,8,128]{2,1,0:T(8,128)S(1)}, u32[]{:S(2)}, u32[]{:S(2)}) async-start(f32[32,8,128]{2,1,0:T(8,128)} %get-tuple-element.45), calls=%async_computation.1 | async-start | bytes 262144 | tf_op jit(solution)/shard_map/all_to_all | solution.py:373
  78.8 1.2 %copy-done.4 = bf16[2,512,512]{2,1,0:T(8,128)(2,1)S(1)} copy-done((bf16[2,512,512]{2,1,0:T(8,128)(2,1)S(1)}, bf16[2,512,512]{2,1,0:T(8,128)(2,1)}, u32[]{:S(2)}) %copy-start.4) | copy-done | bytes 1048600
  81.2 5.1 %powers.3 = f32[2,4,3,256,256]{4,3,2,1,0:T(8,128)S(1)} custom-call(bf16[2,512,512]{2,1,0:T(8,128)(2,1)S(1)} %get-tuple-element.47.s_high, bf16[2,512,512]{2,1,0:T(8,128)(2,1)S(1)} %copy-done.2, bf16[2,512,512]{2,1,0:T(8,128)(2,1)S(1)} %copy-done.4, bf16[2,512,512]{2,1,0:T(8,128)(2,1)S(1)} %copy-done.6), custom_call_target="tpu_custom_call" | custom-call | flops 4831838208 | bytes 14680064 | tf_op jit(solution)/shard_map/powers/pallas_call | solution.py:330
  86.3 2.6 %copy-done.9 = f32[2,4,3,256,256]{4,3,2,1,0:T(8,128)} copy-done((f32[2,4,3,256,256]{4,3,2,1,0:T(8,128)}, f32[2,4,3,256,256]{4,3,2,1,0:T(8,128)S(1)}, u32[]{:S(2)}) %copy-start.9) | copy-done | bytes 6291480
  88.9 2.8 %copy-done.10 = f32[2,4,3,256,256]{4,3,2,1,0:T(8,128)S(1)} copy-done((f32[2,4,3,256,256]{4,3,2,1,0:T(8,128)S(1)}, f32[2,4,3,256,256]{4,3,2,1,0:T(8,128)}, u32[]{:S(2)}) %copy-start.10) | copy-done | bytes 6291480
  91.7 9.3 %sign.3 = (f32[2,4,128,128]{3,2,1,0:T(8,128)S(1)}, f32[2,128,128]{2,1,0:T(8,128)S(1)}, f32[2,128,128]{2,1,0:T(8,128)S(1)}, f32[2,128,128]{2,1,0:T(8,128)S(1)}) custom-call(f32[32,8,128]{2,1,0:T(8,128)S(1)} %all-to-all-done.1.norms, f32[2,3,256,256]{3,2,1,0:T(8,128)S(1)} %get-tuple-element.46.dense, f32[2,4,3,256,256]{4,3,2,1,0:T(8,128)S(1)} %copy-done.10), custom_call_target="tpu_custom_call" | custom-call | flops 8455716864 | bytes 8912896 | tf_op jit(solution)/shard_map/sign/pallas_call | solution.py:330
  101.1 1.8 %collective-permute-start.8 = (f32[2,128,128]{2,1,0:T(8,128)S(1)}, f32[2,128,128]{2,1,0:T(8,128)S(1)}, u32[]{:S(2)}, u32[]{:S(2)}) collective-permute-start(f32[2,128,128]{2,1,0:T(8,128)S(1)} %get-tuple-element.52), channel_id=1, source_target_pairs={{7,0},{0,1},{1,2},{2,3},{3,4},{4,5},{5,6},{6,7},{15,8},{8,9},{9,10... | collective-permute-start | bytes 393224 | tf_op jit(solution)/shard_map/ppermute | solution.py:304
  102.9 3.0 %collective-permute-start.9 = (f32[2,128,128]{2,1,0:T(8,128)S(1)}, f32[2,128,128]{2,1,0:T(8,128)S(1)}, u32[]{:S(2)}, u32[]{:S(2)}) collective-permute-start(f32[2,128,128]{2,1,0:T(8,128)S(1)} %get-tuple-element.53), channel_id=1, source_target_pairs={{1,0},{2,1},{3,2},{4,3},{5,4},{6,5},{7,6},{0,7},{9,8},{10,9},{11,1... | collective-permute-start | bytes 393224 | tf_op jit(solution)/shard_map/ppermute | solution.py:304
  105.8 1.8 %collective-permute-start.11 = (f32[2,128,128]{2,1,0:T(8,128)S(1)}, f32[2,128,128]{2,1,0:T(8,128)S(1)}, u32[]{:S(2)}, u32[]{:S(2)}) collective-permute-start(f32[2,128,128]{2,1,0:T(8,128)S(1)} %get-tuple-element.54), channel_id=1, source_target_pairs={{0,16},{8,24},{16,0},{24,8},{1,17},{9,25},{17,1},{25,9},{2,18},{10... | collective-permute-start | bytes 393224 | tf_op jit(solution)/shard_map/ppermute | solution.py:312
  107.6 2.0 %collective-permute-done.8.refs_2_ = f32[2,128,128]{2,1,0:T(8,128)S(1)} collective-permute-done((f32[2,128,128]{2,1,0:T(8,128)S(1)}, f32[2,128,128]{2,1,0:T(8,128)S(1)}, u32[]{:S(2)}, u32[]{:S(2)}) %collective-permute-start.8) | collective-permute-done | bytes 131104 | tf_op jit(solution)/shard_map/ppermute | solution.py:304
  109.6 1.4 %collective-permute-done.9.refs_3_ = f32[2,128,128]{2,1,0:T(8,128)S(1)} collective-permute-done((f32[2,128,128]{2,1,0:T(8,128)S(1)}, f32[2,128,128]{2,1,0:T(8,128)S(1)}, u32[]{:S(2)}, u32[]{:S(2)}) %collective-permute-start.9) | collective-permute-done | bytes 131104 | tf_op jit(solution)/shard_map/ppermute | solution.py:304
  111.0 2.0 %density.1 = f32[2,4,128,128]{3,2,1,0:T(8,128)} custom-call(s32[64,4]{1,0:T(8,128)S(1)} %copy.5.refs_0_, f32[2,4,128,128]{3,2,1,0:T(8,128)S(1)} %get-tuple-element.51.refs_1_, f32[2,128,128]{2,1,0:T(8,128)S(1)} %collective-permute-done.8.refs_2_, f32[2,128,128]{2,1,0:T(8,128)S(1)} %collective-permute-done.9.refs_3_, ...), custom_call_target="tpu_custom_call" | custom-call | bytes 1573888 | tf_op jit(solution)/shard_map/density/pallas_call | solution.py:330
  (47 shorter events, 13.5 us)
Async XLA Ops:
  0.0 1.0 copy-start
  1.2 11.7 %collective-permute-start = (f32[2,200,128]{2,1,0:T(8,128)S(1)}, f32[2,200,128]{2,1,0:T(8,128)S(1)}, u32[]{:S(2)}, u32[]{:S(2)}) collective-permute-start(f32[2,200,128]{2,1,0:T(8,128)S(1)} %get-tuple-element.31), channel_id=1, source_target_pairs={{7,0},{0,1},{1,2},{2,3},{3,4},{4,5},{5,6},{6,7},{15,8},{8,9},{9,10... | collective-permute-start | bytes 614408 | tf_op jit(solution)/shard_map/ppermute | solution.py:304
  4.2 10.9 %collective-permute-start.1 = (f32[2,200,128]{2,1,0:T(8,128)S(1)}, f32[2,200,128]{2,1,0:T(8,128)S(1)}, u32[]{:S(2)}, u32[]{:S(2)}) collective-permute-start(f32[2,200,128]{2,1,0:T(8,128)S(1)} %get-tuple-element.32), channel_id=1, source_target_pairs={{1,0},{2,1},{3,2},{4,3},{5,4},{6,5},{7,6},{0,7},{9,8},{10,9},{11,1... | collective-permute-start | bytes 614408 | tf_op jit(solution)/shard_map/ppermute | solution.py:304
  7.3 7.8 %collective-permute-start.3 = (f32[2,200,128]{2,1,0:T(8,128)S(1)}, f32[2,200,128]{2,1,0:T(8,128)S(1)}, u32[]{:S(2)}, u32[]{:S(2)}) collective-permute-start(f32[2,200,128]{2,1,0:T(8,128)S(1)} %get-tuple-element.33), channel_id=1, source_target_pairs={{0,16},{8,24},{16,0},{24,8},{1,17},{9,25},{17,1},{25,9},{2,18},{10... | collective-permute-start | bytes 614408 | tf_op jit(solution)/shard_map/ppermute | solution.py:312
  8.9 6.2 %collective-permute-start.2 = (f32[2,200,128]{2,1,0:T(8,128)S(1)}, f32[2,200,128]{2,1,0:T(8,128)S(1)}, u32[]{:S(2)}, u32[]{:S(2)}) collective-permute-start(f32[2,200,128]{2,1,0:T(8,128)S(1)} %get-tuple-element.33), channel_id=1, source_target_pairs={{0,8},{8,0},{16,24},{24,16},{1,9},{9,1},{17,25},{25,17},{2,10},{10... | collective-permute-start | bytes 614408 | tf_op jit(solution)/shard_map/ppermute | solution.py:312
  19.7 1.0 copy-start.13
  21.7 1.0 copy-start.17
  22.7 1.0 copy-start.19
  23.7 17.4 %all-to-all-start = ((f32[32,8,128]{2,1,0:T(8,128)}), f32[32,8,128]{2,1,0:T(8,128)S(1)}, u32[]{:S(2)}, u32[]{:S(2)}) async-start(f32[32,8,128]{2,1,0:T(8,128)} %get-tuple-element.34), calls=%async_computation | async-start | bytes 262144 | tf_op jit(solution)/shard_map/all_to_all | solution.py:373
  28.5 1.2 %copy-start.14 = (bf16[2,512,512]{2,1,0:T(8,128)(2,1)S(1)}, bf16[2,512,512]{2,1,0:T(8,128)(2,1)}, u32[]{:S(2)}) copy-start(bf16[2,512,512]{2,1,0:T(8,128)(2,1)} %copy-done.13) | copy-start | bytes 3145732
  29.7 1.2 %copy-start.16 = (bf16[2,512,512]{2,1,0:T(8,128)(2,1)S(1)}, bf16[2,512,512]{2,1,0:T(8,128)(2,1)}, u32[]{:S(2)}) copy-start(bf16[2,512,512]{2,1,0:T(8,128)(2,1)} %copy-done.15) | copy-start | bytes 3145732
  30.9 1.2 %copy-start.18 = (bf16[2,512,512]{2,1,0:T(8,128)(2,1)S(1)}, bf16[2,512,512]{2,1,0:T(8,128)(2,1)}, u32[]{:S(2)}) copy-start(bf16[2,512,512]{2,1,0:T(8,128)(2,1)} %copy-done.17) | copy-start | bytes 3145732
  32.1 1.2 %copy-start.20 = (bf16[2,512,512]{2,1,0:T(8,128)(2,1)S(1)}, bf16[2,512,512]{2,1,0:T(8,128)(2,1)}, u32[]{:S(2)}) copy-start(bf16[2,512,512]{2,1,0:T(8,128)(2,1)} %copy-done.19) | copy-start | bytes 3145732
  38.4 2.6 %copy-start.11 = (f32[2,4,3,256,256]{4,3,2,1,0:T(8,128)}, f32[2,4,3,256,256]{4,3,2,1,0:T(8,128)S(1)}, u32[]{:S(2)}) copy-start(f32[2,4,3,256,256]{4,3,2,1,0:T(8,128)S(1)} %powers.2) | copy-start | bytes 18874372
  41.1 2.8 %copy-start.12 = (f32[2,4,3,256,256]{4,3,2,1,0:T(8,128)S(1)}, f32[2,4,3,256,256]{4,3,2,1,0:T(8,128)}, u32[]{:S(2)}) copy-start(f32[2,4,3,256,256]{4,3,2,1,0:T(8,128)} %copy-done.11) | copy-start | bytes 18874372
  43.9 22.7 %copy-start.8 = (f32[2,7,128,128]{3,2,1,0:T(8,128)S(1)}, f32[2,7,128,128]{3,2,1,0:T(8,128)}, u32[]{:S(2)}) copy-start(f32[2,7,128,128]{3,2,1,0:T(8,128)} %copy-done.7) | copy-start | bytes 2752516
  53.5 10.9 %collective-permute-start.4 = (f32[2,200,128]{2,1,0:T(8,128)S(1)}, f32[2,200,128]{2,1,0:T(8,128)S(1)}, u32[]{:S(2)}, u32[]{:S(2)}) collective-permute-start(f32[2,200,128]{2,1,0:T(8,128)S(1)} %get-tuple-element.42), channel_id=1, source_target_pairs={{7,0},{0,1},{1,2},{2,3},{3,4},{4,5},{5,6},{6,7},{15,8},{8,9},{9,10... | collective-permute-start | bytes 614408 | tf_op jit(solution)/shard_map/ppermute | solution.py:304
  55.4 11.2 %collective-permute-start.5 = (f32[2,200,128]{2,1,0:T(8,128)S(1)}, f32[2,200,128]{2,1,0:T(8,128)S(1)}, u32[]{:S(2)}, u32[]{:S(2)}) collective-permute-start(f32[2,200,128]{2,1,0:T(8,128)S(1)} %get-tuple-element.43), channel_id=1, source_target_pairs={{1,0},{2,1},{3,2},{4,3},{5,4},{6,5},{7,6},{0,7},{9,8},{10,9},{11,1... | collective-permute-start | bytes 614408 | tf_op jit(solution)/shard_map/ppermute | solution.py:304
  58.3 8.3 %collective-permute-start.7 = (f32[2,200,128]{2,1,0:T(8,128)S(1)}, f32[2,200,128]{2,1,0:T(8,128)S(1)}, u32[]{:S(2)}, u32[]{:S(2)}) collective-permute-start(f32[2,200,128]{2,1,0:T(8,128)S(1)} %get-tuple-element.44), channel_id=1, source_target_pairs={{0,16},{8,24},{16,0},{24,8},{1,17},{9,25},{17,1},{25,9},{2,18},{10... | collective-permute-start | bytes 614408 | tf_op jit(solution)/shard_map/ppermute | solution.py:312
  60.1 6.5 %collective-permute-start.6 = (f32[2,200,128]{2,1,0:T(8,128)S(1)}, f32[2,200,128]{2,1,0:T(8,128)S(1)}, u32[]{:S(2)}, u32[]{:S(2)}) collective-permute-start(f32[2,200,128]{2,1,0:T(8,128)S(1)} %get-tuple-element.44), channel_id=1, source_target_pairs={{0,8},{8,0},{16,24},{24,16},{1,9},{9,1},{17,25},{25,17},{2,10},{10... | collective-permute-start | bytes 614408 | tf_op jit(solution)/shard_map/ppermute | solution.py:312
  70.2 1.0 copy-start.1
  72.2 1.0 copy-start.5
  73.2 15.8 %all-to-all-start.1 = ((f32[32,8,128]{2,1,0:T(8,128)}), f32[32,8,128]{2,1,0:T(8,128)S(1)}, u32[]{:S(2)}, u32[]{:S(2)}) async-start(f32[32,8,128]{2,1,0:T(8,128)} %get-tuple-element.45), calls=%async_computation.1 | async-start | bytes 262144 | tf_op jit(solution)/shard_map/all_to_all | solution.py:373
  77.5 1.2 %copy-start.2 = (bf16[2,512,512]{2,1,0:T(8,128)(2,1)S(1)}, bf16[2,512,512]{2,1,0:T(8,128)(2,1)}, u32[]{:S(2)}) copy-start(bf16[2,512,512]{2,1,0:T(8,128)(2,1)} %copy-done.1) | copy-start | bytes 3145732
  78.8 1.2 %copy-start.4 = (bf16[2,512,512]{2,1,0:T(8,128)(2,1)S(1)}, bf16[2,512,512]{2,1,0:T(8,128)(2,1)}, u32[]{:S(2)}) copy-start(bf16[2,512,512]{2,1,0:T(8,128)(2,1)} %copy-done.3) | copy-start | bytes 3145732
  80.0 1.2 %copy-start.6 = (bf16[2,512,512]{2,1,0:T(8,128)(2,1)S(1)}, bf16[2,512,512]{2,1,0:T(8,128)(2,1)}, u32[]{:S(2)}) copy-start(bf16[2,512,512]{2,1,0:T(8,128)(2,1)} %copy-done.5) | copy-start | bytes 3145732
  86.3 2.6 %copy-start.9 = (f32[2,4,3,256,256]{4,3,2,1,0:T(8,128)}, f32[2,4,3,256,256]{4,3,2,1,0:T(8,128)S(1)}, u32[]{:S(2)}) copy-start(f32[2,4,3,256,256]{4,3,2,1,0:T(8,128)S(1)} %powers.3) | copy-start | bytes 18874372
  88.9 2.8 %copy-start.10 = (f32[2,4,3,256,256]{4,3,2,1,0:T(8,128)S(1)}, f32[2,4,3,256,256]{4,3,2,1,0:T(8,128)}, u32[]{:S(2)}) copy-start(f32[2,4,3,256,256]{4,3,2,1,0:T(8,128)} %copy-done.9) | copy-start | bytes 18874372
  101.1 8.5 %collective-permute-start.8 = (f32[2,128,128]{2,1,0:T(8,128)S(1)}, f32[2,128,128]{2,1,0:T(8,128)S(1)}, u32[]{:S(2)}, u32[]{:S(2)}) collective-permute-start(f32[2,128,128]{2,1,0:T(8,128)S(1)} %get-tuple-element.52), channel_id=1, source_target_pairs={{7,0},{0,1},{1,2},{2,3},{3,4},{4,5},{5,6},{6,7},{15,8},{8,9},{9,10... | collective-permute-start | bytes 393224 | tf_op jit(solution)/shard_map/ppermute | solution.py:304
  102.9 8.1 %collective-permute-start.9 = (f32[2,128,128]{2,1,0:T(8,128)S(1)}, f32[2,128,128]{2,1,0:T(8,128)S(1)}, u32[]{:S(2)}, u32[]{:S(2)}) collective-permute-start(f32[2,128,128]{2,1,0:T(8,128)S(1)} %get-tuple-element.53), channel_id=1, source_target_pairs={{1,0},{2,1},{3,2},{4,3},{5,4},{6,5},{7,6},{0,7},{9,8},{10,9},{11,1... | collective-permute-start | bytes 393224 | tf_op jit(solution)/shard_map/ppermute | solution.py:304
  105.8 5.2 %collective-permute-start.11 = (f32[2,128,128]{2,1,0:T(8,128)S(1)}, f32[2,128,128]{2,1,0:T(8,128)S(1)}, u32[]{:S(2)}, u32[]{:S(2)}) collective-permute-start(f32[2,128,128]{2,1,0:T(8,128)S(1)} %get-tuple-element.54), channel_id=1, source_target_pairs={{0,16},{8,24},{16,0},{24,8},{1,17},{9,25},{17,1},{25,9},{2,18},{10... | collective-permute-start | bytes 393224 | tf_op jit(solution)/shard_map/ppermute | solution.py:312
  107.6 3.4 %collective-permute-start.10 = (f32[2,128,128]{2,1,0:T(8,128)S(1)}, f32[2,128,128]{2,1,0:T(8,128)S(1)}, u32[]{:S(2)}, u32[]{:S(2)}) collective-permute-start(f32[2,128,128]{2,1,0:T(8,128)S(1)} %get-tuple-element.54), channel_id=1, source_target_pairs={{0,8},{8,0},{16,24},{24,16},{1,9},{9,1},{17,25},{25,17},{2,10},{10... | collective-permute-start | bytes 393224 | tf_op jit(solution)/shard_map/ppermute | solution.py:312
  (3 other events, 2.8 us)

commit v2 on v1

--- a/solution.py
+++ b/solution.py
@@ -47,6 +47,17 @@
     tile = order // 2
     for place, (row, col) in enumerate(((0, 0), (0, 1), (1, 1))):
         yield place, pl.ds(row * tile, tile), pl.ds(col * tile, tile), row != col
+
+
+def square_tiles(high, low, mixed):
+    order = high.shape[0]
+    first, second = pl.ds(0, order // 2), pl.ds(order // 2, order // 2)
+    mixed[3] = dot(high[second, :], low[:, first])
+    for place, rows, columns, off in upper_tiles(order):
+        left = high[rows, :]
+        mixed[place] = dot(left, low[:, columns])
+        tile = dot(left, high[:, columns]) + (mixed[place] + turned(mixed[3 if off else place]))
+        yield place, rows, columns, off, tile
 
 
 def store_split(target, slot, rows, columns, value, mirror):
@@ -59,12 +70,32 @@
         target[1][slot, columns, rows] = low
 
 
+def store_arrow(target, slot, blocks):
+    members = (len(blocks) + 1) // 2
+    empty = jnp.zeros((SIDE, SIDE), f32)
+    for row in range(members):
+        for col in range(members):
+            if col == 0:
+                value = blocks[row]
+            elif row == 0:
+                value = turned(blocks[col])
+            elif row == col:
+                value = blocks[members - 1 + row]
+            else:
+                value = empty
+            at = (pl.ds(row * SIDE, SIDE), pl.ds(col * SIDE, SIDE))
+            store_split(target, slot, *at, value, False)
+
+
 def lanes(shape):
     return lax.broadcasted_iota(jnp.int32, shape, 1)
 
 
 def rows_of(shape):
     return lax.broadcasted_iota(jnp.int32, shape, 0)
+
+
+TILE_BLOCKS = ((0, 1, None, 4), (2, 3, 5, 6), (7, 8, None, 9))
 
 
 def pack(block):
@@ -137,118 +168,84 @@
     return faces, [unpack(b, d[0:1, :]) for b, d in zip(bodies, diagonals)]
 
 
-def assemble_kernel(cols, members, has_base, last, *refs):
+def assemble_kernel(cols, members, has_base, *refs):
     lists, half = refs[:2]
     base = refs[2] if has_base else None
-    outputs = 6 + (not last)
-    received = refs[2 + has_base : -outputs]
-    norms, dense, s_high, s_low, q_high, q_low = refs[-outputs:][:6]
-    blocks = None if last else refs[-1]
+    received = refs[2 + has_base : -5]
+    norms, blocks, s_high, s_low, mixed = refs[-5:]
     slots = half.shape[0]
-    order = members * SIDE
     top = None
     links = my_links(lists, cols, slots)
     for slot in range(slots):
         present, bit = links[slot]
         faces, diagonals = neighbour_parts(slot, bit, received, True)
-
-        def place(row, col, value):
-            high, low = split(value)
-            at = (slot, pl.ds(row * SIDE, SIDE), pl.ds(col * SIDE, SIDE))
-            s_high[at] = high
-            s_low[at] = low
-            if row // 2 <= col // 2:
-                inner = (pl.ds(row % 2 * SIDE, SIDE), pl.ds(col % 2 * SIDE, SIDE))
-                dense[(slot, row // 2 + col // 2, *inner)] = value
-
-        centre = half[slot, 0]
+        parts = [half[slot, 0]]
+        parts += [present[k] * (half[slot, k] + 0.5 * turned(faces[k - 1])) for k in range(1, members)]
+        parts += [present[k] * diagonals[k - 1] for k in range(1, members)]
         if has_base:
-            centre = centre + base[slot, 0]
-        if not last:
-            blocks[slot, 0] = centre
-        place(0, 0, centre)
-        empty = jnp.zeros((SIDE, SIDE), f32)
-        for k in range(1, members):
-            column = present[k] * (half[slot, k] + 0.5 * turned(faces[k - 1]))
-            block = present[k] * diagonals[k - 1]
-            if has_base:
-                column = column + base[slot, k]
-                block = block + base[slot, members - 1 + k]
-            if not last:
-                blocks[slot, k] = column
-                blocks[slot, members - 1 + k] = block
-            place(k, 0, column)
-            place(0, k, turned(column))
-            place(k, k, block)
-            for other in range(1, members):
-                if other != k:
-                    place(k, other, empty)
-    for slot in range(slots):
-        matrix = (s_high.at[slot], s_low.at[slot])
+            parts = [part + base[slot, place] for place, part in enumerate(parts)]
+        for place, part in enumerate(parts):
+            blocks[slot, place] = part
+        store_arrow((s_high, s_low), slot, parts)
+    for slot in range(slots):
         total = None
-        for _, rows, columns, off in upper_tiles(order):
-            tile = product(matrix, matrix, rows, columns)
+        for _, _, _, off, tile in square_tiles(s_high.at[slot], s_low.at[slot], mixed.at[slot]):
             part = jnp.sum(tile * tile, axis=0, keepdims=True)
             part = 2.0 * part if off else part
             total = part if total is None else total + part
-            store_split((q_high, q_low), slot, rows, columns, tile, off)
         total = jnp.sum(total, axis=1, keepdims=True)
         top = total if top is None else jnp.maximum(top, total)
     norms[...] = jnp.broadcast_to(top.reshape(1, 1, 1), norms.shape)
 
 
-def powers_kernel(s_high, s_low, q_high, q_low, powers, p_high, p_low):
-    slots, count = powers.shape[:2]
-    order = s_high.shape[1]
-    for power in range(count):
-        for slot in range(slots):
-            square = (q_high.at[slot], q_low.at[slot])
-            if power == 0:
-                lower = (s_high.at[slot], s_low.at[slot])
-            else:
-                lower = (p_high.at[power % 2, slot], p_low.at[power % 2, slot])
-            target = (p_high.at[1 - power % 2], p_low.at[1 - power % 2])
-            for place, rows, columns, off in upper_tiles(order):
-                tile = product(lower, square, rows, columns)
-                powers[slot, power, place] = tile
-                if power + 1 < count:
-                    store_split(target, slot, rows, columns, tile, off)
-
-
-def two_steps():
-    once = {1: 1.5, 3: -0.5}
-    cube = {0: 1.0}
-    for _ in range(3):
-        grown = {}
-        for i, a in cube.items():
-            for j, b in once.items():
-                grown[i + j] = grown.get(i + j, 0.0) + a * b
-        cube = grown
-    return [1.5 * once.get(i, 0.0) - 0.5 * cube.get(i, 0.0) for i in range(1, 10, 2)]
-
-
-def sign_kernel(members, last, norms, dense, powers, own, to_right, to_left, to_partner, x, xh, xl, yh, yl):
-    slots = dense.shape[0]
+def cube_kernel(blocks, out, s_high, s_low, q_high, q_low, mixed):
+    slots, count = blocks.shape[:2]
+    for slot in range(slots):
+        parts = [blocks[slot, place] for place in range(count)]
+        store_arrow((s_high, s_low), slot, parts)
+        for place, part in enumerate(parts):
+            out[slot, place] = part
+    for slot in range(slots):
+        for _, rows, columns, off, tile in square_tiles(s_high.at[slot], s_low.at[slot], mixed.at[slot]):
+            store_split((q_high, q_low), slot, rows, columns, tile, off)
+    for slot in range(slots):
+        matrix = (s_high.at[slot], s_low.at[slot])
+        square = (q_high.at[slot], q_low.at[slot])
+        for place, rows, columns, _ in upper_tiles(s_high.shape[1]):
+            tile = product(matrix, square, rows, columns)
+            for inner, at in enumerate(TILE_BLOCKS[place]):
+                if at is not None:
+                    row, col = inner // 2 * SIDE, inner % 2 * SIDE
+                    out[slot, count + at] = tile[row : row + SIDE, col : col + SIDE]
+
+
+def sign_kernel(members, last, norms, source, own, to_right, to_left, to_partner, x, xh, xl, yh, yl, mixed):
+    slots = source.shape[0]
     order = members * SIDE
     largest = jnp.max(jnp.max(norms[...], axis=0), axis=(0, 1), keepdims=True)
     scaling = 1.5 / jnp.sqrt(jnp.sqrt(largest + epsilon))
-    factors, power = [], scaling
-    for coefficient in two_steps():
-        factors.append(coefficient * power)
-        power = power * (scaling * scaling)
-    for slot in range(slots):
-        for place, rows, columns, off in upper_tiles(order):
-            value = factors[0] * dense[slot, place]
-            for k in range(1, len(factors)):
-                value = value + factors[k] * powers[slot, k - 1, place]
-            x[slot, rows, columns] = value
-            store_split((xh.at[0], xl.at[0]), slot, rows, columns, value, off)
+    linear = 1.5 * scaling
+    cubic = -0.5 * (scaling * scaling * scaling)
+    for slot in range(slots):
+        at = 2 * members - 1
+        for row in range(members):
+            for col in range(row, members):
+                value = cubic * source[slot, at]
+                if row == col:
+                    value = value + linear * source[slot, members - 1 + row if row else 0]
+                elif row == 0:
+                    value = value + linear * turned(source[slot, col])
+                spans = (pl.ds(row * SIDE, SIDE), pl.ds(col * SIDE, SIDE))
+                x[(slot, *spans)] = value
+                if row // 2 == col // 2 and row != col:
+                    x[(slot, *spans[::-1])] = turned(value)
+                store_split((xh.at[0], xl.at[0]), slot, *spans, value, row != col)
+                at += 1
     now = 0
-    for repeat in range(2, ITERS - 1):
+    for repeat in range(1, ITERS - 1):
         for slot in range(slots):
             iterate = (xh.at[now, slot], xl.at[now, slot])
-            for _, rows, columns, off in upper_tiles(order):
-                tile = product(iterate, iterate, rows, columns)
+            for _, rows, columns, off, tile in square_tiles(*iterate, mixed.at[slot]):
                 store_split((yh, yl), slot, rows, columns, tile, off)
         for slot in range(slots):
             iterate = (xh.at[now, slot], xl.at[now, slot])
@@ -342,51 +339,49 @@
 def per_device(hamiltonian, block_lists):
     slots, members = hamiltonian.shape[:2]
     order = members * SIDE
-    tile = order // 2
     cols = lax.axis_size("col")
     devices = lax.axis_size("row") * cols
     face = shape(slots, SIDE, SIDE)
     full = shape(slots, SIDE + PACKED, SIDE)
     own = shape(slots, members, SIDE, SIDE)
-    part = shape(slots, order, order, dtype=bf16)
+    arrow = 2 * members - 1
     part_scratch = pltpu.VMEM((slots, order, order), bf16)
     both_scratch = pltpu.VMEM((2, slots, order, order), bf16)
+    mixed_scratch = pltpu.VMEM((slots, 4, order // 2, order // 2), f32)
     multiply = slots * 3 * 3 * order * order * order // 2
-    count = len(two_steps()) - 1
 
     half, *sent = call(pack_kernel, "pack", [hamiltonian], [own] + [full] * 3)
     base = []
     for step in range(STEPS):
         last = step == STEPS - 1
         received = exchange(*sent)
-        norms, dense, *parts = call(
-            functools.partial(assemble_kernel, cols, members, len(base), last),
+        norms, blocks = call(
+            functools.partial(assemble_kernel, cols, members, len(base)),
             "assemble",
             [block_lists, half, *base, *received],
-            [shape(devices, 8, SIDE), shape(slots, 3, tile, tile)]
-            + [part] * 4
-            + ([] if last else [shape(slots, 2 * members - 1, SIDE, SIDE)]),
+            [shape(devices, 8, SIDE), shape(slots, arrow, SIDE, SIDE)],
+            [part_scratch] * 2 + [mixed_scratch],
             flops=multiply,
             smem_first=True,
         )
-        base = parts[4:]
         norms = lax.all_to_all(norms, ("row", "col"), 0, 0, tiled=True)
-        (powers,) = call(
-            powers_kernel,
-            "powers",
-            parts[:4],
-            [shape(slots, count, 3, tile, tile)],
-            [both_scratch] * 2,
-            flops=count * multiply,
+        (source,) = call(
+            cube_kernel,
+            "cube",
+            [blocks],
+            [shape(slots, arrow + members * (members + 1) // 2, SIDE, SIDE)],
+            [part_scratch] * 4 + [mixed_scratch],
+            flops=2 * multiply,
         )
         half, *sent = call(
             functools.partial(sign_kernel, members, last),
             "sign",
-            [norms, dense, powers],
+            [norms, source],
             [own] + [face if last else full] * 3,
-            [pltpu.VMEM((slots, order, order), f32)] + [both_scratch] * 2 + [part_scratch] * 2,
-            flops=7 * multiply,
+            [pltpu.VMEM((slots, order, order), f32)] + [both_scratch] * 2 + [part_scratch] * 2 + [mixed_scratch],
+            flops=8 * multiply,
         )
+        base = [source]
     received = exchange(*sent)
     (density,) = call(
         functools.partial(density_kernel, cols, members),

time: 114 us -> 90.9 us (0.80)
  local copies, waits for them, and re-layouts: 29 us -> 1.81 us
  waiting for transfers between devices: 15.4 us -> 26.4 us
  starting transfers between devices: 30 us -> 26.6 us
  Pallas kernels: 38.6 us -> 35.7 us
    unnamed x43 -> x3, local copies, waits for them, and re-layouts: 29 us -> 1.81 us
    all_to_all x2, waiting for transfers between devices: 0.01 us -> 10.4 us  [per_device(): norms = lax.all_to_all(norms, ('row', 'col'), 0, 0, tiled=True)]
    pallas_call x8, Pallas kernels: 38.6 us -> 35.7 us  [call(): pl.pallas_call(kernel, out_shape=list(outputs), in_specs=specs, out_specs...]
    all_to_all x2, starting transfers between devices: 9.15 us -> 7.19 us  [per_device(): norms = lax.all_to_all(norms, ('row', 'col'), 0, 0, tiled=True)]
    ppermute x6, starting transfers between devices: 5.13 us -> 3.71 us  [exchange(): lax.ppermute(to_partner, 'row', [(i, i ^ place) for i in rows])]
  transfers between devices with their start and end apart: 14 -> 14, of which waited for: 6 -> 9; matrix products, arithmetic and copies ran while one was open for 1% -> 1% of each run, Pallas kernels for 9% -> 6%
where the time goes in v2:
time: 90.9 us; the launch traced here: 90.6 us
  Pallas kernels  35.7 us (39%)
  starting transfers between devices  26.6 us (29%)
  waiting for transfers between devices  26.4 us (29%)
  local copies, waits for them, and re-layouts  1.81 us (2%)
    pallas_call x8, Pallas kernels, call(): pl.pallas_call(kernel, out_shape=list(outputs), in_specs=specs, out_specs...  35.7 us
    ppermute x6, starting transfers between devices, from_behind(): lax.ppermute(block, axis, [((i - distance) % len(devices), i) for i in de...  15.7 us
    ppermute x6, waiting for transfers between devices, from_behind(): lax.ppermute(block, axis, [((i - distance) % len(devices), i) for i in de...  15.6 us
    all_to_all x2, waiting for transfers between devices, per_device(): norms = lax.all_to_all(norms, ('row', 'col'), 0, 0, tiled=True)  10.4 us
    all_to_all x2, starting transfers between devices, per_device(): norms = lax.all_to_all(norms, ('row', 'col'), 0, 0, tiled=True)  7.19 us
    ppermute x6, starting transfers between devices, exchange(): lax.ppermute(to_partner, 'row', [(i, i ^ place) for i in rows])  3.71 us
  transfers between devices with their start and end apart: 14, of which 9 were waited for; matrix products, arithmetic and copies ran while one was open for 1% of the time, Pallas kernels for 6%

profile of v2, /device:TPU:0, one launch (start us, length us, event | category | flops | bytes accessed | tf_op | source)
XLA Modules:
  0.0 90.6 jit_solution(4678661741052225505)
XLA Ops:
  0.0 1.0 %copy-done = f32[2,4,128,128]{3,2,1,0:T(8,128)S(1)} copy-done((f32[2,4,128,128]{3,2,1,0:T(8,128)S(1)}, f32[2,4,128,128]{3,2,1,0:T(8,128)}, u32[]{:S(2)}) %copy-start) | copy-done | bytes 524312
  1.0 0.2 pack.1
  1.2 3.0 %collective-permute-start = (f32[2,200,128]{2,1,0:T(8,128)S(1)}, f32[2,200,128]{2,1,0:T(8,128)S(1)}, u32[]{:S(2)}, u32[]{:S(2)}) collective-permute-start(f32[2,200,128]{2,1,0:T(8,128)S(1)} %get-tuple-element.22), channel_id=1, source_target_pairs={{7,0},{0,1},{1,2},{2,3},{3,4},{4,5},{5,6},{6,7},{15,8},{8,9},{9,10... | collective-permute-start | bytes 614408 | tf_op jit(solution)/shard_map/ppermute | solution.py:301
  4.2 3.1 %collective-permute-start.1 = (f32[2,200,128]{2,1,0:T(8,128)S(1)}, f32[2,200,128]{2,1,0:T(8,128)S(1)}, u32[]{:S(2)}, u32[]{:S(2)}) collective-permute-start(f32[2,200,128]{2,1,0:T(8,128)S(1)} %get-tuple-element.23), channel_id=1, source_target_pairs={{1,0},{2,1},{3,2},{4,3},{5,4},{6,5},{7,6},{0,7},{9,8},{10,9},{11,1... | collective-permute-start | bytes 614408 | tf_op jit(solution)/shard_map/ppermute | solution.py:301
  7.3 1.6 %collective-permute-start.3 = (f32[2,200,128]{2,1,0:T(8,128)S(1)}, f32[2,200,128]{2,1,0:T(8,128)S(1)}, u32[]{:S(2)}, u32[]{:S(2)}) collective-permute-start(f32[2,200,128]{2,1,0:T(8,128)S(1)} %get-tuple-element.24), channel_id=1, source_target_pairs={{0,16},{8,24},{16,0},{24,8},{1,17},{9,25},{17,1},{25,9},{2,18},{10... | collective-permute-start | bytes 614408 | tf_op jit(solution)/shard_map/ppermute | solution.py:309
  8.9 0.0 collective-permute-start.2
  8.9 0.8 copy.5.refs_0_
  9.7 3.3 %collective-permute-done.refs_2_ = f32[2,200,128]{2,1,0:T(8,128)S(1)} collective-permute-done((f32[2,200,128]{2,1,0:T(8,128)S(1)}, f32[2,200,128]{2,1,0:T(8,128)S(1)}, u32[]{:S(2)}, u32[]{:S(2)}) %collective-permute-start) | collective-permute-done | bytes 204832 | tf_op jit(solution)/shard_map/ppermute | solution.py:301
  13.0 2.2 %collective-permute-done.1.refs_3_ = f32[2,200,128]{2,1,0:T(8,128)S(1)} collective-permute-done((f32[2,200,128]{2,1,0:T(8,128)S(1)}, f32[2,200,128]{2,1,0:T(8,128)S(1)}, u32[]{:S(2)}, u32[]{:S(2)}) %collective-permute-start.1) | collective-permute-done | bytes 204832 | tf_op jit(solution)/shard_map/ppermute | solution.py:301
  15.2 3.3 %assemble.2 = (f32[32,8,128]{2,1,0:T(8,128)}, f32[2,7,128,128]{3,2,1,0:T(8,128)S(1)}) custom-call(s32[64,4]{1,0:T(8,128)S(1)} %copy.5.refs_0_, f32[2,4,128,128]{3,2,1,0:T(8,128)S(1)} %get-tuple-element.21.refs_1_, f32[2,200,128]{2,1,0:T(8,128)S(1)} %collective-permute-done.refs_2_, f32[2,200,128]{2,1,0:T(8,128)S(1)} %collective-permute-done.1.refs_3_, ...), custom_call_target="tpu_custom_call" | custom-call | flops 1207959552 | bytes 2393088 | tf_op jit(solution)/shard_map/assemble/pallas_call | solution.py:327
  18.4 4.6 %all-to-all-start = ((f32[32,8,128]{2,1,0:T(8,128)}), f32[32,8,128]{2,1,0:T(8,128)S(1)}, u32[]{:S(2)}, u32[]{:S(2)}) async-start(f32[32,8,128]{2,1,0:T(8,128)} %get-tuple-element.25), calls=%async_computation | async-start | bytes 262144 | tf_op jit(solution)/shard_map/all_to_all | solution.py:367
  23.1 2.5 %cube.2.source.refs_2_ = f32[2,17,128,128]{3,2,1,0:T(8,128)S(1)} custom-call(f32[2,7,128,128]{3,2,1,0:T(8,128)S(1)} %get-tuple-element.26.blocks), custom_call_target="tpu_custom_call" | custom-call | flops 2415919104 | bytes 3145728 | tf_op jit(solution)/shard_map/cube/pallas_call | solution.py:327
  25.6 5.2 %all-to-all-done.norms = f32[32,8,128]{2,1,0:T(8,128)S(1)} async-done(((f32[32,8,128]{2,1,0:T(8,128)}), f32[32,8,128]{2,1,0:T(8,128)S(1)}, u32[]{:S(2)}, u32[]{:S(2)}) %all-to-all-start) | async-done | bytes 131104 | tf_op jit(solution)/shard_map/all_to_all | solution.py:367
  30.8 11.1 %sign.2 = (f32[2,4,128,128]{3,2,1,0:T(8,128)S(1)}, f32[2,200,128]{2,1,0:T(8,128)S(1)}, f32[2,200,128]{2,1,0:T(8,128)S(1)}, f32[2,200,128]{2,1,0:T(8,128)S(1)}) custom-call(f32[32,8,128]{2,1,0:T(8,128)S(1)} %all-to-all-done.norms, f32[2,17,128,128]{3,2,1,0:T(8,128)S(1)} %cube.2.source.refs_2_), custom_call_target="tpu_custom_call" | custom-call | flops 9663676416 | bytes 3497984 | tf_op jit(solution)/shard_map/sign/pallas_call | solution.py:327
  41.9 1.3 %collective-permute-start.4 = (f32[2,200,128]{2,1,0:T(8,128)S(1)}, f32[2,200,128]{2,1,0:T(8,128)S(1)}, u32[]{:S(2)}, u32[]{:S(2)}) collective-permute-start(f32[2,200,128]{2,1,0:T(8,128)S(1)} %get-tuple-element.28), channel_id=1, source_target_pairs={{7,0},{0,1},{1,2},{2,3},{3,4},{4,5},{5,6},{6,7},{15,8},{8,9},{9,10... | collective-permute-start | bytes 614408 | tf_op jit(solution)/shard_map/ppermute | solution.py:301
  43.2 3.5 %collective-permute-start.5 = (f32[2,200,128]{2,1,0:T(8,128)S(1)}, f32[2,200,128]{2,1,0:T(8,128)S(1)}, u32[]{:S(2)}, u32[]{:S(2)}) collective-permute-start(f32[2,200,128]{2,1,0:T(8,128)S(1)} %get-tuple-element.29), channel_id=1, source_target_pairs={{1,0},{2,1},{3,2},{4,3},{5,4},{6,5},{7,6},{0,7},{9,8},{10,9},{11,1... | collective-permute-start | bytes 614408 | tf_op jit(solution)/shard_map/ppermute | solution.py:301
  46.7 1.1 %collective-permute-start.7 = (f32[2,200,128]{2,1,0:T(8,128)S(1)}, f32[2,200,128]{2,1,0:T(8,128)S(1)}, u32[]{:S(2)}, u32[]{:S(2)}) collective-permute-start(f32[2,200,128]{2,1,0:T(8,128)S(1)} %get-tuple-element.30), channel_id=1, source_target_pairs={{0,16},{8,24},{16,0},{24,8},{1,17},{9,25},{17,1},{25,9},{2,18},{10... | collective-permute-start | bytes 614408 | tf_op jit(solution)/shard_map/ppermute | solution.py:309
  47.7 0.0 collective-permute-start.6
  47.7 4.4 %collective-permute-done.4.refs_3_ = f32[2,200,128]{2,1,0:T(8,128)S(1)} collective-permute-done((f32[2,200,128]{2,1,0:T(8,128)S(1)}, f32[2,200,128]{2,1,0:T(8,128)S(1)}, u32[]{:S(2)}, u32[]{:S(2)}) %collective-permute-start.4) | collective-permute-done | bytes 204832 | tf_op jit(solution)/shard_map/ppermute | solution.py:301
  52.2 2.2 %collective-permute-done.5.refs_4_ = f32[2,200,128]{2,1,0:T(8,128)S(1)} collective-permute-done((f32[2,200,128]{2,1,0:T(8,128)S(1)}, f32[2,200,128]{2,1,0:T(8,128)S(1)}, u32[]{:S(2)}, u32[]{:S(2)}) %collective-permute-start.5) | collective-permute-done | bytes 204832 | tf_op jit(solution)/shard_map/ppermute | solution.py:301
  54.4 3.3 %assemble.3 = (f32[32,8,128]{2,1,0:T(8,128)}, f32[2,7,128,128]{3,2,1,0:T(8,128)S(1)}) custom-call(s32[64,4]{1,0:T(8,128)S(1)} %copy.5.refs_0_, f32[2,4,128,128]{3,2,1,0:T(8,128)S(1)} %get-tuple-element.27.refs_1_, f32[2,17,128,128]{3,2,1,0:T(8,128)S(1)} %cube.2.source.refs_2_, f32[2,200,128]{2,1,0:T(8,128)S(1)} %collective-permute-done.4.refs_3_, ...), custom_call_target="tpu_custom_call" | custom-call | flops 1207959552 | bytes 4621312 | tf_op jit(solution)/shard_map/assemble/pallas_call | solution.py:327
  57.7 2.6 %all-to-all-start.1 = ((f32[32,8,128]{2,1,0:T(8,128)}), f32[32,8,128]{2,1,0:T(8,128)S(1)}, u32[]{:S(2)}, u32[]{:S(2)}) async-start(f32[32,8,128]{2,1,0:T(8,128)} %get-tuple-element.31), calls=%async_computation.1 | async-start | bytes 262144 | tf_op jit(solution)/shard_map/all_to_all | solution.py:367
  60.2 2.5 %cube.3.source = f32[2,17,128,128]{3,2,1,0:T(8,128)S(1)} custom-call(f32[2,7,128,128]{3,2,1,0:T(8,128)S(1)} %get-tuple-element.32.blocks), custom_call_target="tpu_custom_call" | custom-call | flops 2415919104 | bytes 3145728 | tf_op jit(solution)/shard_map/cube/pallas_call | solution.py:327
  62.8 5.2 %all-to-all-done.1.norms = f32[32,8,128]{2,1,0:T(8,128)S(1)} async-done(((f32[32,8,128]{2,1,0:T(8,128)}), f32[32,8,128]{2,1,0:T(8,128)S(1)}, u32[]{:S(2)}, u32[]{:S(2)}) %all-to-all-start.1) | async-done | bytes 131104 | tf_op jit(solution)/shard_map/all_to_all | solution.py:367
  68.0 10.8 %sign.3 = (f32[2,4,128,128]{3,2,1,0:T(8,128)S(1)}, f32[2,128,128]{2,1,0:T(8,128)S(1)}, f32[2,128,128]{2,1,0:T(8,128)S(1)}, f32[2,128,128]{2,1,0:T(8,128)S(1)}) custom-call(f32[32,8,128]{2,1,0:T(8,128)S(1)} %all-to-all-done.1.norms, f32[2,17,128,128]{3,2,1,0:T(8,128)S(1)} %cube.3.source), custom_call_target="tpu_custom_call" | custom-call | flops 9663676416 | bytes 3276800 | tf_op jit(solution)/shard_map/sign/pallas_call | solution.py:327
  78.8 1.3 %collective-permute-start.8 = (f32[2,128,128]{2,1,0:T(8,128)S(1)}, f32[2,128,128]{2,1,0:T(8,128)S(1)}, u32[]{:S(2)}, u32[]{:S(2)}) collective-permute-start(f32[2,128,128]{2,1,0:T(8,128)S(1)} %get-tuple-element.34), channel_id=1, source_target_pairs={{7,0},{0,1},{1,2},{2,3},{3,4},{4,5},{5,6},{6,7},{15,8},{8,9},{9,10... | collective-permute-start | bytes 393224 | tf_op jit(solution)/shard_map/ppermute | solution.py:301
  80.1 3.5 %collective-permute-start.9 = (f32[2,128,128]{2,1,0:T(8,128)S(1)}, f32[2,128,128]{2,1,0:T(8,128)S(1)}, u32[]{:S(2)}, u32[]{:S(2)}) collective-permute-start(f32[2,128,128]{2,1,0:T(8,128)S(1)} %get-tuple-element.35), channel_id=1, source_target_pairs={{1,0},{2,1},{3,2},{4,3},{5,4},{6,5},{7,6},{0,7},{9,8},{10,9},{11,1... | collective-permute-start | bytes 393224 | tf_op jit(solution)/shard_map/ppermute | solution.py:301
  83.6 1.1 %collective-permute-start.11 = (f32[2,128,128]{2,1,0:T(8,128)S(1)}, f32[2,128,128]{2,1,0:T(8,128)S(1)}, u32[]{:S(2)}, u32[]{:S(2)}) collective-permute-start(f32[2,128,128]{2,1,0:T(8,128)S(1)} %get-tuple-element.36), channel_id=1, source_target_pairs={{0,16},{8,24},{16,0},{24,8},{1,17},{9,25},{17,1},{25,9},{2,18},{10... | collective-permute-start | bytes 393224 | tf_op jit(solution)/shard_map/ppermute | solution.py:309
  84.7 2.5 %collective-permute-done.8.refs_2_ = f32[2,128,128]{2,1,0:T(8,128)S(1)} collective-permute-done((f32[2,128,128]{2,1,0:T(8,128)S(1)}, f32[2,128,128]{2,1,0:T(8,128)S(1)}, u32[]{:S(2)}, u32[]{:S(2)}) %collective-permute-start.8) | collective-permute-done | bytes 131104 | tf_op jit(solution)/shard_map/ppermute | solution.py:301
  87.2 1.0 %collective-permute-done.9.refs_3_ = f32[2,128,128]{2,1,0:T(8,128)S(1)} collective-permute-done((f32[2,128,128]{2,1,0:T(8,128)S(1)}, f32[2,128,128]{2,1,0:T(8,128)S(1)}, u32[]{:S(2)}, u32[]{:S(2)}) %collective-permute-start.9) | collective-permute-done | bytes 131104 | tf_op jit(solution)/shard_map/ppermute | solution.py:301
  88.1 0.4 collective-permute-done.11.refs_5_
  88.6 2.0 %density.1 = f32[2,4,128,128]{3,2,1,0:T(8,128)} custom-call(s32[64,4]{1,0:T(8,128)S(1)} %copy.5.refs_0_, f32[2,4,128,128]{3,2,1,0:T(8,128)S(1)} %get-tuple-element.33.refs_1_, f32[2,128,128]{2,1,0:T(8,128)S(1)} %collective-permute-done.8.refs_2_, f32[2,128,128]{2,1,0:T(8,128)S(1)} %collective-permute-done.9.refs_3_, ...), custom_call_target="tpu_custom_call" | custom-call | bytes 1573888 | tf_op jit(solution)/shard_map/density/pallas_call | solution.py:327
  (7 shorter events, 0.0 us)
Async XLA Ops:
  0.0 1.0 %copy-start = (f32[2,4,128,128]{3,2,1,0:T(8,128)S(1)}, f32[2,4,128,128]{3,2,1,0:T(8,128)}, u32[]{:S(2)}) copy-start(f32[2,4,128,128]{3,2,1,0:T(8,128)} %own.1) | copy-start | bytes 1572868
  1.2 11.7 %collective-permute-start = (f32[2,200,128]{2,1,0:T(8,128)S(1)}, f32[2,200,128]{2,1,0:T(8,128)S(1)}, u32[]{:S(2)}, u32[]{:S(2)}) collective-permute-start(f32[2,200,128]{2,1,0:T(8,128)S(1)} %get-tuple-element.22), channel_id=1, source_target_pairs={{7,0},{0,1},{1,2},{2,3},{3,4},{4,5},{5,6},{6,7},{15,8},{8,9},{9,10... | collective-permute-start | bytes 614408 | tf_op jit(solution)/shard_map/ppermute | solution.py:301
  4.2 10.9 %collective-permute-start.1 = (f32[2,200,128]{2,1,0:T(8,128)S(1)}, f32[2,200,128]{2,1,0:T(8,128)S(1)}, u32[]{:S(2)}, u32[]{:S(2)}) collective-permute-start(f32[2,200,128]{2,1,0:T(8,128)S(1)} %get-tuple-element.23), channel_id=1, source_target_pairs={{1,0},{2,1},{3,2},{4,3},{5,4},{6,5},{7,6},{0,7},{9,8},{10,9},{11,1... | collective-permute-start | bytes 614408 | tf_op jit(solution)/shard_map/ppermute | solution.py:301
  7.3 7.8 %collective-permute-start.3 = (f32[2,200,128]{2,1,0:T(8,128)S(1)}, f32[2,200,128]{2,1,0:T(8,128)S(1)}, u32[]{:S(2)}, u32[]{:S(2)}) collective-permute-start(f32[2,200,128]{2,1,0:T(8,128)S(1)} %get-tuple-element.24), channel_id=1, source_target_pairs={{0,16},{8,24},{16,0},{24,8},{1,17},{9,25},{17,1},{25,9},{2,18},{10... | collective-permute-start | bytes 614408 | tf_op jit(solution)/shard_map/ppermute | solution.py:309
  8.9 6.2 %collective-permute-start.2 = (f32[2,200,128]{2,1,0:T(8,128)S(1)}, f32[2,200,128]{2,1,0:T(8,128)S(1)}, u32[]{:S(2)}, u32[]{:S(2)}) collective-permute-start(f32[2,200,128]{2,1,0:T(8,128)S(1)} %get-tuple-element.24), channel_id=1, source_target_pairs={{0,8},{8,0},{16,24},{24,16},{1,9},{9,1},{17,25},{25,17},{2,10},{10... | collective-permute-start | bytes 614408 | tf_op jit(solution)/shard_map/ppermute | solution.py:309
  18.4 12.4 %all-to-all-start = ((f32[32,8,128]{2,1,0:T(8,128)}), f32[32,8,128]{2,1,0:T(8,128)S(1)}, u32[]{:S(2)}, u32[]{:S(2)}) async-start(f32[32,8,128]{2,1,0:T(8,128)} %get-tuple-element.25), calls=%async_computation | async-start | bytes 262144 | tf_op jit(solution)/shard_map/all_to_all | solution.py:367
  41.9 10.3 %collective-permute-start.4 = (f32[2,200,128]{2,1,0:T(8,128)S(1)}, f32[2,200,128]{2,1,0:T(8,128)S(1)}, u32[]{:S(2)}, u32[]{:S(2)}) collective-permute-start(f32[2,200,128]{2,1,0:T(8,128)S(1)} %get-tuple-element.28), channel_id=1, source_target_pairs={{7,0},{0,1},{1,2},{2,3},{3,4},{4,5},{5,6},{6,7},{15,8},{8,9},{9,10... | collective-permute-start | bytes 614408 | tf_op jit(solution)/shard_map/ppermute | solution.py:301
  43.2 11.2 %collective-permute-start.5 = (f32[2,200,128]{2,1,0:T(8,128)S(1)}, f32[2,200,128]{2,1,0:T(8,128)S(1)}, u32[]{:S(2)}, u32[]{:S(2)}) collective-permute-start(f32[2,200,128]{2,1,0:T(8,128)S(1)} %get-tuple-element.29), channel_id=1, source_target_pairs={{1,0},{2,1},{3,2},{4,3},{5,4},{6,5},{7,6},{0,7},{9,8},{10,9},{11,1... | collective-permute-start | bytes 614408 | tf_op jit(solution)/shard_map/ppermute | solution.py:301
  46.7 7.7 %collective-permute-start.7 = (f32[2,200,128]{2,1,0:T(8,128)S(1)}, f32[2,200,128]{2,1,0:T(8,128)S(1)}, u32[]{:S(2)}, u32[]{:S(2)}) collective-permute-start(f32[2,200,128]{2,1,0:T(8,128)S(1)} %get-tuple-element.30), channel_id=1, source_target_pairs={{0,16},{8,24},{16,0},{24,8},{1,17},{9,25},{17,1},{25,9},{2,18},{10... | collective-permute-start | bytes 614408 | tf_op jit(solution)/shard_map/ppermute | solution.py:309
  47.7 6.7 %collective-permute-start.6 = (f32[2,200,128]{2,1,0:T(8,128)S(1)}, f32[2,200,128]{2,1,0:T(8,128)S(1)}, u32[]{:S(2)}, u32[]{:S(2)}) collective-permute-start(f32[2,200,128]{2,1,0:T(8,128)S(1)} %get-tuple-element.30), channel_id=1, source_target_pairs={{0,8},{8,0},{16,24},{24,16},{1,9},{9,1},{17,25},{25,17},{2,10},{10... | collective-permute-start | bytes 614408 | tf_op jit(solution)/shard_map/ppermute | solution.py:309
  57.7 10.3 %all-to-all-start.1 = ((f32[32,8,128]{2,1,0:T(8,128)}), f32[32,8,128]{2,1,0:T(8,128)S(1)}, u32[]{:S(2)}, u32[]{:S(2)}) async-start(f32[32,8,128]{2,1,0:T(8,128)} %get-tuple-element.31), calls=%async_computation.1 | async-start | bytes 262144 | tf_op jit(solution)/shard_map/all_to_all | solution.py:367
  78.8 8.4 %collective-permute-start.8 = (f32[2,128,128]{2,1,0:T(8,128)S(1)}, f32[2,128,128]{2,1,0:T(8,128)S(1)}, u32[]{:S(2)}, u32[]{:S(2)}) collective-permute-start(f32[2,128,128]{2,1,0:T(8,128)S(1)} %get-tuple-element.34), channel_id=1, source_target_pairs={{7,0},{0,1},{1,2},{2,3},{3,4},{4,5},{5,6},{6,7},{15,8},{8,9},{9,10... | collective-permute-start | bytes 393224 | tf_op jit(solution)/shard_map/ppermute | solution.py:301
  80.1 8.0 %collective-permute-start.9 = (f32[2,128,128]{2,1,0:T(8,128)S(1)}, f32[2,128,128]{2,1,0:T(8,128)S(1)}, u32[]{:S(2)}, u32[]{:S(2)}) collective-permute-start(f32[2,128,128]{2,1,0:T(8,128)S(1)} %get-tuple-element.35), channel_id=1, source_target_pairs={{1,0},{2,1},{3,2},{4,3},{5,4},{6,5},{7,6},{0,7},{9,8},{10,9},{11,1... | collective-permute-start | bytes 393224 | tf_op jit(solution)/shard_map/ppermute | solution.py:301
  83.6 5.0 %collective-permute-start.11 = (f32[2,128,128]{2,1,0:T(8,128)S(1)}, f32[2,128,128]{2,1,0:T(8,128)S(1)}, u32[]{:S(2)}, u32[]{:S(2)}) collective-permute-start(f32[2,128,128]{2,1,0:T(8,128)S(1)} %get-tuple-element.36), channel_id=1, source_target_pairs={{0,16},{8,24},{16,0},{24,8},{1,17},{9,25},{17,1},{25,9},{2,18},{10... | collective-permute-start | bytes 393224 | tf_op jit(solution)/shard_map/ppermute | solution.py:309
  84.7 3.9 %collective-permute-start.10 = (f32[2,128,128]{2,1,0:T(8,128)S(1)}, f32[2,128,128]{2,1,0:T(8,128)S(1)}, u32[]{:S(2)}, u32[]{:S(2)}) collective-permute-start(f32[2,128,128]{2,1,0:T(8,128)S(1)} %get-tuple-element.36), channel_id=1, source_target_pairs={{0,8},{8,0},{16,24},{24,16},{1,9},{9,1},{17,25},{25,17},{2,10},{10... | collective-permute-start | bytes 393224 | tf_op jit(solution)/shard_map/ppermute | solution.py:309

commit v3 on v2

--- a/solution.py
+++ b/solution.py
@@ -125,40 +125,55 @@
         target[slot, pl.ds(SIDE + HALF, PACKED - HALF), :] = packed[1]
 
 
-def pack_kernel(own, half, to_right, to_left, to_partner):
+def fill_all(targets, slot, faces, packed):
+    left, right, partner = faces
+    even = lax.axis_index("col") % 2 == 0
+    fill(targets[0], slot, jnp.where(even, right, left), packed)
+    fill(targets[1], slot, jnp.where(even, left, right), packed)
+    fill(targets[2], slot, partner, packed)
+
+
+def pack_kernel(own, half, *targets):
     for slot in range(own.shape[0]):
         centre = symmetric(own[slot, 0])
         packed = pack(centre)
         half[slot, 0] = centre
         for k in range(1, own.shape[1]):
             half[slot, k] = 0.5 * own[slot, k]
-        fill(to_right, slot, own[slot, 2], packed)
-        fill(to_left, slot, own[slot, 1], packed)
-        fill(to_partner, slot, own[slot, 3], packed)
-
-
-def my_links(lists, cols, slots):
+        fill_all(targets, slot, [own[slot, k] for k in range(1, own.shape[1])], packed)
+
+
+def links_kernel(slots, cols, lists, links):
     my_row = lax.axis_index("row")
     device = my_row * cols + lax.axis_index("col")
-    links = []
+    count = links.shape[0] // slots
     for slot in range(slots):
         column = device * slots + slot
-        present = [jnp.where(lists[column, k] >= 0, 1.0, 0.0).astype(f32) for k in range(4)]
         partner_row = lists[column, 3] // (slots * cols)
-        links.append((present, jnp.bitwise_xor(my_row, partner_row)))
-    return links
+        values = [jnp.where(lists[column, k] >= 0, 1.0, 0.0) for k in range(count - 1)]
+        values.append(jnp.bitwise_xor(my_row, partner_row).astype(f32))
+        for k, value in enumerate(values):
+            links[pl.ds(slot * count + k, 1), :] = jnp.full((1, SIDE), value, f32)
+
+
+def my_links(links, slots):
+    count = links.shape[0] // slots
+    rows = [links[pl.ds(place, 1), :] for place in range(slots * count)]
+    return [(rows[slot * count : slot * count + count - 1], rows[slot * count + count - 1]) for slot in range(slots)]
 
 
 def neighbour_parts(slot, bit, received, with_diagonals):
-    from_left, from_right = received[:2]
+    from_even, from_odd = received[:2]
     from_rows = received[2:]
+    even = lax.axis_index("col") % 2 == 0
 
     def read(first, count):
         span = pl.ds(first, count)
         partner = from_rows[0][slot, span, :]
         for place in range(1, len(from_rows)):
-            partner = jnp.where(bit == (1 << place), from_rows[place][slot, span, :], partner)
-        return from_left[slot, span, :], from_right[slot, span, :], partner
+            partner = jnp.where(bit == float(1 << place), from_rows[place][slot, span, :], partner)
+        near, far = from_even[slot, span, :], from_odd[slot, span, :]
+        return jnp.where(even, far, near), jnp.where(even, near, far), partner
 
     faces = read(0, SIDE)
     if not with_diagonals:
@@ -168,14 +183,14 @@
     return faces, [unpack(b, d[0:1, :]) for b, d in zip(bodies, diagonals)]
 
 
-def assemble_kernel(cols, members, has_base, *refs):
-    lists, half = refs[:2]
+def assemble_kernel(members, has_base, *refs):
+    links, half = refs[:2]
     base = refs[2] if has_base else None
     received = refs[2 + has_base : -5]
     norms, blocks, s_high, s_low, mixed = refs[-5:]
     slots = half.shape[0]
     top = None
-    links = my_links(lists, cols, slots)
+    links = my_links(links, slots)
     for slot in range(slots):
         present, bit = links[slot]
         faces, diagonals = neighbour_parts(slot, bit, received, True)
@@ -219,7 +234,9 @@
                     out[slot, count + at] = tile[row : row + SIDE, col : col + SIDE]
 
 
-def sign_kernel(members, last, norms, source, own, to_right, to_left, to_partner, x, xh, xl, yh, yl, mixed):
+def sign_kernel(members, last, norms, source, own, *refs):
+    targets = refs[:3]
+    x, xh, xl, yh, yl, mixed = refs[3:]
     slots = source.shape[0]
     order = members * SIDE
     largest = jnp.max(jnp.max(norms[...], axis=0), axis=(0, 1), keepdims=True)
@@ -275,19 +292,17 @@
         parts = [central[k * SIDE : (k + 1) * SIDE] for k in range(members)]
         parts[0] = symmetric(parts[0]) + eye
         packed = None if last else pack(parts[0])
-        fill(to_right, slot, parts[2], packed)
-        fill(to_left, slot, parts[1], packed)
-        fill(to_partner, slot, parts[3], packed)
+        fill_all(targets, slot, parts[1:], packed)
         own[slot, 0] = parts[0]
         for k in range(1, members):
             own[slot, k] = 0.5 * parts[k]
 
 
-def density_kernel(cols, members, *refs):
-    lists, half = refs[:2]
+def density_kernel(members, *refs):
+    links, half = refs[:2]
     received = refs[2:-1]
     out = refs[-1]
-    links = my_links(lists, cols, half.shape[0])
+    links = my_links(links, half.shape[0])
     for slot in range(half.shape[0]):
         present, bit = links[slot]
         faces, _ = neighbour_parts(slot, bit, received, False)
@@ -296,14 +311,12 @@
             out[slot, k] = present[k] * (half[slot, k] + 0.5 * turned(faces[k - 1]))
 
 
-def from_behind(block, axis, distance):
-    devices = range(lax.axis_size(axis))
-    return lax.ppermute(block, axis, [((i - distance) % len(devices), i) for i in devices])
-
-
-def exchange(to_right, to_left, to_partner):
-    received = [from_behind(to_right, "col", 1), from_behind(to_left, "col", -1)]
+def exchange(over_even, over_odd, to_partner):
+    cols = range(lax.axis_size("col"))
     rows = range(lax.axis_size("row"))
+    odd = [(i, (i + 1 if i % 2 else i - 1) % len(cols)) for i in cols]
+    received = [lax.ppermute(over_even, "col", [(i, i ^ 1) for i in cols])]
+    received.append(lax.ppermute(over_odd, "col", odd))
     place = 1
     while place < len(rows):
         received.append(lax.ppermute(to_partner, "row", [(i, i ^ place) for i in rows]))
@@ -351,18 +364,24 @@
     multiply = slots * 3 * 3 * order * order * order // 2
 
     half, *sent = call(pack_kernel, "pack", [hamiltonian], [own] + [full] * 3)
+    (links,) = call(
+        functools.partial(links_kernel, slots, cols),
+        "links",
+        [block_lists],
+        [shape(slots * (members + 1), SIDE)],
+        smem_first=True,
+    )
     base = []
     for step in range(STEPS):
         last = step == STEPS - 1
         received = exchange(*sent)
         norms, blocks = call(
-            functools.partial(assemble_kernel, cols, members, len(base)),
+            functools.partial(assemble_kernel, members, len(base)),
             "assemble",
-            [block_lists, half, *base, *received],
-            [shape(devices, 8, SIDE), shape(slots, arrow, SIDE, SIDE)],
+            [links, half, *base, *received],
+            [shape(devices, 1, SIDE), shape(slots, arrow, SIDE, SIDE)],
             [part_scratch] * 2 + [mixed_scratch],
             flops=multiply,
-            smem_first=True,
         )
         norms = lax.all_to_all(norms, ("row", "col"), 0, 0, tiled=True)
         (source,) = call(
@@ -384,11 +403,10 @@
         base = [source]
     received = exchange(*sent)
     (density,) = call(
-        functools.partial(density_kernel, cols, members),
+        functools.partial(density_kernel, members),
         "density",
-        [block_lists, half, *received],
+        [links, half, *received],
         [own],
-        smem_first=True,
     )
     return density
 

time: 90.9 us -> 83.5 us (0.919)
  starting transfers between devices: 26.6 us -> 21.7 us
  Pallas kernels: 35.7 us -> 33.5 us
    ppermute x6, starting transfers between devices: 15.7 us -> 10.7 us  [the longest x3 6.31 us: exchange(): received.append(lax.ppermute(over_odd, 'col', odd))]
    pallas_call x8 -> x9, Pallas kernels: 35.7 us -> 33.5 us  [call(): pl.pallas_call(kernel, out_shape=list(outputs), in_specs=specs, out_specs...]
    all_to_all x2, waiting for transfers between devices: 10.4 us -> 8.96 us  [per_device(): norms = lax.all_to_all(norms, ('row', 'col'), 0, 0, tiled=True)]
    ppermute x6, waiting for transfers between devices: 15.6 us -> 16.8 us  [the longest x3 14.7 us: exchange(): received = [lax.ppermute(over_even, 'col', [(i, i ^ 1) for i in cols])]]
    all_to_all x2, starting transfers between devices: 7.19 us -> 8.3 us  [per_device(): norms = lax.all_to_all(norms, ('row', 'col'), 0, 0, tiled=True)]
    ppermute x6, starting transfers between devices: 3.71 us -> 2.72 us  [exchange(): lax.ppermute(to_partner, 'row', [(i, i ^ place) for i in rows])]
  transfers between devices with their start and end apart: 14 -> 14, of which waited for: 9 -> 7; matrix products, arithmetic and copies ran while one was open for 1% -> 1% of each run, Pallas kernels for 6% -> 7%
where the time goes in v3:
time: 83.5 us; the launch traced here: 83.3 us
  Pallas kernels  33.5 us (40%)
  waiting for transfers between devices  26.1 us (31%)
  starting transfers between devices  21.7 us (26%)
  local copies, waits for them, and re-layouts  1.81 us (2%)
    pallas_call x9, Pallas kernels, call(): pl.pallas_call(kernel, out_shape=list(outputs), in_specs=specs, out_specs...  33.5 us
    ppermute x3, waiting for transfers between devices, exchange(): received = [lax.ppermute(over_even, 'col', [(i, i ^ 1) for i in cols])]  14.7 us
    all_to_all x2, waiting for transfers between devices, per_device(): norms = lax.all_to_all(norms, ('row', 'col'), 0, 0, tiled=True)  8.96 us
    all_to_all x2, starting transfers between devices, per_device(): norms = lax.all_to_all(norms, ('row', 'col'), 0, 0, tiled=True)  8.3 us
    ppermute x3, starting transfers between devices, exchange(): received.append(lax.ppermute(over_odd, 'col', odd))  6.31 us
    ppermute x3, starting transfers between devices, exchange(): received = [lax.ppermute(over_even, 'col', [(i, i ^ 1) for i in cols])]  4.4 us
    ppermute x6, starting transfers between devices, exchange(): lax.ppermute(to_partner, 'row', [(i, i ^ place) for i in rows])  2.72 us
    ppermute x3, waiting for transfers between devices, exchange(): received.append(lax.ppermute(over_odd, 'col', odd))  2.11 us
  transfers between devices with their start and end apart: 14, of which 7 were waited for; matrix products, arithmetic and copies ran while one was open for 1% of the time, Pallas kernels for 7%

profile of v3, /device:TPU:0, one launch (start us, length us, event | category | flops | bytes accessed | tf_op | source)
XLA Modules:
  0.0 83.3 jit_solution(4450810876812090941)
XLA Ops:
  0.0 1.0 %copy-done = f32[2,4,128,128]{3,2,1,0:T(8,128)S(1)} copy-done((f32[2,4,128,128]{3,2,1,0:T(8,128)S(1)}, f32[2,4,128,128]{3,2,1,0:T(8,128)}, u32[]{:S(2)}) %copy-start) | copy-done | bytes 524312
  1.0 0.2 pack.1
  1.2 3.0 %collective-permute-start = (f32[2,200,128]{2,1,0:T(8,128)S(1)}, f32[2,200,128]{2,1,0:T(8,128)S(1)}, u32[]{:S(2)}, u32[]{:S(2)}) collective-permute-start(f32[2,200,128]{2,1,0:T(8,128)S(1)} %get-tuple-element.22), channel_id=1, source_target_pairs={{0,1},{1,0},{2,3},{3,2},{4,5},{5,4},{6,7},{7,6},{8,9},{9,8},{10,11... | collective-permute-start | bytes 614408 | tf_op jit(solution)/shard_map/ppermute | solution.py:318
  4.3 3.5 %collective-permute-start.1 = (f32[2,200,128]{2,1,0:T(8,128)S(1)}, f32[2,200,128]{2,1,0:T(8,128)S(1)}, u32[]{:S(2)}, u32[]{:S(2)}) collective-permute-start(f32[2,200,128]{2,1,0:T(8,128)S(1)} %get-tuple-element.23), channel_id=1, source_target_pairs={{0,7},{1,2},{2,1},{3,4},{4,3},{5,6},{6,5},{7,0},{8,15},{9,10},{10,... | collective-permute-start | bytes 614408 | tf_op jit(solution)/shard_map/ppermute | solution.py:319
  7.8 1.5 %collective-permute-start.3 = (f32[2,200,128]{2,1,0:T(8,128)S(1)}, f32[2,200,128]{2,1,0:T(8,128)S(1)}, u32[]{:S(2)}, u32[]{:S(2)}) collective-permute-start(f32[2,200,128]{2,1,0:T(8,128)S(1)} %get-tuple-element.24), channel_id=1, source_target_pairs={{0,16},{8,24},{16,0},{24,8},{1,17},{9,25},{17,1},{25,9},{2,18},{10... | collective-permute-start | bytes 614408 | tf_op jit(solution)/shard_map/ppermute | solution.py:322
  9.3 0.0 collective-permute-start.2
  9.3 0.8 copy.3.lists
  10.1 1.1 %links.1.refs_0_ = f32[10,128]{1,0:T(8,128)S(1)} custom-call(s32[64,4]{1,0:T(8,128)S(1)} %copy.3.lists), custom_call_target="tpu_custom_call" | custom-call | bytes 6144 | tf_op jit(solution)/shard_map/links/pallas_call | solution.py:340
  11.2 2.5 %collective-permute-done.refs_2_ = f32[2,200,128]{2,1,0:T(8,128)S(1)} collective-permute-done((f32[2,200,128]{2,1,0:T(8,128)S(1)}, f32[2,200,128]{2,1,0:T(8,128)S(1)}, u32[]{:S(2)}, u32[]{:S(2)}) %collective-permute-start) | collective-permute-done | bytes 204832 | tf_op jit(solution)/shard_map/ppermute | solution.py:318
  13.7 0.3 collective-permute-done.3.refs_5_
  14.1 2.1 %assemble.2 = (f32[32,1,128]{2,1,0:T(1,128)}, f32[2,7,128,128]{3,2,1,0:T(8,128)S(1)}) custom-call(f32[10,128]{1,0:T(8,128)S(1)} %links.1.refs_0_, f32[2,4,128,128]{3,2,1,0:T(8,128)S(1)} %get-tuple-element.21.refs_1_, f32[2,200,128]{2,1,0:T(8,128)S(1)} %collective-permute-done.refs_2_, f32[2,200,128]{2,1,0:T(8,128)S(1)} %collective-permute-done.1.refs_3_, ...), custom_call_target="tpu_custom_call" | custom-call | flops 1207959552 | bytes 2282496 | tf_op jit(solution)/shard_map/assemble/pallas_call | solution.py:340
  16.2 5.8 %all-to-all-start = ((f32[32,1,128]{2,1,0:T(1,128)}), f32[32,1,128]{2,1,0:T(1,128)S(1)}, u32[]{:S(2)}, u32[]{:S(2)}) async-start(f32[32,1,128]{2,1,0:T(1,128)} %get-tuple-element.25), calls=%async_computation | async-start | bytes 32768 | tf_op jit(solution)/shard_map/all_to_all | solution.py:386
  21.9 2.5 %cube.2.source.refs_2_ = f32[2,17,128,128]{3,2,1,0:T(8,128)S(1)} custom-call(f32[2,7,128,128]{3,2,1,0:T(8,128)S(1)} %get-tuple-element.26.blocks), custom_call_target="tpu_custom_call" | custom-call | flops 2415919104 | bytes 3145728 | tf_op jit(solution)/shard_map/cube/pallas_call | solution.py:340
  24.5 4.5 %all-to-all-done.norms = f32[32,1,128]{2,1,0:T(1,128)S(1)} async-done(((f32[32,1,128]{2,1,0:T(1,128)}), f32[32,1,128]{2,1,0:T(1,128)S(1)}, u32[]{:S(2)}, u32[]{:S(2)}) %all-to-all-start) | async-done | bytes 16416 | tf_op jit(solution)/shard_map/all_to_all | solution.py:386
  29.0 11.1 %sign.2 = (f32[2,4,128,128]{3,2,1,0:T(8,128)S(1)}, f32[2,200,128]{2,1,0:T(8,128)S(1)}, f32[2,200,128]{2,1,0:T(8,128)S(1)}, f32[2,200,128]{2,1,0:T(8,128)S(1)}) custom-call(f32[32,1,128]{2,1,0:T(1,128)S(1)} %all-to-all-done.norms, f32[2,17,128,128]{3,2,1,0:T(8,128)S(1)} %cube.2.source.refs_2_), custom_call_target="tpu_custom_call" | custom-call | flops 9663676416 | bytes 3383296 | tf_op jit(solution)/shard_map/sign/pallas_call | solution.py:340
  40.1 0.7 collective-permute-start.4
  40.8 1.4 %collective-permute-start.5 = (f32[2,200,128]{2,1,0:T(8,128)S(1)}, f32[2,200,128]{2,1,0:T(8,128)S(1)}, u32[]{:S(2)}, u32[]{:S(2)}) collective-permute-start(f32[2,200,128]{2,1,0:T(8,128)S(1)} %get-tuple-element.29), channel_id=1, source_target_pairs={{0,7},{1,2},{2,1},{3,4},{4,3},{5,6},{6,5},{7,0},{8,15},{9,10},{10,... | collective-permute-start | bytes 614408 | tf_op jit(solution)/shard_map/ppermute | solution.py:319
  42.1 0.6 collective-permute-start.7
  42.8 0.0 collective-permute-start.6
  42.8 8.6 %collective-permute-done.4.refs_3_ = f32[2,200,128]{2,1,0:T(8,128)S(1)} collective-permute-done((f32[2,200,128]{2,1,0:T(8,128)S(1)}, f32[2,200,128]{2,1,0:T(8,128)S(1)}, u32[]{:S(2)}, u32[]{:S(2)}) %collective-permute-start.4) | collective-permute-done | bytes 204832 | tf_op jit(solution)/shard_map/ppermute | solution.py:318
  51.4 0.0 collective-permute-done.7.refs_6_
  51.4 2.1 %assemble.3 = (f32[32,1,128]{2,1,0:T(1,128)}, f32[2,7,128,128]{3,2,1,0:T(8,128)S(1)}) custom-call(f32[10,128]{1,0:T(8,128)S(1)} %links.1.refs_0_, f32[2,4,128,128]{3,2,1,0:T(8,128)S(1)} %get-tuple-element.27.refs_1_, f32[2,17,128,128]{3,2,1,0:T(8,128)S(1)} %cube.2.source.refs_2_, f32[2,200,128]{2,1,0:T(8,128)S(1)} %collective-permute-done.4.refs_3_, ...), custom_call_target="tpu_custom_call" | custom-call | flops 1207959552 | bytes 4510720 | tf_op jit(solution)/shard_map/assemble/pallas_call | solution.py:340
  53.5 2.5 %all-to-all-start.1 = ((f32[32,1,128]{2,1,0:T(1,128)}), f32[32,1,128]{2,1,0:T(1,128)S(1)}, u32[]{:S(2)}, u32[]{:S(2)}) async-start(f32[32,1,128]{2,1,0:T(1,128)} %get-tuple-element.31), calls=%async_computation.1 | async-start | bytes 32768 | tf_op jit(solution)/shard_map/all_to_all | solution.py:386
  56.1 2.6 %cube.3.source = f32[2,17,128,128]{3,2,1,0:T(8,128)S(1)} custom-call(f32[2,7,128,128]{3,2,1,0:T(8,128)S(1)} %get-tuple-element.32.blocks), custom_call_target="tpu_custom_call" | custom-call | flops 2415919104 | bytes 3145728 | tf_op jit(solution)/shard_map/cube/pallas_call | solution.py:340
  58.6 4.5 %all-to-all-done.1.norms = f32[32,1,128]{2,1,0:T(1,128)S(1)} async-done(((f32[32,1,128]{2,1,0:T(1,128)}), f32[32,1,128]{2,1,0:T(1,128)S(1)}, u32[]{:S(2)}, u32[]{:S(2)}) %all-to-all-start.1) | async-done | bytes 16416 | tf_op jit(solution)/shard_map/all_to_all | solution.py:386
  63.1 10.8 %sign.3 = (f32[2,4,128,128]{3,2,1,0:T(8,128)S(1)}, f32[2,128,128]{2,1,0:T(8,128)S(1)}, f32[2,128,128]{2,1,0:T(8,128)S(1)}, f32[2,128,128]{2,1,0:T(8,128)S(1)}) custom-call(f32[32,1,128]{2,1,0:T(1,128)S(1)} %all-to-all-done.1.norms, f32[2,17,128,128]{3,2,1,0:T(8,128)S(1)} %cube.3.source), custom_call_target="tpu_custom_call" | custom-call | flops 9663676416 | bytes 3162112 | tf_op jit(solution)/shard_map/sign/pallas_call | solution.py:340
  73.9 0.7 collective-permute-start.8
  74.6 1.4 %collective-permute-start.9 = (f32[2,128,128]{2,1,0:T(8,128)S(1)}, f32[2,128,128]{2,1,0:T(8,128)S(1)}, u32[]{:S(2)}, u32[]{:S(2)}) collective-permute-start(f32[2,128,128]{2,1,0:T(8,128)S(1)} %get-tuple-element.35), channel_id=1, source_target_pairs={{0,7},{1,2},{2,1},{3,4},{4,3},{5,6},{6,5},{7,0},{8,15},{9,10},{10,... | collective-permute-start | bytes 393224 | tf_op jit(solution)/shard_map/ppermute | solution.py:319
  76.0 0.6 collective-permute-start.11
  76.6 3.6 %collective-permute-done.8.refs_2_ = f32[2,128,128]{2,1,0:T(8,128)S(1)} collective-permute-done((f32[2,128,128]{2,1,0:T(8,128)S(1)}, f32[2,128,128]{2,1,0:T(8,128)S(1)}, u32[]{:S(2)}, u32[]{:S(2)}) %collective-permute-start.8) | collective-permute-done | bytes 131104 | tf_op jit(solution)/shard_map/ppermute | solution.py:318
  80.2 2.1 %collective-permute-done.9.refs_3_ = f32[2,128,128]{2,1,0:T(8,128)S(1)} collective-permute-done((f32[2,128,128]{2,1,0:T(8,128)S(1)}, f32[2,128,128]{2,1,0:T(8,128)S(1)}, u32[]{:S(2)}, u32[]{:S(2)}) %collective-permute-start.9) | collective-permute-done | bytes 131104 | tf_op jit(solution)/shard_map/ppermute | solution.py:319
  82.3 1.0 %density.1 = f32[2,4,128,128]{3,2,1,0:T(8,128)} custom-call(f32[10,128]{1,0:T(8,128)S(1)} %links.1.refs_0_, f32[2,4,128,128]{3,2,1,0:T(8,128)S(1)} %get-tuple-element.33.refs_1_, f32[2,128,128]{2,1,0:T(8,128)S(1)} %collective-permute-done.8.refs_2_, f32[2,128,128]{2,1,0:T(8,128)S(1)} %collective-permute-done.9.refs_3_, ...), custom_call_target="tpu_custom_call" | custom-call | bytes 1577984 | tf_op jit(solution)/shard_map/density/pallas_call | solution.py:340
  (8 shorter events, 0.0 us)
Async XLA Ops:
  0.0 1.0 %copy-start = (f32[2,4,128,128]{3,2,1,0:T(8,128)S(1)}, f32[2,4,128,128]{3,2,1,0:T(8,128)}, u32[]{:S(2)}) copy-start(f32[2,4,128,128]{3,2,1,0:T(8,128)} %own.1) | copy-start | bytes 1572868
  1.2 12.5 %collective-permute-start = (f32[2,200,128]{2,1,0:T(8,128)S(1)}, f32[2,200,128]{2,1,0:T(8,128)S(1)}, u32[]{:S(2)}, u32[]{:S(2)}) collective-permute-start(f32[2,200,128]{2,1,0:T(8,128)S(1)} %get-tuple-element.22), channel_id=1, source_target_pairs={{0,1},{1,0},{2,3},{3,2},{4,5},{5,4},{6,7},{7,6},{8,9},{9,8},{10,11... | collective-permute-start | bytes 614408 | tf_op jit(solution)/shard_map/ppermute | solution.py:318
  4.3 9.5 %collective-permute-start.1 = (f32[2,200,128]{2,1,0:T(8,128)S(1)}, f32[2,200,128]{2,1,0:T(8,128)S(1)}, u32[]{:S(2)}, u32[]{:S(2)}) collective-permute-start(f32[2,200,128]{2,1,0:T(8,128)S(1)} %get-tuple-element.23), channel_id=1, source_target_pairs={{0,7},{1,2},{2,1},{3,4},{4,3},{5,6},{6,5},{7,0},{8,15},{9,10},{10,... | collective-permute-start | bytes 614408 | tf_op jit(solution)/shard_map/ppermute | solution.py:319
  7.8 6.3 %collective-permute-start.3 = (f32[2,200,128]{2,1,0:T(8,128)S(1)}, f32[2,200,128]{2,1,0:T(8,128)S(1)}, u32[]{:S(2)}, u32[]{:S(2)}) collective-permute-start(f32[2,200,128]{2,1,0:T(8,128)S(1)} %get-tuple-element.24), channel_id=1, source_target_pairs={{0,16},{8,24},{16,0},{24,8},{1,17},{9,25},{17,1},{25,9},{2,18},{10... | collective-permute-start | bytes 614408 | tf_op jit(solution)/shard_map/ppermute | solution.py:322
  9.3 4.8 %collective-permute-start.2 = (f32[2,200,128]{2,1,0:T(8,128)S(1)}, f32[2,200,128]{2,1,0:T(8,128)S(1)}, u32[]{:S(2)}, u32[]{:S(2)}) collective-permute-start(f32[2,200,128]{2,1,0:T(8,128)S(1)} %get-tuple-element.24), channel_id=1, source_target_pairs={{0,8},{8,0},{16,24},{24,16},{1,9},{9,1},{17,25},{25,17},{2,10},{10... | collective-permute-start | bytes 614408 | tf_op jit(solution)/shard_map/ppermute | solution.py:322
  16.2 12.8 %all-to-all-start = ((f32[32,1,128]{2,1,0:T(1,128)}), f32[32,1,128]{2,1,0:T(1,128)S(1)}, u32[]{:S(2)}, u32[]{:S(2)}) async-start(f32[32,1,128]{2,1,0:T(1,128)} %get-tuple-element.25), calls=%async_computation | async-start | bytes 32768 | tf_op jit(solution)/shard_map/all_to_all | solution.py:386
  40.1 11.3 %collective-permute-start.4 = (f32[2,200,128]{2,1,0:T(8,128)S(1)}, f32[2,200,128]{2,1,0:T(8,128)S(1)}, u32[]{:S(2)}, u32[]{:S(2)}) collective-permute-start(f32[2,200,128]{2,1,0:T(8,128)S(1)} %get-tuple-element.28), channel_id=1, source_target_pairs={{0,1},{1,0},{2,3},{3,2},{4,5},{5,4},{6,7},{7,6},{8,9},{9,8},{10,11... | collective-permute-start | bytes 614408 | tf_op jit(solution)/shard_map/ppermute | solution.py:318
  40.8 10.6 %collective-permute-start.5 = (f32[2,200,128]{2,1,0:T(8,128)S(1)}, f32[2,200,128]{2,1,0:T(8,128)S(1)}, u32[]{:S(2)}, u32[]{:S(2)}) collective-permute-start(f32[2,200,128]{2,1,0:T(8,128)S(1)} %get-tuple-element.29), channel_id=1, source_target_pairs={{0,7},{1,2},{2,1},{3,4},{4,3},{5,6},{6,5},{7,0},{8,15},{9,10},{10,... | collective-permute-start | bytes 614408 | tf_op jit(solution)/shard_map/ppermute | solution.py:319
  42.1 9.2 %collective-permute-start.7 = (f32[2,200,128]{2,1,0:T(8,128)S(1)}, f32[2,200,128]{2,1,0:T(8,128)S(1)}, u32[]{:S(2)}, u32[]{:S(2)}) collective-permute-start(f32[2,200,128]{2,1,0:T(8,128)S(1)} %get-tuple-element.30), channel_id=1, source_target_pairs={{0,16},{8,24},{16,0},{24,8},{1,17},{9,25},{17,1},{25,9},{2,18},{10... | collective-permute-start | bytes 614408 | tf_op jit(solution)/shard_map/ppermute | solution.py:322
  42.8 8.6 %collective-permute-start.6 = (f32[2,200,128]{2,1,0:T(8,128)S(1)}, f32[2,200,128]{2,1,0:T(8,128)S(1)}, u32[]{:S(2)}, u32[]{:S(2)}) collective-permute-start(f32[2,200,128]{2,1,0:T(8,128)S(1)} %get-tuple-element.30), channel_id=1, source_target_pairs={{0,8},{8,0},{16,24},{24,16},{1,9},{9,1},{17,25},{25,17},{2,10},{10... | collective-permute-start | bytes 614408 | tf_op jit(solution)/shard_map/ppermute | solution.py:322
  53.5 9.6 %all-to-all-start.1 = ((f32[32,1,128]{2,1,0:T(1,128)}), f32[32,1,128]{2,1,0:T(1,128)S(1)}, u32[]{:S(2)}, u32[]{:S(2)}) async-start(f32[32,1,128]{2,1,0:T(1,128)} %get-tuple-element.31), calls=%async_computation.1 | async-start | bytes 32768 | tf_op jit(solution)/shard_map/all_to_all | solution.py:386
  73.9 6.2 %collective-permute-start.8 = (f32[2,128,128]{2,1,0:T(8,128)S(1)}, f32[2,128,128]{2,1,0:T(8,128)S(1)}, u32[]{:S(2)}, u32[]{:S(2)}) collective-permute-start(f32[2,128,128]{2,1,0:T(8,128)S(1)} %get-tuple-element.34), channel_id=1, source_target_pairs={{0,1},{1,0},{2,3},{3,2},{4,5},{5,4},{6,7},{7,6},{8,9},{9,8},{10,11... | collective-permute-start | bytes 393224 | tf_op jit(solution)/shard_map/ppermute | solution.py:318
  74.6 7.7 %collective-permute-start.9 = (f32[2,128,128]{2,1,0:T(8,128)S(1)}, f32[2,128,128]{2,1,0:T(8,128)S(1)}, u32[]{:S(2)}, u32[]{:S(2)}) collective-permute-start(f32[2,128,128]{2,1,0:T(8,128)S(1)} %get-tuple-element.35), channel_id=1, source_target_pairs={{0,7},{1,2},{2,1},{3,4},{4,3},{5,6},{6,5},{7,0},{8,15},{9,10},{10,... | collective-permute-start | bytes 393224 | tf_op jit(solution)/shard_map/ppermute | solution.py:319
  76.0 6.3 %collective-permute-start.11 = (f32[2,128,128]{2,1,0:T(8,128)S(1)}, f32[2,128,128]{2,1,0:T(8,128)S(1)}, u32[]{:S(2)}, u32[]{:S(2)}) collective-permute-start(f32[2,128,128]{2,1,0:T(8,128)S(1)} %get-tuple-element.36), channel_id=1, source_target_pairs={{0,16},{8,24},{16,0},{24,8},{1,17},{9,25},{17,1},{25,9},{2,18},{10... | collective-permute-start | bytes 393224 | tf_op jit(solution)/shard_map/ppermute | solution.py:322
  76.6 5.7 %collective-permute-start.10 = (f32[2,128,128]{2,1,0:T(8,128)S(1)}, f32[2,128,128]{2,1,0:T(8,128)S(1)}, u32[]{:S(2)}, u32[]{:S(2)}) collective-permute-start(f32[2,128,128]{2,1,0:T(8,128)S(1)} %get-tuple-element.36), channel_id=1, source_target_pairs={{0,8},{8,0},{16,24},{24,16},{1,9},{9,1},{17,25},{25,17},{2,10},{10... | collective-permute-start | bytes 393224 | tf_op jit(solution)/shard_map/ppermute | solution.py:322

commit v4 on v3

--- a/solution.py
+++ b/solution.py
@@ -234,12 +234,20 @@
                     out[slot, count + at] = tile[row : row + SIDE, col : col + SIDE]
 
 
+def schedule(square, advance, slots, repeats):
+    for repeat in range(repeats):
+        for work in (square, advance):
+            for slot in range(slots):
+                for _ in work(slot, repeat):
+                    pass
+
+
 def sign_kernel(members, last, norms, source, own, *refs):
     targets = refs[:3]
     x, xh, xl, yh, yl, mixed = refs[3:]
     slots = source.shape[0]
     order = members * SIDE
-    largest = jnp.max(jnp.max(norms[...], axis=0), axis=(0, 1), keepdims=True)
+    largest = jnp.max(norms[...], axis=0)
     scaling = 1.5 / jnp.sqrt(jnp.sqrt(largest + epsilon))
     linear = 1.5 * scaling
     cubic = -0.5 * (scaling * scaling * scaling)
@@ -258,41 +266,39 @@
                     x[(slot, *spans[::-1])] = turned(value)
                 store_split((xh.at[0], xl.at[0]), slot, *spans, value, row != col)
                 at += 1
-    now = 0
-    for repeat in range(1, ITERS - 1):
-        for slot in range(slots):
-            iterate = (xh.at[now, slot], xl.at[now, slot])
-            for _, rows, columns, off, tile in square_tiles(*iterate, mixed.at[slot]):
-                store_split((yh, yl), slot, rows, columns, tile, off)
-        for slot in range(slots):
-            iterate = (xh.at[now, slot], xl.at[now, slot])
-            square = (yh.at[slot], yl.at[slot])
-            target = (xh.at[1 - now], xl.at[1 - now])
-            for _, rows, columns, off in upper_tiles(order):
-                tile = product(iterate, square, rows, columns)
-                value = 1.5 * x[slot, rows, columns] - 0.5 * tile
-                x[slot, rows, columns] = value
-                store_split(target, slot, rows, columns, value, off)
-                if off and repeat == ITERS - 2:
-                    x[slot, columns, rows] = turned(value)
-        now = 1 - now
+    def square(slot, repeat):
+        iterate = (xh.at[repeat % 2, slot], xl.at[repeat % 2, slot])
+        for _, rows, columns, off, tile in square_tiles(*iterate, mixed.at[slot]):
+            store_split((yh, yl), slot, rows, columns, tile, off)
+            yield
+
+    def advance(slot, repeat):
+        iterate = (xh.at[repeat % 2, slot], xl.at[repeat % 2, slot])
+        target = (xh.at[1 - repeat % 2], xl.at[1 - repeat % 2])
+        for _, rows, columns, off in upper_tiles(order):
+            tile = product(iterate, (yh.at[slot], yl.at[slot]), rows, columns)
+            value = 1.5 * x[slot, rows, columns] - 0.5 * tile
+            x[slot, rows, columns] = value
+            store_split(target, slot, rows, columns, value, off)
+            yield
+
+    schedule(square, advance, slots, ITERS - 2)
+    now = (ITERS - 2) % 2
     first = pl.ds(0, SIDE)
 
     def thin(slot, high, low):
-        left_high, left_low = xh[now, slot], xl[now, slot]
-        both = dot(left_high, jnp.concatenate([high, low], 1))
-        return both[:, :SIDE] + both[:, SIDE:] + dot(left_low, high)
-
-    middle = [thin(slot, xh[now, slot, :, first], xl[now, slot, :, first]) for slot in range(slots)]
+        both = dot(jnp.concatenate([high, low], 0), xh[now, slot])
+        return both[:SIDE] + both[SIDE:] + dot(high, xl[now, slot])
+
+    middle = [thin(slot, xh[now, slot, first, :], xl[now, slot, first, :]) for slot in range(slots)]
     outer = [thin(slot, *split(middle[slot])) for slot in range(slots)]
     square = (SIDE, SIDE)
     eye = jnp.where(lanes(square) == rows_of(square), 0.5, 0.0)
     for slot in range(slots):
-        central = 0.25 * outer[slot] - 0.75 * x[slot, :, first]
-        parts = [central[k * SIDE : (k + 1) * SIDE] for k in range(members)]
+        central = 0.25 * outer[slot] - 0.75 * x[slot, first, :]
+        parts = [turned(central[:, k * SIDE : (k + 1) * SIDE]) for k in range(members)]
         parts[0] = symmetric(parts[0]) + eye
-        packed = None if last else pack(parts[0])
-        fill_all(targets, slot, parts[1:], packed)
+        fill_all(targets, slot, parts[1:], None if last else pack(parts[0]))
         own[slot, 0] = parts[0]
         for k in range(1, members):
             own[slot, k] = 0.5 * parts[k]

time: 83.5 us -> 82.4 us (0.987)
  Pallas kernels: 33.5 us -> 32.5 us
    pallas_call x9, Pallas kernels: 33.5 us -> 32.5 us  [call(): pl.pallas_call(kernel, out_shape=list(outputs), in_specs=specs, out_specs...]
  transfers between devices with their start and end apart: 14 -> 14, of which waited for: 7 -> 7; matrix products, arithmetic and copies ran while one was open for 1% -> 1% of each run, Pallas kernels for 7% -> 8%
where the time goes in v4:
time: 82.4 us; the launch traced here: 82.2 us
  Pallas kernels  32.5 us (39%)
  waiting for transfers between devices  25.9 us (31%)
  starting transfers between devices  21.9 us (27%)
  local copies, waits for them, and re-layouts  1.81 us (2%)
    pallas_call x9, Pallas kernels, call(): pl.pallas_call(kernel, out_shape=list(outputs), in_specs=specs, out_specs...  32.5 us
    ppermute x3, waiting for transfers between devices, exchange(): received = [lax.ppermute(over_even, 'col', [(i, i ^ 1) for i in cols])]  14.7 us
    all_to_all x2, waiting for transfers between devices, per_device(): norms = lax.all_to_all(norms, ('row', 'col'), 0, 0, tiled=True)  8.79 us
    all_to_all x2, starting transfers between devices, per_device(): norms = lax.all_to_all(norms, ('row', 'col'), 0, 0, tiled=True)  8.48 us
    ppermute x3, starting transfers between devices, exchange(): received.append(lax.ppermute(over_odd, 'col', odd))  6.31 us
    ppermute x3, starting transfers between devices, exchange(): received = [lax.ppermute(over_even, 'col', [(i, i ^ 1) for i in cols])]  4.4 us
    ppermute x6, starting transfers between devices, exchange(): lax.ppermute(to_partner, 'row', [(i, i ^ place) for i in rows])  2.72 us
    ppermute x3, waiting for transfers between devices, exchange(): received.append(lax.ppermute(over_odd, 'col', odd))  2.11 us
  transfers between devices with their start and end apart: 14, of which 7 were waited for; matrix products, arithmetic and copies ran while one was open for 1% of the time, Pallas kernels for 8%

profile of v4, /device:TPU:0, one launch (start us, length us, event | category | flops | bytes accessed | tf_op | source)
XLA Modules:
  0.0 82.2 jit_solution(5680329310880622514)
XLA Ops:
  0.0 1.0 %copy-done = f32[2,4,128,128]{3,2,1,0:T(8,128)S(1)} copy-done((f32[2,4,128,128]{3,2,1,0:T(8,128)S(1)}, f32[2,4,128,128]{3,2,1,0:T(8,128)}, u32[]{:S(2)}) %copy-start) | copy-done | bytes 524312
  1.0 0.2 pack.1
  1.2 3.0 %collective-permute-start = (f32[2,200,128]{2,1,0:T(8,128)S(1)}, f32[2,200,128]{2,1,0:T(8,128)S(1)}, u32[]{:S(2)}, u32[]{:S(2)}) collective-permute-start(f32[2,200,128]{2,1,0:T(8,128)S(1)} %get-tuple-element.22), channel_id=1, source_target_pairs={{0,1},{1,0},{2,3},{3,2},{4,5},{5,4},{6,7},{7,6},{8,9},{9,8},{10,11... | collective-permute-start | bytes 614408 | tf_op jit(solution)/shard_map/ppermute | solution.py:324
  4.3 3.5 %collective-permute-start.1 = (f32[2,200,128]{2,1,0:T(8,128)S(1)}, f32[2,200,128]{2,1,0:T(8,128)S(1)}, u32[]{:S(2)}, u32[]{:S(2)}) collective-permute-start(f32[2,200,128]{2,1,0:T(8,128)S(1)} %get-tuple-element.23), channel_id=1, source_target_pairs={{0,7},{1,2},{2,1},{3,4},{4,3},{5,6},{6,5},{7,0},{8,15},{9,10},{10,... | collective-permute-start | bytes 614408 | tf_op jit(solution)/shard_map/ppermute | solution.py:325
  7.8 1.5 %collective-permute-start.3 = (f32[2,200,128]{2,1,0:T(8,128)S(1)}, f32[2,200,128]{2,1,0:T(8,128)S(1)}, u32[]{:S(2)}, u32[]{:S(2)}) collective-permute-start(f32[2,200,128]{2,1,0:T(8,128)S(1)} %get-tuple-element.24), channel_id=1, source_target_pairs={{0,16},{8,24},{16,0},{24,8},{1,17},{9,25},{17,1},{25,9},{2,18},{10... | collective-permute-start | bytes 614408 | tf_op jit(solution)/shard_map/ppermute | solution.py:328
  9.3 0.0 collective-permute-start.2
  9.3 0.8 copy.3.lists
  10.1 1.1 %links.1.refs_0_ = f32[10,128]{1,0:T(8,128)S(1)} custom-call(s32[64,4]{1,0:T(8,128)S(1)} %copy.3.lists), custom_call_target="tpu_custom_call" | custom-call | bytes 6144 | tf_op jit(solution)/shard_map/links/pallas_call | solution.py:346
  11.2 2.5 %collective-permute-done.refs_2_ = f32[2,200,128]{2,1,0:T(8,128)S(1)} collective-permute-done((f32[2,200,128]{2,1,0:T(8,128)S(1)}, f32[2,200,128]{2,1,0:T(8,128)S(1)}, u32[]{:S(2)}, u32[]{:S(2)}) %collective-permute-start) | collective-permute-done | bytes 204832 | tf_op jit(solution)/shard_map/ppermute | solution.py:324
  13.7 0.3 collective-permute-done.3.refs_5_
  14.1 2.1 %assemble.2 = (f32[32,1,128]{2,1,0:T(1,128)}, f32[2,7,128,128]{3,2,1,0:T(8,128)S(1)}) custom-call(f32[10,128]{1,0:T(8,128)S(1)} %links.1.refs_0_, f32[2,4,128,128]{3,2,1,0:T(8,128)S(1)} %get-tuple-element.21.refs_1_, f32[2,200,128]{2,1,0:T(8,128)S(1)} %collective-permute-done.refs_2_, f32[2,200,128]{2,1,0:T(8,128)S(1)} %collective-permute-done.1.refs_3_, ...), custom_call_target="tpu_custom_call" | custom-call | flops 1207959552 | bytes 2282496 | tf_op jit(solution)/shard_map/assemble/pallas_call | solution.py:346
  16.2 5.8 %all-to-all-start = ((f32[32,1,128]{2,1,0:T(1,128)}), f32[32,1,128]{2,1,0:T(1,128)S(1)}, u32[]{:S(2)}, u32[]{:S(2)}) async-start(f32[32,1,128]{2,1,0:T(1,128)} %get-tuple-element.25), calls=%async_computation | async-start | bytes 32768 | tf_op jit(solution)/shard_map/all_to_all | solution.py:392
  21.9 2.5 %cube.2.source.refs_2_ = f32[2,17,128,128]{3,2,1,0:T(8,128)S(1)} custom-call(f32[2,7,128,128]{3,2,1,0:T(8,128)S(1)} %get-tuple-element.26.blocks), custom_call_target="tpu_custom_call" | custom-call | flops 2415919104 | bytes 3145728 | tf_op jit(solution)/shard_map/cube/pallas_call | solution.py:346
  24.5 4.5 %all-to-all-done.norms = f32[32,1,128]{2,1,0:T(1,128)S(1)} async-done(((f32[32,1,128]{2,1,0:T(1,128)}), f32[32,1,128]{2,1,0:T(1,128)S(1)}, u32[]{:S(2)}, u32[]{:S(2)}) %all-to-all-start) | async-done | bytes 16416 | tf_op jit(solution)/shard_map/all_to_all | solution.py:392
  29.0 10.5 %sign.2 = (f32[2,4,128,128]{3,2,1,0:T(8,128)S(1)}, f32[2,200,128]{2,1,0:T(8,128)S(1)}, f32[2,200,128]{2,1,0:T(8,128)S(1)}, f32[2,200,128]{2,1,0:T(8,128)S(1)}) custom-call(f32[32,1,128]{2,1,0:T(1,128)S(1)} %all-to-all-done.norms, f32[2,17,128,128]{3,2,1,0:T(8,128)S(1)} %cube.2.source.refs_2_), custom_call_target="tpu_custom_call" | custom-call | flops 9663676416 | bytes 3383296 | tf_op jit(solution)/shard_map/sign/pallas_call | solution.py:346
  39.4 0.7 collective-permute-start.4
  40.1 1.4 %collective-permute-start.5 = (f32[2,200,128]{2,1,0:T(8,128)S(1)}, f32[2,200,128]{2,1,0:T(8,128)S(1)}, u32[]{:S(2)}, u32[]{:S(2)}) collective-permute-start(f32[2,200,128]{2,1,0:T(8,128)S(1)} %get-tuple-element.29), channel_id=1, source_target_pairs={{0,7},{1,2},{2,1},{3,4},{4,3},{5,6},{6,5},{7,0},{8,15},{9,10},{10,... | collective-permute-start | bytes 614408 | tf_op jit(solution)/shard_map/ppermute | solution.py:325
  41.5 0.6 collective-permute-start.7
  42.1 0.0 collective-permute-start.6
  42.1 8.6 %collective-permute-done.4.refs_3_ = f32[2,200,128]{2,1,0:T(8,128)S(1)} collective-permute-done((f32[2,200,128]{2,1,0:T(8,128)S(1)}, f32[2,200,128]{2,1,0:T(8,128)S(1)}, u32[]{:S(2)}, u32[]{:S(2)}) %collective-permute-start.4) | collective-permute-done | bytes 204832 | tf_op jit(solution)/shard_map/ppermute | solution.py:324
  50.7 2.1 %assemble.3 = (f32[32,1,128]{2,1,0:T(1,128)}, f32[2,7,128,128]{3,2,1,0:T(8,128)S(1)}) custom-call(f32[10,128]{1,0:T(8,128)S(1)} %links.1.refs_0_, f32[2,4,128,128]{3,2,1,0:T(8,128)S(1)} %get-tuple-element.27.refs_1_, f32[2,17,128,128]{3,2,1,0:T(8,128)S(1)} %cube.2.source.refs_2_, f32[2,200,128]{2,1,0:T(8,128)S(1)} %collective-permute-done.4.refs_3_, ...), custom_call_target="tpu_custom_call" | custom-call | flops 1207959552 | bytes 4510720 | tf_op jit(solution)/shard_map/assemble/pallas_call | solution.py:346
  52.9 2.7 %all-to-all-start.1 = ((f32[32,1,128]{2,1,0:T(1,128)}), f32[32,1,128]{2,1,0:T(1,128)S(1)}, u32[]{:S(2)}, u32[]{:S(2)}) async-start(f32[32,1,128]{2,1,0:T(1,128)} %get-tuple-element.31), calls=%async_computation.1 | async-start | bytes 32768 | tf_op jit(solution)/shard_map/all_to_all | solution.py:392
  55.6 2.5 %cube.3.source = f32[2,17,128,128]{3,2,1,0:T(8,128)S(1)} custom-call(f32[2,7,128,128]{3,2,1,0:T(8,128)S(1)} %get-tuple-element.32.blocks), custom_call_target="tpu_custom_call" | custom-call | flops 2415919104 | bytes 3145728 | tf_op jit(solution)/shard_map/cube/pallas_call | solution.py:346
  58.2 4.3 %all-to-all-done.1.norms = f32[32,1,128]{2,1,0:T(1,128)S(1)} async-done(((f32[32,1,128]{2,1,0:T(1,128)}), f32[32,1,128]{2,1,0:T(1,128)S(1)}, u32[]{:S(2)}, u32[]{:S(2)}) %all-to-all-start.1) | async-done | bytes 16416 | tf_op jit(solution)/shard_map/all_to_all | solution.py:392
  62.5 10.4 %sign.3 = (f32[2,4,128,128]{3,2,1,0:T(8,128)S(1)}, f32[2,128,128]{2,1,0:T(8,128)S(1)}, f32[2,128,128]{2,1,0:T(8,128)S(1)}, f32[2,128,128]{2,1,0:T(8,128)S(1)}) custom-call(f32[32,1,128]{2,1,0:T(1,128)S(1)} %all-to-all-done.1.norms, f32[2,17,128,128]{3,2,1,0:T(8,128)S(1)} %cube.3.source), custom_call_target="tpu_custom_call" | custom-call | flops 9663676416 | bytes 3162112 | tf_op jit(solution)/shard_map/sign/pallas_call | solution.py:346
  72.9 0.7 collective-permute-start.8
  73.6 1.4 %collective-permute-start.9 = (f32[2,128,128]{2,1,0:T(8,128)S(1)}, f32[2,128,128]{2,1,0:T(8,128)S(1)}, u32[]{:S(2)}, u32[]{:S(2)}) collective-permute-start(f32[2,128,128]{2,1,0:T(8,128)S(1)} %get-tuple-element.35), channel_id=1, source_target_pairs={{0,7},{1,2},{2,1},{3,4},{4,3},{5,6},{6,5},{7,0},{8,15},{9,10},{10,... | collective-permute-start | bytes 393224 | tf_op jit(solution)/shard_map/ppermute | solution.py:325
  74.9 0.6 collective-permute-start.11
  75.6 3.6 %collective-permute-done.8.refs_2_ = f32[2,128,128]{2,1,0:T(8,128)S(1)} collective-permute-done((f32[2,128,128]{2,1,0:T(8,128)S(1)}, f32[2,128,128]{2,1,0:T(8,128)S(1)}, u32[]{:S(2)}, u32[]{:S(2)}) %collective-permute-start.8) | collective-permute-done | bytes 131104 | tf_op jit(solution)/shard_map/ppermute | solution.py:324
  79.1 2.1 %collective-permute-done.9.refs_3_ = f32[2,128,128]{2,1,0:T(8,128)S(1)} collective-permute-done((f32[2,128,128]{2,1,0:T(8,128)S(1)}, f32[2,128,128]{2,1,0:T(8,128)S(1)}, u32[]{:S(2)}, u32[]{:S(2)}) %collective-permute-start.9) | collective-permute-done | bytes 131104 | tf_op jit(solution)/shard_map/ppermute | solution.py:325
  81.2 0.0 collective-permute-done.11.refs_5_
  81.2 1.0 %density.1 = f32[2,4,128,128]{3,2,1,0:T(8,128)} custom-call(f32[10,128]{1,0:T(8,128)S(1)} %links.1.refs_0_, f32[2,4,128,128]{3,2,1,0:T(8,128)S(1)} %get-tuple-element.33.refs_1_, f32[2,128,128]{2,1,0:T(8,128)S(1)} %collective-permute-done.8.refs_2_, f32[2,128,128]{2,1,0:T(8,128)S(1)} %collective-permute-done.9.refs_3_, ...), custom_call_target="tpu_custom_call" | custom-call | bytes 1577984 | tf_op jit(solution)/shard_map/density/pallas_call | solution.py:346
  (8 shorter events, 0.0 us)
Async XLA Ops:
  0.0 1.0 %copy-start = (f32[2,4,128,128]{3,2,1,0:T(8,128)S(1)}, f32[2,4,128,128]{3,2,1,0:T(8,128)}, u32[]{:S(2)}) copy-start(f32[2,4,128,128]{3,2,1,0:T(8,128)} %own.1) | copy-start | bytes 1572868
  1.2 12.5 %collective-permute-start = (f32[2,200,128]{2,1,0:T(8,128)S(1)}, f32[2,200,128]{2,1,0:T(8,128)S(1)}, u32[]{:S(2)}, u32[]{:S(2)}) collective-permute-start(f32[2,200,128]{2,1,0:T(8,128)S(1)} %get-tuple-element.22), channel_id=1, source_target_pairs={{0,1},{1,0},{2,3},{3,2},{4,5},{5,4},{6,7},{7,6},{8,9},{9,8},{10,11... | collective-permute-start | bytes 614408 | tf_op jit(solution)/shard_map/ppermute | solution.py:324
  4.3 9.5 %collective-permute-start.1 = (f32[2,200,128]{2,1,0:T(8,128)S(1)}, f32[2,200,128]{2,1,0:T(8,128)S(1)}, u32[]{:S(2)}, u32[]{:S(2)}) collective-permute-start(f32[2,200,128]{2,1,0:T(8,128)S(1)} %get-tuple-element.23), channel_id=1, source_target_pairs={{0,7},{1,2},{2,1},{3,4},{4,3},{5,6},{6,5},{7,0},{8,15},{9,10},{10,... | collective-permute-start | bytes 614408 | tf_op jit(solution)/shard_map/ppermute | solution.py:325
  7.8 6.3 %collective-permute-start.3 = (f32[2,200,128]{2,1,0:T(8,128)S(1)}, f32[2,200,128]{2,1,0:T(8,128)S(1)}, u32[]{:S(2)}, u32[]{:S(2)}) collective-permute-start(f32[2,200,128]{2,1,0:T(8,128)S(1)} %get-tuple-element.24), channel_id=1, source_target_pairs={{0,16},{8,24},{16,0},{24,8},{1,17},{9,25},{17,1},{25,9},{2,18},{10... | collective-permute-start | bytes 614408 | tf_op jit(solution)/shard_map/ppermute | solution.py:328
  9.3 4.8 %collective-permute-start.2 = (f32[2,200,128]{2,1,0:T(8,128)S(1)}, f32[2,200,128]{2,1,0:T(8,128)S(1)}, u32[]{:S(2)}, u32[]{:S(2)}) collective-permute-start(f32[2,200,128]{2,1,0:T(8,128)S(1)} %get-tuple-element.24), channel_id=1, source_target_pairs={{0,8},{8,0},{16,24},{24,16},{1,9},{9,1},{17,25},{25,17},{2,10},{10... | collective-permute-start | bytes 614408 | tf_op jit(solution)/shard_map/ppermute | solution.py:328
  16.2 12.8 %all-to-all-start = ((f32[32,1,128]{2,1,0:T(1,128)}), f32[32,1,128]{2,1,0:T(1,128)S(1)}, u32[]{:S(2)}, u32[]{:S(2)}) async-start(f32[32,1,128]{2,1,0:T(1,128)} %get-tuple-element.25), calls=%async_computation | async-start | bytes 32768 | tf_op jit(solution)/shard_map/all_to_all | solution.py:392
  39.4 11.3 %collective-permute-start.4 = (f32[2,200,128]{2,1,0:T(8,128)S(1)}, f32[2,200,128]{2,1,0:T(8,128)S(1)}, u32[]{:S(2)}, u32[]{:S(2)}) collective-permute-start(f32[2,200,128]{2,1,0:T(8,128)S(1)} %get-tuple-element.28), channel_id=1, source_target_pairs={{0,1},{1,0},{2,3},{3,2},{4,5},{5,4},{6,7},{7,6},{8,9},{9,8},{10,11... | collective-permute-start | bytes 614408 | tf_op jit(solution)/shard_map/ppermute | solution.py:324
  40.1 10.6 %collective-permute-start.5 = (f32[2,200,128]{2,1,0:T(8,128)S(1)}, f32[2,200,128]{2,1,0:T(8,128)S(1)}, u32[]{:S(2)}, u32[]{:S(2)}) collective-permute-start(f32[2,200,128]{2,1,0:T(8,128)S(1)} %get-tuple-element.29), channel_id=1, source_target_pairs={{0,7},{1,2},{2,1},{3,4},{4,3},{5,6},{6,5},{7,0},{8,15},{9,10},{10,... | collective-permute-start | bytes 614408 | tf_op jit(solution)/shard_map/ppermute | solution.py:325
  41.5 9.2 %collective-permute-start.7 = (f32[2,200,128]{2,1,0:T(8,128)S(1)}, f32[2,200,128]{2,1,0:T(8,128)S(1)}, u32[]{:S(2)}, u32[]{:S(2)}) collective-permute-start(f32[2,200,128]{2,1,0:T(8,128)S(1)} %get-tuple-element.30), channel_id=1, source_target_pairs={{0,16},{8,24},{16,0},{24,8},{1,17},{9,25},{17,1},{25,9},{2,18},{10... | collective-permute-start | bytes 614408 | tf_op jit(solution)/shard_map/ppermute | solution.py:328
  42.1 8.6 %collective-permute-start.6 = (f32[2,200,128]{2,1,0:T(8,128)S(1)}, f32[2,200,128]{2,1,0:T(8,128)S(1)}, u32[]{:S(2)}, u32[]{:S(2)}) collective-permute-start(f32[2,200,128]{2,1,0:T(8,128)S(1)} %get-tuple-element.30), channel_id=1, source_target_pairs={{0,8},{8,0},{16,24},{24,16},{1,9},{9,1},{17,25},{25,17},{2,10},{10... | collective-permute-start | bytes 614408 | tf_op jit(solution)/shard_map/ppermute | solution.py:328
  52.9 9.6 %all-to-all-start.1 = ((f32[32,1,128]{2,1,0:T(1,128)}), f32[32,1,128]{2,1,0:T(1,128)S(1)}, u32[]{:S(2)}, u32[]{:S(2)}) async-start(f32[32,1,128]{2,1,0:T(1,128)} %get-tuple-element.31), calls=%async_computation.1 | async-start | bytes 32768 | tf_op jit(solution)/shard_map/all_to_all | solution.py:392
  72.9 6.2 %collective-permute-start.8 = (f32[2,128,128]{2,1,0:T(8,128)S(1)}, f32[2,128,128]{2,1,0:T(8,128)S(1)}, u32[]{:S(2)}, u32[]{:S(2)}) collective-permute-start(f32[2,128,128]{2,1,0:T(8,128)S(1)} %get-tuple-element.34), channel_id=1, source_target_pairs={{0,1},{1,0},{2,3},{3,2},{4,5},{5,4},{6,7},{7,6},{8,9},{9,8},{10,11... | collective-permute-start | bytes 393224 | tf_op jit(solution)/shard_map/ppermute | solution.py:324
  73.6 7.7 %collective-permute-start.9 = (f32[2,128,128]{2,1,0:T(8,128)S(1)}, f32[2,128,128]{2,1,0:T(8,128)S(1)}, u32[]{:S(2)}, u32[]{:S(2)}) collective-permute-start(f32[2,128,128]{2,1,0:T(8,128)S(1)} %get-tuple-element.35), channel_id=1, source_target_pairs={{0,7},{1,2},{2,1},{3,4},{4,3},{5,6},{6,5},{7,0},{8,15},{9,10},{10,... | collective-permute-start | bytes 393224 | tf_op jit(solution)/shard_map/ppermute | solution.py:325
  74.9 6.3 %collective-permute-start.11 = (f32[2,128,128]{2,1,0:T(8,128)S(1)}, f32[2,128,128]{2,1,0:T(8,128)S(1)}, u32[]{:S(2)}, u32[]{:S(2)}) collective-permute-start(f32[2,128,128]{2,1,0:T(8,128)S(1)} %get-tuple-element.36), channel_id=1, source_target_pairs={{0,16},{8,24},{16,0},{24,8},{1,17},{9,25},{17,1},{25,9},{2,18},{10... | collective-permute-start | bytes 393224 | tf_op jit(solution)/shard_map/ppermute | solution.py:328
  75.5 5.7 %collective-permute-start.10 = (f32[2,128,128]{2,1,0:T(8,128)S(1)}, f32[2,128,128]{2,1,0:T(8,128)S(1)}, u32[]{:S(2)}, u32[]{:S(2)}) collective-permute-start(f32[2,128,128]{2,1,0:T(8,128)S(1)} %get-tuple-element.36), channel_id=1, source_target_pairs={{0,8},{8,0},{16,24},{24,16},{1,9},{9,1},{17,25},{25,17},{2,10},{10... | collective-permute-start | bytes 393224 | tf_op jit(solution)/shard_map/ppermute | solution.py:328

commit v5 on v4

--- a/solution.py
+++ b/solution.py
@@ -68,6 +68,14 @@
         high, low = split(turned(value))
         target[0][slot, columns, rows] = high
         target[1][slot, columns, rows] = low
+
+
+def symmetric_tile(tile):
+    half = tile.shape[0] // 2
+    beside = tile[:half, half:]
+    upper = jnp.concatenate([symmetric(tile[:half, :half]), beside], 1)
+    lower = jnp.concatenate([turned(beside), symmetric(tile[half:, half:])], 1)
+    return jnp.concatenate([upper, lower], 0)
 
 
 def store_arrow(target, slot, blocks):
@@ -255,7 +263,7 @@
         at = 2 * members - 1
         for row in range(members):
             for col in range(row, members):
-                value = cubic * source[slot, at]
+                value = cubic * (symmetric(source[slot, at]) if row == col else source[slot, at])
                 if row == col:
                     value = value + linear * source[slot, members - 1 + row if row else 0]
                 elif row == 0:
@@ -277,6 +285,8 @@
         target = (xh.at[1 - repeat % 2], xl.at[1 - repeat % 2])
         for _, rows, columns, off in upper_tiles(order):
             tile = product(iterate, (yh.at[slot], yl.at[slot]), rows, columns)
+            if not off:
+                tile = symmetric_tile(tile)
             value = 1.5 * x[slot, rows, columns] - 0.5 * tile
             x[slot, rows, columns] = value
             store_split(target, slot, rows, columns, value, off)

time: 82.4 us -> 82.4 us (level)
  no operation moved by 1% of the time
where the time goes in v5:
time: 82.4 us; the launch traced here: 82.2 us
  Pallas kernels  32.4 us (39%)
  waiting for transfers between devices  25.9 us (31%)
  starting transfers between devices  21.9 us (27%)
  local copies, waits for them, and re-layouts  1.81 us (2%)
    pallas_call x9, Pallas kernels, call(): pl.pallas_call(kernel, out_shape=list(outputs), in_specs=specs, out_specs...  32.4 us
    ppermute x3, waiting for transfers between devices, exchange(): received = [lax.ppermute(over_even, 'col', [(i, i ^ 1) for i in cols])]  14.7 us
    all_to_all x2, waiting for transfers between devices, per_device(): norms = lax.all_to_all(norms, ('row', 'col'), 0, 0, tiled=True)  8.79 us
    all_to_all x2, starting transfers between devices, per_device(): norms = lax.all_to_all(norms, ('row', 'col'), 0, 0, tiled=True)  8.48 us
    ppermute x3, starting transfers between devices, exchange(): received.append(lax.ppermute(over_odd, 'col', odd))  6.31 us
    ppermute x3, starting transfers between devices, exchange(): received = [lax.ppermute(over_even, 'col', [(i, i ^ 1) for i in cols])]  4.4 us
    ppermute x6, starting transfers between devices, exchange(): lax.ppermute(to_partner, 'row', [(i, i ^ place) for i in rows])  2.72 us
    ppermute x3, waiting for transfers between devices, exchange(): received.append(lax.ppermute(over_odd, 'col', odd))  2.11 us
  transfers between devices with their start and end apart: 14, of which 7 were waited for; matrix products, arithmetic and copies ran while one was open for 1% of the time, Pallas kernels for 8%

profile of v5, /device:TPU:0, one launch (start us, length us, event | category | flops | bytes accessed | tf_op | source)
XLA Modules:
  0.0 82.2 jit_solution(17912164355057212689)
XLA Ops:
  0.0 1.0 %copy-done = f32[2,4,128,128]{3,2,1,0:T(8,128)S(1)} copy-done((f32[2,4,128,128]{3,2,1,0:T(8,128)S(1)}, f32[2,4,128,128]{3,2,1,0:T(8,128)}, u32[]{:S(2)}) %copy-start) | copy-done | bytes 524312
  1.0 0.2 pack.1
  1.2 3.0 %collective-permute-start = (f32[2,200,128]{2,1,0:T(8,128)S(1)}, f32[2,200,128]{2,1,0:T(8,128)S(1)}, u32[]{:S(2)}, u32[]{:S(2)}) collective-permute-start(f32[2,200,128]{2,1,0:T(8,128)S(1)} %get-tuple-element.22), channel_id=1, source_target_pairs={{0,1},{1,0},{2,3},{3,2},{4,5},{5,4},{6,7},{7,6},{8,9},{9,8},{10,11... | collective-permute-start | bytes 614408 | tf_op jit(solution)/shard_map/ppermute | solution.py:334
  4.3 3.5 %collective-permute-start.1 = (f32[2,200,128]{2,1,0:T(8,128)S(1)}, f32[2,200,128]{2,1,0:T(8,128)S(1)}, u32[]{:S(2)}, u32[]{:S(2)}) collective-permute-start(f32[2,200,128]{2,1,0:T(8,128)S(1)} %get-tuple-element.23), channel_id=1, source_target_pairs={{0,7},{1,2},{2,1},{3,4},{4,3},{5,6},{6,5},{7,0},{8,15},{9,10},{10,... | collective-permute-start | bytes 614408 | tf_op jit(solution)/shard_map/ppermute | solution.py:335
  7.8 1.5 %collective-permute-start.3 = (f32[2,200,128]{2,1,0:T(8,128)S(1)}, f32[2,200,128]{2,1,0:T(8,128)S(1)}, u32[]{:S(2)}, u32[]{:S(2)}) collective-permute-start(f32[2,200,128]{2,1,0:T(8,128)S(1)} %get-tuple-element.24), channel_id=1, source_target_pairs={{0,16},{8,24},{16,0},{24,8},{1,17},{9,25},{17,1},{25,9},{2,18},{10... | collective-permute-start | bytes 614408 | tf_op jit(solution)/shard_map/ppermute | solution.py:338
  9.3 0.0 collective-permute-start.2
  9.3 0.8 copy.3.lists
  10.1 1.1 %links.1.refs_0_ = f32[10,128]{1,0:T(8,128)S(1)} custom-call(s32[64,4]{1,0:T(8,128)S(1)} %copy.3.lists), custom_call_target="tpu_custom_call" | custom-call | bytes 6144 | tf_op jit(solution)/shard_map/links/pallas_call | solution.py:356
  11.2 2.5 %collective-permute-done.refs_2_ = f32[2,200,128]{2,1,0:T(8,128)S(1)} collective-permute-done((f32[2,200,128]{2,1,0:T(8,128)S(1)}, f32[2,200,128]{2,1,0:T(8,128)S(1)}, u32[]{:S(2)}, u32[]{:S(2)}) %collective-permute-start) | collective-permute-done | bytes 204832 | tf_op jit(solution)/shard_map/ppermute | solution.py:334
  13.7 0.3 collective-permute-done.3.refs_5_
  14.1 2.1 %assemble.2 = (f32[32,1,128]{2,1,0:T(1,128)}, f32[2,7,128,128]{3,2,1,0:T(8,128)S(1)}) custom-call(f32[10,128]{1,0:T(8,128)S(1)} %links.1.refs_0_, f32[2,4,128,128]{3,2,1,0:T(8,128)S(1)} %get-tuple-element.21.refs_1_, f32[2,200,128]{2,1,0:T(8,128)S(1)} %collective-permute-done.refs_2_, f32[2,200,128]{2,1,0:T(8,128)S(1)} %collective-permute-done.1.refs_3_, ...), custom_call_target="tpu_custom_call" | custom-call | flops 1207959552 | bytes 2282496 | tf_op jit(solution)/shard_map/assemble/pallas_call | solution.py:356
  16.2 5.8 %all-to-all-start = ((f32[32,1,128]{2,1,0:T(1,128)}), f32[32,1,128]{2,1,0:T(1,128)S(1)}, u32[]{:S(2)}, u32[]{:S(2)}) async-start(f32[32,1,128]{2,1,0:T(1,128)} %get-tuple-element.25), calls=%async_computation | async-start | bytes 32768 | tf_op jit(solution)/shard_map/all_to_all | solution.py:402
  21.9 2.5 %cube.2.source.refs_2_ = f32[2,17,128,128]{3,2,1,0:T(8,128)S(1)} custom-call(f32[2,7,128,128]{3,2,1,0:T(8,128)S(1)} %get-tuple-element.26.blocks), custom_call_target="tpu_custom_call" | custom-call | flops 2415919104 | bytes 3145728 | tf_op jit(solution)/shard_map/cube/pallas_call | solution.py:356
  24.5 4.5 %all-to-all-done.norms = f32[32,1,128]{2,1,0:T(1,128)S(1)} async-done(((f32[32,1,128]{2,1,0:T(1,128)}), f32[32,1,128]{2,1,0:T(1,128)S(1)}, u32[]{:S(2)}, u32[]{:S(2)}) %all-to-all-start) | async-done | bytes 16416 | tf_op jit(solution)/shard_map/all_to_all | solution.py:402
  29.0 10.4 %sign.2 = (f32[2,4,128,128]{3,2,1,0:T(8,128)S(1)}, f32[2,200,128]{2,1,0:T(8,128)S(1)}, f32[2,200,128]{2,1,0:T(8,128)S(1)}, f32[2,200,128]{2,1,0:T(8,128)S(1)}) custom-call(f32[32,1,128]{2,1,0:T(1,128)S(1)} %all-to-all-done.norms, f32[2,17,128,128]{3,2,1,0:T(8,128)S(1)} %cube.2.source.refs_2_), custom_call_target="tpu_custom_call" | custom-call | flops 9663676416 | bytes 3383296 | tf_op jit(solution)/shard_map/sign/pallas_call | solution.py:356
  39.4 0.7 collective-permute-start.4
  40.1 1.4 %collective-permute-start.5 = (f32[2,200,128]{2,1,0:T(8,128)S(1)}, f32[2,200,128]{2,1,0:T(8,128)S(1)}, u32[]{:S(2)}, u32[]{:S(2)}) collective-permute-start(f32[2,200,128]{2,1,0:T(8,128)S(1)} %get-tuple-element.29), channel_id=1, source_target_pairs={{0,7},{1,2},{2,1},{3,4},{4,3},{5,6},{6,5},{7,0},{8,15},{9,10},{10,... | collective-permute-start | bytes 614408 | tf_op jit(solution)/shard_map/ppermute | solution.py:335
  41.5 0.6 collective-permute-start.7
  42.1 0.0 collective-permute-start.6
  42.1 8.6 %collective-permute-done.4.refs_3_ = f32[2,200,128]{2,1,0:T(8,128)S(1)} collective-permute-done((f32[2,200,128]{2,1,0:T(8,128)S(1)}, f32[2,200,128]{2,1,0:T(8,128)S(1)}, u32[]{:S(2)}, u32[]{:S(2)}) %collective-permute-start.4) | collective-permute-done | bytes 204832 | tf_op jit(solution)/shard_map/ppermute | solution.py:334
  50.7 0.0 collective-permute-done.5.refs_4_
  50.7 2.1 %assemble.3 = (f32[32,1,128]{2,1,0:T(1,128)}, f32[2,7,128,128]{3,2,1,0:T(8,128)S(1)}) custom-call(f32[10,128]{1,0:T(8,128)S(1)} %links.1.refs_0_, f32[2,4,128,128]{3,2,1,0:T(8,128)S(1)} %get-tuple-element.27.refs_1_, f32[2,17,128,128]{3,2,1,0:T(8,128)S(1)} %cube.2.source.refs_2_, f32[2,200,128]{2,1,0:T(8,128)S(1)} %collective-permute-done.4.refs_3_, ...), custom_call_target="tpu_custom_call" | custom-call | flops 1207959552 | bytes 4510720 | tf_op jit(solution)/shard_map/assemble/pallas_call | solution.py:356
  52.8 2.7 %all-to-all-start.1 = ((f32[32,1,128]{2,1,0:T(1,128)}), f32[32,1,128]{2,1,0:T(1,128)S(1)}, u32[]{:S(2)}, u32[]{:S(2)}) async-start(f32[32,1,128]{2,1,0:T(1,128)} %get-tuple-element.31), calls=%async_computation.1 | async-start | bytes 32768 | tf_op jit(solution)/shard_map/all_to_all | solution.py:402
  55.6 2.5 %cube.3.source = f32[2,17,128,128]{3,2,1,0:T(8,128)S(1)} custom-call(f32[2,7,128,128]{3,2,1,0:T(8,128)S(1)} %get-tuple-element.32.blocks), custom_call_target="tpu_custom_call" | custom-call | flops 2415919104 | bytes 3145728 | tf_op jit(solution)/shard_map/cube/pallas_call | solution.py:356
  58.1 4.3 %all-to-all-done.1.norms = f32[32,1,128]{2,1,0:T(1,128)S(1)} async-done(((f32[32,1,128]{2,1,0:T(1,128)}), f32[32,1,128]{2,1,0:T(1,128)S(1)}, u32[]{:S(2)}, u32[]{:S(2)}) %all-to-all-start.1) | async-done | bytes 16416 | tf_op jit(solution)/shard_map/all_to_all | solution.py:402
  62.4 10.4 %sign.3 = (f32[2,4,128,128]{3,2,1,0:T(8,128)S(1)}, f32[2,128,128]{2,1,0:T(8,128)S(1)}, f32[2,128,128]{2,1,0:T(8,128)S(1)}, f32[2,128,128]{2,1,0:T(8,128)S(1)}) custom-call(f32[32,1,128]{2,1,0:T(1,128)S(1)} %all-to-all-done.1.norms, f32[2,17,128,128]{3,2,1,0:T(8,128)S(1)} %cube.3.source), custom_call_target="tpu_custom_call" | custom-call | flops 9663676416 | bytes 3162112 | tf_op jit(solution)/shard_map/sign/pallas_call | solution.py:356
  72.8 0.7 collective-permute-start.8
  73.5 1.4 %collective-permute-start.9 = (f32[2,128,128]{2,1,0:T(8,128)S(1)}, f32[2,128,128]{2,1,0:T(8,128)S(1)}, u32[]{:S(2)}, u32[]{:S(2)}) collective-permute-start(f32[2,128,128]{2,1,0:T(8,128)S(1)} %get-tuple-element.35), channel_id=1, source_target_pairs={{0,7},{1,2},{2,1},{3,4},{4,3},{5,6},{6,5},{7,0},{8,15},{9,10},{10,... | collective-permute-start | bytes 393224 | tf_op jit(solution)/shard_map/ppermute | solution.py:335
  74.9 0.6 collective-permute-start.11
  75.5 3.6 %collective-permute-done.8.refs_2_ = f32[2,128,128]{2,1,0:T(8,128)S(1)} collective-permute-done((f32[2,128,128]{2,1,0:T(8,128)S(1)}, f32[2,128,128]{2,1,0:T(8,128)S(1)}, u32[]{:S(2)}, u32[]{:S(2)}) %collective-permute-start.8) | collective-permute-done | bytes 131104 | tf_op jit(solution)/shard_map/ppermute | solution.py:334
  79.1 2.1 %collective-permute-done.9.refs_3_ = f32[2,128,128]{2,1,0:T(8,128)S(1)} collective-permute-done((f32[2,128,128]{2,1,0:T(8,128)S(1)}, f32[2,128,128]{2,1,0:T(8,128)S(1)}, u32[]{:S(2)}, u32[]{:S(2)}) %collective-permute-start.9) | collective-permute-done | bytes 131104 | tf_op jit(solution)/shard_map/ppermute | solution.py:335
  81.2 1.0 %density.1 = f32[2,4,128,128]{3,2,1,0:T(8,128)} custom-call(f32[10,128]{1,0:T(8,128)S(1)} %links.1.refs_0_, f32[2,4,128,128]{3,2,1,0:T(8,128)S(1)} %get-tuple-element.33.refs_1_, f32[2,128,128]{2,1,0:T(8,128)S(1)} %collective-permute-done.8.refs_2_, f32[2,128,128]{2,1,0:T(8,128)S(1)} %collective-permute-done.9.refs_3_, ...), custom_call_target="tpu_custom_call" | custom-call | bytes 1577984 | tf_op jit(solution)/shard_map/density/pallas_call | solution.py:356
  (8 shorter events, 0.0 us)
Async XLA Ops:
  0.0 1.0 %copy-start = (f32[2,4,128,128]{3,2,1,0:T(8,128)S(1)}, f32[2,4,128,128]{3,2,1,0:T(8,128)}, u32[]{:S(2)}) copy-start(f32[2,4,128,128]{3,2,1,0:T(8,128)} %own.1) | copy-start | bytes 1572868
  1.2 12.5 %collective-permute-start = (f32[2,200,128]{2,1,0:T(8,128)S(1)}, f32[2,200,128]{2,1,0:T(8,128)S(1)}, u32[]{:S(2)}, u32[]{:S(2)}) collective-permute-start(f32[2,200,128]{2,1,0:T(8,128)S(1)} %get-tuple-element.22), channel_id=1, source_target_pairs={{0,1},{1,0},{2,3},{3,2},{4,5},{5,4},{6,7},{7,6},{8,9},{9,8},{10,11... | collective-permute-start | bytes 614408 | tf_op jit(solution)/shard_map/ppermute | solution.py:334
  4.3 9.5 %collective-permute-start.1 = (f32[2,200,128]{2,1,0:T(8,128)S(1)}, f32[2,200,128]{2,1,0:T(8,128)S(1)}, u32[]{:S(2)}, u32[]{:S(2)}) collective-permute-start(f32[2,200,128]{2,1,0:T(8,128)S(1)} %get-tuple-element.23), channel_id=1, source_target_pairs={{0,7},{1,2},{2,1},{3,4},{4,3},{5,6},{6,5},{7,0},{8,15},{9,10},{10,... | collective-permute-start | bytes 614408 | tf_op jit(solution)/shard_map/ppermute | solution.py:335
  7.8 6.3 %collective-permute-start.3 = (f32[2,200,128]{2,1,0:T(8,128)S(1)}, f32[2,200,128]{2,1,0:T(8,128)S(1)}, u32[]{:S(2)}, u32[]{:S(2)}) collective-permute-start(f32[2,200,128]{2,1,0:T(8,128)S(1)} %get-tuple-element.24), channel_id=1, source_target_pairs={{0,16},{8,24},{16,0},{24,8},{1,17},{9,25},{17,1},{25,9},{2,18},{10... | collective-permute-start | bytes 614408 | tf_op jit(solution)/shard_map/ppermute | solution.py:338
  9.3 4.8 %collective-permute-start.2 = (f32[2,200,128]{2,1,0:T(8,128)S(1)}, f32[2,200,128]{2,1,0:T(8,128)S(1)}, u32[]{:S(2)}, u32[]{:S(2)}) collective-permute-start(f32[2,200,128]{2,1,0:T(8,128)S(1)} %get-tuple-element.24), channel_id=1, source_target_pairs={{0,8},{8,0},{16,24},{24,16},{1,9},{9,1},{17,25},{25,17},{2,10},{10... | collective-permute-start | bytes 614408 | tf_op jit(solution)/shard_map/ppermute | solution.py:338
  16.2 12.8 %all-to-all-start = ((f32[32,1,128]{2,1,0:T(1,128)}), f32[32,1,128]{2,1,0:T(1,128)S(1)}, u32[]{:S(2)}, u32[]{:S(2)}) async-start(f32[32,1,128]{2,1,0:T(1,128)} %get-tuple-element.25), calls=%async_computation | async-start | bytes 32768 | tf_op jit(solution)/shard_map/all_to_all | solution.py:402
  39.4 11.3 %collective-permute-start.4 = (f32[2,200,128]{2,1,0:T(8,128)S(1)}, f32[2,200,128]{2,1,0:T(8,128)S(1)}, u32[]{:S(2)}, u32[]{:S(2)}) collective-permute-start(f32[2,200,128]{2,1,0:T(8,128)S(1)} %get-tuple-element.28), channel_id=1, source_target_pairs={{0,1},{1,0},{2,3},{3,2},{4,5},{5,4},{6,7},{7,6},{8,9},{9,8},{10,11... | collective-permute-start | bytes 614408 | tf_op jit(solution)/shard_map/ppermute | solution.py:334
  40.1 10.6 %collective-permute-start.5 = (f32[2,200,128]{2,1,0:T(8,128)S(1)}, f32[2,200,128]{2,1,0:T(8,128)S(1)}, u32[]{:S(2)}, u32[]{:S(2)}) collective-permute-start(f32[2,200,128]{2,1,0:T(8,128)S(1)} %get-tuple-element.29), channel_id=1, source_target_pairs={{0,7},{1,2},{2,1},{3,4},{4,3},{5,6},{6,5},{7,0},{8,15},{9,10},{10,... | collective-permute-start | bytes 614408 | tf_op jit(solution)/shard_map/ppermute | solution.py:335
  41.5 9.2 %collective-permute-start.7 = (f32[2,200,128]{2,1,0:T(8,128)S(1)}, f32[2,200,128]{2,1,0:T(8,128)S(1)}, u32[]{:S(2)}, u32[]{:S(2)}) collective-permute-start(f32[2,200,128]{2,1,0:T(8,128)S(1)} %get-tuple-element.30), channel_id=1, source_target_pairs={{0,16},{8,24},{16,0},{24,8},{1,17},{9,25},{17,1},{25,9},{2,18},{10... | collective-permute-start | bytes 614408 | tf_op jit(solution)/shard_map/ppermute | solution.py:338
  42.1 8.6 %collective-permute-start.6 = (f32[2,200,128]{2,1,0:T(8,128)S(1)}, f32[2,200,128]{2,1,0:T(8,128)S(1)}, u32[]{:S(2)}, u32[]{:S(2)}) collective-permute-start(f32[2,200,128]{2,1,0:T(8,128)S(1)} %get-tuple-element.30), channel_id=1, source_target_pairs={{0,8},{8,0},{16,24},{24,16},{1,9},{9,1},{17,25},{25,17},{2,10},{10... | collective-permute-start | bytes 614408 | tf_op jit(solution)/shard_map/ppermute | solution.py:338
  52.8 9.6 %all-to-all-start.1 = ((f32[32,1,128]{2,1,0:T(1,128)}), f32[32,1,128]{2,1,0:T(1,128)S(1)}, u32[]{:S(2)}, u32[]{:S(2)}) async-start(f32[32,1,128]{2,1,0:T(1,128)} %get-tuple-element.31), calls=%async_computation.1 | async-start | bytes 32768 | tf_op jit(solution)/shard_map/all_to_all | solution.py:402
  72.8 6.2 %collective-permute-start.8 = (f32[2,128,128]{2,1,0:T(8,128)S(1)}, f32[2,128,128]{2,1,0:T(8,128)S(1)}, u32[]{:S(2)}, u32[]{:S(2)}) collective-permute-start(f32[2,128,128]{2,1,0:T(8,128)S(1)} %get-tuple-element.34), channel_id=1, source_target_pairs={{0,1},{1,0},{2,3},{3,2},{4,5},{5,4},{6,7},{7,6},{8,9},{9,8},{10,11... | collective-permute-start | bytes 393224 | tf_op jit(solution)/shard_map/ppermute | solution.py:334
  73.5 7.7 %collective-permute-start.9 = (f32[2,128,128]{2,1,0:T(8,128)S(1)}, f32[2,128,128]{2,1,0:T(8,128)S(1)}, u32[]{:S(2)}, u32[]{:S(2)}) collective-permute-start(f32[2,128,128]{2,1,0:T(8,128)S(1)} %get-tuple-element.35), channel_id=1, source_target_pairs={{0,7},{1,2},{2,1},{3,4},{4,3},{5,6},{6,5},{7,0},{8,15},{9,10},{10,... | collective-permute-start | bytes 393224 | tf_op jit(solution)/shard_map/ppermute | solution.py:335
  74.9 6.3 %collective-permute-start.11 = (f32[2,128,128]{2,1,0:T(8,128)S(1)}, f32[2,128,128]{2,1,0:T(8,128)S(1)}, u32[]{:S(2)}, u32[]{:S(2)}) collective-permute-start(f32[2,128,128]{2,1,0:T(8,128)S(1)} %get-tuple-element.36), channel_id=1, source_target_pairs={{0,16},{8,24},{16,0},{24,8},{1,17},{9,25},{17,1},{25,9},{2,18},{10... | collective-permute-start | bytes 393224 | tf_op jit(solution)/shard_map/ppermute | solution.py:338
  75.5 5.7 %collective-permute-start.10 = (f32[2,128,128]{2,1,0:T(8,128)S(1)}, f32[2,128,128]{2,1,0:T(8,128)S(1)}, u32[]{:S(2)}, u32[]{:S(2)}) collective-permute-start(f32[2,128,128]{2,1,0:T(8,128)S(1)} %get-tuple-element.36), channel_id=1, source_target_pairs={{0,8},{8,0},{16,24},{24,16},{1,9},{9,1},{17,25},{25,17},{2,10},{10... | collective-permute-start | bytes 393224 | tf_op jit(solution)/shard_map/ppermute | solution.py:338

commit v6 on v4

--- a/solution.py
+++ b/solution.py
@@ -34,30 +34,44 @@
     return lax.dot_general(left, right, (((1,), (0,)), ((), ())), preferred_element_type=f32)
 
 
-def product(left, right, rows, cols):
-    left_high, left_low = left[0][rows, :], left[1][rows, :]
-    right_high, right_low = right[0][:, cols], right[1][:, cols]
-    return dot(
-        jnp.concatenate([left_high, left_low, left_high], 1),
-        jnp.concatenate([right_high, right_high, right_low], 0),
-    )
-
-
-def upper_tiles(order):
-    tile = order // 2
-    for place, (row, col) in enumerate(((0, 0), (0, 1), (1, 1))):
-        yield place, pl.ds(row * tile, tile), pl.ds(col * tile, tile), row != col
-
-
-def square_tiles(high, low, mixed):
-    order = high.shape[0]
-    first, second = pl.ds(0, order // 2), pl.ds(order // 2, order // 2)
-    mixed[3] = dot(high[second, :], low[:, first])
-    for place, rows, columns, off in upper_tiles(order):
-        left = high[rows, :]
-        mixed[place] = dot(left, low[:, columns])
-        tile = dot(left, high[:, columns]) + (mixed[place] + turned(mixed[3 if off else place]))
-        yield place, rows, columns, off, tile
+def span(first, count=1):
+    return pl.ds(first * SIDE, count * SIDE)
+
+
+STRIPS = (((0,), (0, 1)), ((1, 3), (1, 2)), ((2,), (2, 0)), ((3,), (3, 0)))
+PLACES = tuple((row, col) for rows, cols in STRIPS for row in rows for col in cols)
+
+
+def block_rows(matrix, rows):
+    return jnp.concatenate([matrix[span(row), :] for row in rows], 0)
+
+
+def block_columns(matrix, cols):
+    return jnp.concatenate([matrix[:, span(col)] for col in cols], 1)
+
+
+def blocks_of(strip, rows, cols):
+    for i, row in enumerate(rows):
+        for j, col in enumerate(cols):
+            yield row, col, strip[i * SIDE : (i + 1) * SIDE, j * SIDE : (j + 1) * SIDE]
+
+
+def product_blocks(left, right):
+    for rows, cols in STRIPS:
+        high, low = block_rows(left[0], rows), block_rows(left[1], rows)
+        right_high, right_low = block_columns(right[0], cols), block_columns(right[1], cols)
+        both = dot(jnp.concatenate([high, low], 0), right_high)
+        count = high.shape[0]
+        yield from blocks_of(both[:count] + both[count:] + dot(high, right_low), rows, cols)
+
+
+def square_blocks(high, low, mixed):
+    for first in range(0, high.shape[0] // SIDE, 2):
+        mixed[:, span(first, 2)] = dot(high[...], low[:, span(first, 2)])
+    for rows, cols in STRIPS:
+        strip = dot(block_rows(high, rows), block_columns(high, cols))
+        for row, col, block in blocks_of(strip, rows, cols):
+            yield row, col, block + (mixed[span(row), span(col)] + turned(mixed[span(col), span(row)]))
 
 
 def store_split(target, slot, rows, columns, value, mirror):
@@ -95,9 +109,6 @@
     return lax.broadcasted_iota(jnp.int32, shape, 0)
 
 
-TILE_BLOCKS = ((0, 1, None, 4), (2, 3, 5, 6), (7, 8, None, 9))
-
-
 def pack(block):
     shape = (HALF, SIDE)
     lower = pltpu.roll(block[HALF:, :], HALF, 1)
@@ -168,11 +179,11 @@
     even = lax.axis_index("col") % 2 == 0
 
     def read(first, count):
-        span = pl.ds(first, count)
-        partner = from_rows[0][slot, span, :]
+        part = pl.ds(first, count)
+        partner = from_rows[0][slot, part, :]
         for place in range(1, len(from_rows)):
-            partner = jnp.where(bit == float(1 << place), from_rows[place][slot, span, :], partner)
-        near, far = from_even[slot, span, :], from_odd[slot, span, :]
+            partner = jnp.where(bit == float(1 << place), from_rows[place][slot, part, :], partner)
+        near, far = from_even[slot, part, :], from_odd[slot, part, :]
         return jnp.where(even, far, near), jnp.where(even, near, far), partner
 
     faces = read(0, SIDE)
@@ -204,9 +215,9 @@
         store_arrow((s_high, s_low), slot, parts)
     for slot in range(slots):
         total = None
-        for _, _, _, off, tile in square_tiles(s_high.at[slot], s_low.at[slot], mixed.at[slot]):
-            part = jnp.sum(tile * tile, axis=0, keepdims=True)
-            part = 2.0 * part if off else part
+        for row, col, block in square_blocks(s_high.at[slot], s_low.at[slot], mixed.at[slot]):
+            part = jnp.sum(block * block, axis=0, keepdims=True)
+            part = part if row == col else 2.0 * part
             total = part if total is None else total + part
         total = jnp.sum(total, axis=1, keepdims=True)
         top = total if top is None else jnp.maximum(top, total)
@@ -221,17 +232,13 @@
         for place, part in enumerate(parts):
             out[slot, place] = part
     for slot in range(slots):
-        for _, rows, columns, off, tile in square_tiles(s_high.at[slot], s_low.at[slot], mixed.at[slot]):
-            store_split((q_high, q_low), slot, rows, columns, tile, off)
+        for row, col, block in square_blocks(s_high.at[slot], s_low.at[slot], mixed.at[slot]):
+            store_split((q_high, q_low), slot, span(row), span(col), block, row != col)
     for slot in range(slots):
         matrix = (s_high.at[slot], s_low.at[slot])
         square = (q_high.at[slot], q_low.at[slot])
-        for place, rows, columns, _ in upper_tiles(s_high.shape[1]):
-            tile = product(matrix, square, rows, columns)
-            for inner, at in enumerate(TILE_BLOCKS[place]):
-                if at is not None:
-                    row, col = inner // 2 * SIDE, inner % 2 * SIDE
-                    out[slot, count + at] = tile[row : row + SIDE, col : col + SIDE]
+        for place, (_, _, block) in enumerate(product_blocks(matrix, square)):
+            out[slot, count + place] = block
 
 
 def schedule(square, advance, slots, repeats):
@@ -252,34 +259,32 @@
     linear = 1.5 * scaling
     cubic = -0.5 * (scaling * scaling * scaling)
     for slot in range(slots):
-        at = 2 * members - 1
-        for row in range(members):
-            for col in range(row, members):
-                value = cubic * source[slot, at]
-                if row == col:
-                    value = value + linear * source[slot, members - 1 + row if row else 0]
-                elif row == 0:
-                    value = value + linear * turned(source[slot, col])
-                spans = (pl.ds(row * SIDE, SIDE), pl.ds(col * SIDE, SIDE))
-                x[(slot, *spans)] = value
-                if row // 2 == col // 2 and row != col:
-                    x[(slot, *spans[::-1])] = turned(value)
-                store_split((xh.at[0], xl.at[0]), slot, *spans, value, row != col)
-                at += 1
+        for place, (row, col) in enumerate(PLACES):
+            value = source[slot, 2 * members - 1 + place]
+            value = cubic * (symmetric(value) if row == col else value)
+            if row == col:
+                value = value + linear * source[slot, members - 1 + row if row else 0]
+            elif col == 0:
+                value = value + linear * source[slot, row]
+            elif row == 0:
+                value = value + linear * turned(source[slot, col])
+            x[slot, span(row), span(col)] = value
+            store_split((xh.at[0], xl.at[0]), slot, span(row), span(col), value, row != col)
+
     def square(slot, repeat):
         iterate = (xh.at[repeat % 2, slot], xl.at[repeat % 2, slot])
-        for _, rows, columns, off, tile in square_tiles(*iterate, mixed.at[slot]):
-            store_split((yh, yl), slot, rows, columns, tile, off)
+        for row, col, block in square_blocks(*iterate, mixed.at[slot]):
+            store_split((yh, yl), slot, span(row), span(col), block, row != col)
             yield
 
     def advance(slot, repeat):
         iterate = (xh.at[repeat % 2, slot], xl.at[repeat % 2, slot])
         target = (xh.at[1 - repeat % 2], xl.at[1 - repeat % 2])
-        for _, rows, columns, off in upper_tiles(order):
-            tile = product(iterate, (yh.at[slot], yl.at[slot]), rows, columns)
-            value = 1.5 * x[slot, rows, columns] - 0.5 * tile
-            x[slot, rows, columns] = value
-            store_split(target, slot, rows, columns, value, off)
+        for row, col, block in product_blocks(iterate, (yh.at[slot], yl.at[slot])):
+            at = (slot, span(row), span(col))
+            value = 1.5 * x[at] - 0.5 * (symmetric(block) if row == col else block)
+            x[at] = value
+            store_split(target, *at, value, row != col)
             yield
 
     schedule(square, advance, slots, ITERS - 2)
@@ -295,8 +300,10 @@
     square = (SIDE, SIDE)
     eye = jnp.where(lanes(square) == rows_of(square), 0.5, 0.0)
     for slot in range(slots):
-        central = 0.25 * outer[slot] - 0.75 * x[slot, first, :]
-        parts = [turned(central[:, k * SIDE : (k + 1) * SIDE]) for k in range(members)]
+        parts = []
+        for k in range(members):
+            stored = x[slot, first, span(k)] if (0, k) in PLACES else turned(x[slot, span(k), first])
+            parts.append(turned(0.25 * outer[slot][:, k * SIDE : (k + 1) * SIDE] - 0.75 * stored))
         parts[0] = symmetric(parts[0]) + eye
         fill_all(targets, slot, parts[1:], None if last else pack(parts[0]))
         own[slot, 0] = parts[0]
@@ -366,7 +373,7 @@
     arrow = 2 * members - 1
     part_scratch = pltpu.VMEM((slots, order, order), bf16)
     both_scratch = pltpu.VMEM((2, slots, order, order), bf16)
-    mixed_scratch = pltpu.VMEM((slots, 4, order // 2, order // 2), f32)
+    mixed_scratch = pltpu.VMEM((slots, order, order), f32)
     multiply = slots * 3 * 3 * order * order * order // 2
 
     half, *sent = call(pack_kernel, "pack", [hamiltonian], [own] + [full] * 3)
@@ -394,7 +401,7 @@
             cube_kernel,
             "cube",
             [blocks],
-            [shape(slots, arrow + members * (members + 1) // 2, SIDE, SIDE)],
+            [shape(slots, arrow + len(PLACES), SIDE, SIDE)],
             [part_scratch] * 4 + [mixed_scratch],
             flops=2 * multiply,
         )

time: 82.4 us -> 80.2 us (0.973)
  Pallas kernels: 32.5 us -> 29.8 us
    pallas_call x9, Pallas kernels: 32.5 us -> 29.8 us  [call(): pl.pallas_call(kernel, out_shape=list(outputs), in_specs=specs, out_specs...]
  transfers between devices with their start and end apart: 14 -> 14, of which waited for: 7 -> 7; matrix products, arithmetic and copies ran while one was open for 1% -> 1% of each run, Pallas kernels for 8% -> 7%
where the time goes in v6:
time: 80.2 us; the launch traced here: 79.9 us
  Pallas kernels  29.8 us (37%)
  waiting for transfers between devices  26.6 us (33%)
  starting transfers between devices  21.7 us (27%)
  local copies, waits for them, and re-layouts  1.81 us (2%)
    pallas_call x9, Pallas kernels, call(): pl.pallas_call(kernel, out_shape=list(outputs), in_specs=specs, out_specs...  29.8 us
    ppermute x3, waiting for transfers between devices, exchange(): received = [lax.ppermute(over_even, 'col', [(i, i ^ 1) for i in cols])]  14.7 us
    all_to_all x2, waiting for transfers between devices, per_device(): norms = lax.all_to_all(norms, ('row', 'col'), 0, 0, tiled=True)  9.44 us
    all_to_all x2, starting transfers between devices, per_device(): norms = lax.all_to_all(norms, ('row', 'col'), 0, 0, tiled=True)  8.3 us
    ppermute x3, starting transfers between devices, exchange(): received.append(lax.ppermute(over_odd, 'col', odd))  6.31 us
    ppermute x3, starting transfers between devices, exchange(): received = [lax.ppermute(over_even, 'col', [(i, i ^ 1) for i in cols])]  4.39 us
    ppermute x6, starting transfers between devices, exchange(): lax.ppermute(to_partner, 'row', [(i, i ^ place) for i in rows])  2.72 us
    ppermute x3, waiting for transfers between devices, exchange(): received.append(lax.ppermute(over_odd, 'col', odd))  2.11 us
  transfers between devices with their start and end apart: 14, of which 7 were waited for; matrix products, arithmetic and copies ran while one was open for 1% of the time, Pallas kernels for 7%

profile of v6, /device:TPU:0, one launch (start us, length us, event | category | flops | bytes accessed | tf_op | source)
XLA Modules:
  0.0 79.9 jit_solution(15349572947938764213)
XLA Ops:
  0.0 1.0 %copy-done = f32[2,4,128,128]{3,2,1,0:T(8,128)S(1)} copy-done((f32[2,4,128,128]{3,2,1,0:T(8,128)S(1)}, f32[2,4,128,128]{3,2,1,0:T(8,128)}, u32[]{:S(2)}) %copy-start) | copy-done | bytes 524312
  1.0 0.2 pack.1
  1.2 3.0 %collective-permute-start = (f32[2,200,128]{2,1,0:T(8,128)S(1)}, f32[2,200,128]{2,1,0:T(8,128)S(1)}, u32[]{:S(2)}, u32[]{:S(2)}) collective-permute-start(f32[2,200,128]{2,1,0:T(8,128)S(1)} %get-tuple-element.22), channel_id=1, source_target_pairs={{0,1},{1,0},{2,3},{3,2},{4,5},{5,4},{6,7},{7,6},{8,9},{9,8},{10,11... | collective-permute-start | bytes 614408 | tf_op jit(solution)/shard_map/ppermute | solution.py:331
  4.3 3.5 %collective-permute-start.1 = (f32[2,200,128]{2,1,0:T(8,128)S(1)}, f32[2,200,128]{2,1,0:T(8,128)S(1)}, u32[]{:S(2)}, u32[]{:S(2)}) collective-permute-start(f32[2,200,128]{2,1,0:T(8,128)S(1)} %get-tuple-element.23), channel_id=1, source_target_pairs={{0,7},{1,2},{2,1},{3,4},{4,3},{5,6},{6,5},{7,0},{8,15},{9,10},{10,... | collective-permute-start | bytes 614408 | tf_op jit(solution)/shard_map/ppermute | solution.py:332
  7.8 1.5 %collective-permute-start.3 = (f32[2,200,128]{2,1,0:T(8,128)S(1)}, f32[2,200,128]{2,1,0:T(8,128)S(1)}, u32[]{:S(2)}, u32[]{:S(2)}) collective-permute-start(f32[2,200,128]{2,1,0:T(8,128)S(1)} %get-tuple-element.24), channel_id=1, source_target_pairs={{0,16},{8,24},{16,0},{24,8},{1,17},{9,25},{17,1},{25,9},{2,18},{10... | collective-permute-start | bytes 614408 | tf_op jit(solution)/shard_map/ppermute | solution.py:335
  9.3 0.0 collective-permute-start.2
  9.3 0.8 copy.3.lists
  10.1 1.1 %links.1.refs_0_ = f32[10,128]{1,0:T(8,128)S(1)} custom-call(s32[64,4]{1,0:T(8,128)S(1)} %copy.3.lists), custom_call_target="tpu_custom_call" | custom-call | bytes 6144 | tf_op jit(solution)/shard_map/links/pallas_call | solution.py:353
  11.2 2.5 %collective-permute-done.refs_2_ = f32[2,200,128]{2,1,0:T(8,128)S(1)} collective-permute-done((f32[2,200,128]{2,1,0:T(8,128)S(1)}, f32[2,200,128]{2,1,0:T(8,128)S(1)}, u32[]{:S(2)}, u32[]{:S(2)}) %collective-permute-start) | collective-permute-done | bytes 204832 | tf_op jit(solution)/shard_map/ppermute | solution.py:331
  13.7 0.3 collective-permute-done.3.refs_5_
  14.1 2.1 %assemble.2 = (f32[32,1,128]{2,1,0:T(1,128)}, f32[2,7,128,128]{3,2,1,0:T(8,128)S(1)}) custom-call(f32[10,128]{1,0:T(8,128)S(1)} %links.1.refs_0_, f32[2,4,128,128]{3,2,1,0:T(8,128)S(1)} %get-tuple-element.21.refs_1_, f32[2,200,128]{2,1,0:T(8,128)S(1)} %collective-permute-done.refs_2_, f32[2,200,128]{2,1,0:T(8,128)S(1)} %collective-permute-done.1.refs_3_, ...), custom_call_target="tpu_custom_call" | custom-call | flops 1207959552 | bytes 2282496 | tf_op jit(solution)/shard_map/assemble/pallas_call | solution.py:353
  16.1 5.8 %all-to-all-start = ((f32[32,1,128]{2,1,0:T(1,128)}), f32[32,1,128]{2,1,0:T(1,128)S(1)}, u32[]{:S(2)}, u32[]{:S(2)}) async-start(f32[32,1,128]{2,1,0:T(1,128)} %get-tuple-element.25), calls=%async_computation | async-start | bytes 32768 | tf_op jit(solution)/shard_map/all_to_all | solution.py:399
  21.9 2.3 %cube.2.source.refs_2_ = f32[2,17,128,128]{3,2,1,0:T(8,128)S(1)} custom-call(f32[2,7,128,128]{3,2,1,0:T(8,128)S(1)} %get-tuple-element.26.blocks), custom_call_target="tpu_custom_call" | custom-call | flops 2415919104 | bytes 3145728 | tf_op jit(solution)/shard_map/cube/pallas_call | solution.py:353
  24.2 4.7 %all-to-all-done.norms = f32[32,1,128]{2,1,0:T(1,128)S(1)} async-done(((f32[32,1,128]{2,1,0:T(1,128)}), f32[32,1,128]{2,1,0:T(1,128)S(1)}, u32[]{:S(2)}, u32[]{:S(2)}) %all-to-all-start) | async-done | bytes 16416 | tf_op jit(solution)/shard_map/all_to_all | solution.py:399
  28.9 9.3 %sign.2 = (f32[2,4,128,128]{3,2,1,0:T(8,128)S(1)}, f32[2,200,128]{2,1,0:T(8,128)S(1)}, f32[2,200,128]{2,1,0:T(8,128)S(1)}, f32[2,200,128]{2,1,0:T(8,128)S(1)}) custom-call(f32[32,1,128]{2,1,0:T(1,128)S(1)} %all-to-all-done.norms, f32[2,17,128,128]{3,2,1,0:T(8,128)S(1)} %cube.2.source.refs_2_), custom_call_target="tpu_custom_call" | custom-call | flops 9663676416 | bytes 3383296 | tf_op jit(solution)/shard_map/sign/pallas_call | solution.py:353
  38.2 0.7 collective-permute-start.4
  38.9 1.4 %collective-permute-start.5 = (f32[2,200,128]{2,1,0:T(8,128)S(1)}, f32[2,200,128]{2,1,0:T(8,128)S(1)}, u32[]{:S(2)}, u32[]{:S(2)}) collective-permute-start(f32[2,200,128]{2,1,0:T(8,128)S(1)} %get-tuple-element.29), channel_id=1, source_target_pairs={{0,7},{1,2},{2,1},{3,4},{4,3},{5,6},{6,5},{7,0},{8,15},{9,10},{10,... | collective-permute-start | bytes 614408 | tf_op jit(solution)/shard_map/ppermute | solution.py:332
  40.3 0.6 collective-permute-start.7
  40.9 0.0 collective-permute-start.6
  40.9 8.6 %collective-permute-done.4.refs_3_ = f32[2,200,128]{2,1,0:T(8,128)S(1)} collective-permute-done((f32[2,200,128]{2,1,0:T(8,128)S(1)}, f32[2,200,128]{2,1,0:T(8,128)S(1)}, u32[]{:S(2)}, u32[]{:S(2)}) %collective-permute-start.4) | collective-permute-done | bytes 204832 | tf_op jit(solution)/shard_map/ppermute | solution.py:331
  49.5 0.0 collective-permute-done.5.refs_4_
  49.5 2.3 %assemble.3 = (f32[32,1,128]{2,1,0:T(1,128)}, f32[2,7,128,128]{3,2,1,0:T(8,128)S(1)}) custom-call(f32[10,128]{1,0:T(8,128)S(1)} %links.1.refs_0_, f32[2,4,128,128]{3,2,1,0:T(8,128)S(1)} %get-tuple-element.27.refs_1_, f32[2,17,128,128]{3,2,1,0:T(8,128)S(1)} %cube.2.source.refs_2_, f32[2,200,128]{2,1,0:T(8,128)S(1)} %collective-permute-done.4.refs_3_, ...), custom_call_target="tpu_custom_call" | custom-call | flops 1207959552 | bytes 4510720 | tf_op jit(solution)/shard_map/assemble/pallas_call | solution.py:353
  51.8 2.5 %all-to-all-start.1 = ((f32[32,1,128]{2,1,0:T(1,128)}), f32[32,1,128]{2,1,0:T(1,128)S(1)}, u32[]{:S(2)}, u32[]{:S(2)}) async-start(f32[32,1,128]{2,1,0:T(1,128)} %get-tuple-element.31), calls=%async_computation.1 | async-start | bytes 32768 | tf_op jit(solution)/shard_map/all_to_all | solution.py:399
  54.4 2.3 %cube.3.source = f32[2,17,128,128]{3,2,1,0:T(8,128)S(1)} custom-call(f32[2,7,128,128]{3,2,1,0:T(8,128)S(1)} %get-tuple-element.32.blocks), custom_call_target="tpu_custom_call" | custom-call | flops 2415919104 | bytes 3145728 | tf_op jit(solution)/shard_map/cube/pallas_call | solution.py:353
  56.7 4.7 %all-to-all-done.1.norms = f32[32,1,128]{2,1,0:T(1,128)S(1)} async-done(((f32[32,1,128]{2,1,0:T(1,128)}), f32[32,1,128]{2,1,0:T(1,128)S(1)}, u32[]{:S(2)}, u32[]{:S(2)}) %all-to-all-start.1) | async-done | bytes 16416 | tf_op jit(solution)/shard_map/all_to_all | solution.py:399
  61.4 9.2 %sign.3 = (f32[2,4,128,128]{3,2,1,0:T(8,128)S(1)}, f32[2,128,128]{2,1,0:T(8,128)S(1)}, f32[2,128,128]{2,1,0:T(8,128)S(1)}, f32[2,128,128]{2,1,0:T(8,128)S(1)}) custom-call(f32[32,1,128]{2,1,0:T(1,128)S(1)} %all-to-all-done.1.norms, f32[2,17,128,128]{3,2,1,0:T(8,128)S(1)} %cube.3.source), custom_call_target="tpu_custom_call" | custom-call | flops 9663676416 | bytes 3162112 | tf_op jit(solution)/shard_map/sign/pallas_call | solution.py:353
  70.6 0.7 collective-permute-start.8
  71.3 1.4 %collective-permute-start.9 = (f32[2,128,128]{2,1,0:T(8,128)S(1)}, f32[2,128,128]{2,1,0:T(8,128)S(1)}, u32[]{:S(2)}, u32[]{:S(2)}) collective-permute-start(f32[2,128,128]{2,1,0:T(8,128)S(1)} %get-tuple-element.35), channel_id=1, source_target_pairs={{0,7},{1,2},{2,1},{3,4},{4,3},{5,6},{6,5},{7,0},{8,15},{9,10},{10,... | collective-permute-start | bytes 393224 | tf_op jit(solution)/shard_map/ppermute | solution.py:332
  72.7 0.6 collective-permute-start.11
  73.3 3.6 %collective-permute-done.8.refs_2_ = f32[2,128,128]{2,1,0:T(8,128)S(1)} collective-permute-done((f32[2,128,128]{2,1,0:T(8,128)S(1)}, f32[2,128,128]{2,1,0:T(8,128)S(1)}, u32[]{:S(2)}, u32[]{:S(2)}) %collective-permute-start.8) | collective-permute-done | bytes 131104 | tf_op jit(solution)/shard_map/ppermute | solution.py:331
  76.9 2.1 %collective-permute-done.9.refs_3_ = f32[2,128,128]{2,1,0:T(8,128)S(1)} collective-permute-done((f32[2,128,128]{2,1,0:T(8,128)S(1)}, f32[2,128,128]{2,1,0:T(8,128)S(1)}, u32[]{:S(2)}, u32[]{:S(2)}) %collective-permute-start.9) | collective-permute-done | bytes 131104 | tf_op jit(solution)/shard_map/ppermute | solution.py:332
  79.0 1.0 %density.1 = f32[2,4,128,128]{3,2,1,0:T(8,128)} custom-call(f32[10,128]{1,0:T(8,128)S(1)} %links.1.refs_0_, f32[2,4,128,128]{3,2,1,0:T(8,128)S(1)} %get-tuple-element.33.refs_1_, f32[2,128,128]{2,1,0:T(8,128)S(1)} %collective-permute-done.8.refs_2_, f32[2,128,128]{2,1,0:T(8,128)S(1)} %collective-permute-done.9.refs_3_, ...), custom_call_target="tpu_custom_call" | custom-call | bytes 1577984 | tf_op jit(solution)/shard_map/density/pallas_call | solution.py:353
  (8 shorter events, 0.0 us)
Async XLA Ops:
  0.0 1.0 %copy-start = (f32[2,4,128,128]{3,2,1,0:T(8,128)S(1)}, f32[2,4,128,128]{3,2,1,0:T(8,128)}, u32[]{:S(2)}) copy-start(f32[2,4,128,128]{3,2,1,0:T(8,128)} %own.1) | copy-start | bytes 1572868
  1.2 12.5 %collective-permute-start = (f32[2,200,128]{2,1,0:T(8,128)S(1)}, f32[2,200,128]{2,1,0:T(8,128)S(1)}, u32[]{:S(2)}, u32[]{:S(2)}) collective-permute-start(f32[2,200,128]{2,1,0:T(8,128)S(1)} %get-tuple-element.22), channel_id=1, source_target_pairs={{0,1},{1,0},{2,3},{3,2},{4,5},{5,4},{6,7},{7,6},{8,9},{9,8},{10,11... | collective-permute-start | bytes 614408 | tf_op jit(solution)/shard_map/ppermute | solution.py:331
  4.3 9.5 %collective-permute-start.1 = (f32[2,200,128]{2,1,0:T(8,128)S(1)}, f32[2,200,128]{2,1,0:T(8,128)S(1)}, u32[]{:S(2)}, u32[]{:S(2)}) collective-permute-start(f32[2,200,128]{2,1,0:T(8,128)S(1)} %get-tuple-element.23), channel_id=1, source_target_pairs={{0,7},{1,2},{2,1},{3,4},{4,3},{5,6},{6,5},{7,0},{8,15},{9,10},{10,... | collective-permute-start | bytes 614408 | tf_op jit(solution)/shard_map/ppermute | solution.py:332
  7.8 6.3 %collective-permute-start.3 = (f32[2,200,128]{2,1,0:T(8,128)S(1)}, f32[2,200,128]{2,1,0:T(8,128)S(1)}, u32[]{:S(2)}, u32[]{:S(2)}) collective-permute-start(f32[2,200,128]{2,1,0:T(8,128)S(1)} %get-tuple-element.24), channel_id=1, source_target_pairs={{0,16},{8,24},{16,0},{24,8},{1,17},{9,25},{17,1},{25,9},{2,18},{10... | collective-permute-start | bytes 614408 | tf_op jit(solution)/shard_map/ppermute | solution.py:335
  9.3 4.8 %collective-permute-start.2 = (f32[2,200,128]{2,1,0:T(8,128)S(1)}, f32[2,200,128]{2,1,0:T(8,128)S(1)}, u32[]{:S(2)}, u32[]{:S(2)}) collective-permute-start(f32[2,200,128]{2,1,0:T(8,128)S(1)} %get-tuple-element.24), channel_id=1, source_target_pairs={{0,8},{8,0},{16,24},{24,16},{1,9},{9,1},{17,25},{25,17},{2,10},{10... | collective-permute-start | bytes 614408 | tf_op jit(solution)/shard_map/ppermute | solution.py:335
  16.1 12.8 %all-to-all-start = ((f32[32,1,128]{2,1,0:T(1,128)}), f32[32,1,128]{2,1,0:T(1,128)S(1)}, u32[]{:S(2)}, u32[]{:S(2)}) async-start(f32[32,1,128]{2,1,0:T(1,128)} %get-tuple-element.25), calls=%async_computation | async-start | bytes 32768 | tf_op jit(solution)/shard_map/all_to_all | solution.py:399
  38.2 11.3 %collective-permute-start.4 = (f32[2,200,128]{2,1,0:T(8,128)S(1)}, f32[2,200,128]{2,1,0:T(8,128)S(1)}, u32[]{:S(2)}, u32[]{:S(2)}) collective-permute-start(f32[2,200,128]{2,1,0:T(8,128)S(1)} %get-tuple-element.28), channel_id=1, source_target_pairs={{0,1},{1,0},{2,3},{3,2},{4,5},{5,4},{6,7},{7,6},{8,9},{9,8},{10,11... | collective-permute-start | bytes 614408 | tf_op jit(solution)/shard_map/ppermute | solution.py:331
  38.9 10.6 %collective-permute-start.5 = (f32[2,200,128]{2,1,0:T(8,128)S(1)}, f32[2,200,128]{2,1,0:T(8,128)S(1)}, u32[]{:S(2)}, u32[]{:S(2)}) collective-permute-start(f32[2,200,128]{2,1,0:T(8,128)S(1)} %get-tuple-element.29), channel_id=1, source_target_pairs={{0,7},{1,2},{2,1},{3,4},{4,3},{5,6},{6,5},{7,0},{8,15},{9,10},{10,... | collective-permute-start | bytes 614408 | tf_op jit(solution)/shard_map/ppermute | solution.py:332
  40.3 9.2 %collective-permute-start.7 = (f32[2,200,128]{2,1,0:T(8,128)S(1)}, f32[2,200,128]{2,1,0:T(8,128)S(1)}, u32[]{:S(2)}, u32[]{:S(2)}) collective-permute-start(f32[2,200,128]{2,1,0:T(8,128)S(1)} %get-tuple-element.30), channel_id=1, source_target_pairs={{0,16},{8,24},{16,0},{24,8},{1,17},{9,25},{17,1},{25,9},{2,18},{10... | collective-permute-start | bytes 614408 | tf_op jit(solution)/shard_map/ppermute | solution.py:335
  40.9 8.6 %collective-permute-start.6 = (f32[2,200,128]{2,1,0:T(8,128)S(1)}, f32[2,200,128]{2,1,0:T(8,128)S(1)}, u32[]{:S(2)}, u32[]{:S(2)}) collective-permute-start(f32[2,200,128]{2,1,0:T(8,128)S(1)} %get-tuple-element.30), channel_id=1, source_target_pairs={{0,8},{8,0},{16,24},{24,16},{1,9},{9,1},{17,25},{25,17},{2,10},{10... | collective-permute-start | bytes 614408 | tf_op jit(solution)/shard_map/ppermute | solution.py:335
  51.8 9.6 %all-to-all-start.1 = ((f32[32,1,128]{2,1,0:T(1,128)}), f32[32,1,128]{2,1,0:T(1,128)S(1)}, u32[]{:S(2)}, u32[]{:S(2)}) async-start(f32[32,1,128]{2,1,0:T(1,128)} %get-tuple-element.31), calls=%async_computation.1 | async-start | bytes 32768 | tf_op jit(solution)/shard_map/all_to_all | solution.py:399
  70.6 6.2 %collective-permute-start.8 = (f32[2,128,128]{2,1,0:T(8,128)S(1)}, f32[2,128,128]{2,1,0:T(8,128)S(1)}, u32[]{:S(2)}, u32[]{:S(2)}) collective-permute-start(f32[2,128,128]{2,1,0:T(8,128)S(1)} %get-tuple-element.34), channel_id=1, source_target_pairs={{0,1},{1,0},{2,3},{3,2},{4,5},{5,4},{6,7},{7,6},{8,9},{9,8},{10,11... | collective-permute-start | bytes 393224 | tf_op jit(solution)/shard_map/ppermute | solution.py:331
  71.3 7.7 %collective-permute-start.9 = (f32[2,128,128]{2,1,0:T(8,128)S(1)}, f32[2,128,128]{2,1,0:T(8,128)S(1)}, u32[]{:S(2)}, u32[]{:S(2)}) collective-permute-start(f32[2,128,128]{2,1,0:T(8,128)S(1)} %get-tuple-element.35), channel_id=1, source_target_pairs={{0,7},{1,2},{2,1},{3,4},{4,3},{5,6},{6,5},{7,0},{8,15},{9,10},{10,... | collective-permute-start | bytes 393224 | tf_op jit(solution)/shard_map/ppermute | solution.py:332
  72.7 6.3 %collective-permute-start.11 = (f32[2,128,128]{2,1,0:T(8,128)S(1)}, f32[2,128,128]{2,1,0:T(8,128)S(1)}, u32[]{:S(2)}, u32[]{:S(2)}) collective-permute-start(f32[2,128,128]{2,1,0:T(8,128)S(1)} %get-tuple-element.36), channel_id=1, source_target_pairs={{0,16},{8,24},{16,0},{24,8},{1,17},{9,25},{17,1},{25,9},{2,18},{10... | collective-permute-start | bytes 393224 | tf_op jit(solution)/shard_map/ppermute | solution.py:335
  73.3 5.7 %collective-permute-start.10 = (f32[2,128,128]{2,1,0:T(8,128)S(1)}, f32[2,128,128]{2,1,0:T(8,128)S(1)}, u32[]{:S(2)}, u32[]{:S(2)}) collective-permute-start(f32[2,128,128]{2,1,0:T(8,128)S(1)} %get-tuple-element.36), channel_id=1, source_target_pairs={{0,8},{8,0},{16,24},{24,16},{1,9},{9,1},{17,25},{25,17},{2,10},{10... | collective-permute-start | bytes 393224 | tf_op jit(solution)/shard_map/ppermute | solution.py:335

commit v7 on v6

--- a/solution.py
+++ b/solution.py
@@ -10,7 +10,7 @@
 STEPS = 2
 SIDE = 128
 HALF = SIDE // 2
-PACKED = HALF + 8
+EXTRA = 8
 
 epsilon = 1e-06
 f32 = jnp.float32
@@ -114,8 +114,7 @@
     lower = pltpu.roll(block[HALF:, :], HALF, 1)
     body = jnp.where(lanes(shape) < rows_of(shape), lower, block[:HALF, :])
     whole = block.shape
-    diagonal = jnp.sum(jnp.where(lanes(whole) == rows_of(whole), block, 0.0), 0, keepdims=True)
-    return body, jnp.broadcast_to(diagonal, (PACKED - HALF, SIDE))
+    return body, jnp.sum(jnp.where(lanes(whole) == rows_of(whole), block, 0.0), 0, keepdims=True)
 
 
 def unpack(body, diagonal):
@@ -129,11 +128,21 @@
     return folded + turned(folded)
 
 
+def message_rows(slots, with_diagonals):
+    return slots * (SIDE + HALF) + EXTRA if with_diagonals else slots * SIDE
+
+
 def fill(target, slot, face, packed):
-    target[slot, pl.ds(0, SIDE), :] = face
+    first = slot * (SIDE if packed is None else SIDE + HALF)
+    target[pl.ds(first, SIDE), :] = face
     if packed is not None:
-        target[slot, pl.ds(SIDE, HALF), :] = packed[0]
-        target[slot, pl.ds(SIDE + HALF, PACKED - HALF), :] = packed[1]
+        body, diagonal = packed
+        last = target.shape[0] - EXTRA
+        target[pl.ds(first + SIDE, HALF), :] = body
+        if slot == 0:
+            target[pl.ds(last, EXTRA), :] = jnp.broadcast_to(diagonal, (EXTRA, SIDE))
+        else:
+            target[pl.ds(last + slot, 1), :] = diagonal
 
 
 def fill_all(targets, slot, faces, packed):
@@ -180,18 +189,19 @@
 
     def read(first, count):
         part = pl.ds(first, count)
-        partner = from_rows[0][slot, part, :]
+        partner = from_rows[0][part, :]
         for place in range(1, len(from_rows)):
-            partner = jnp.where(bit == float(1 << place), from_rows[place][slot, part, :], partner)
-        near, far = from_even[slot, part, :], from_odd[slot, part, :]
+            partner = jnp.where(bit == float(1 << place), from_rows[place][part, :], partner)
+        near, far = from_even[part, :], from_odd[part, :]
         return jnp.where(even, far, near), jnp.where(even, near, far), partner
 
-    faces = read(0, SIDE)
+    start = slot * (SIDE + HALF if with_diagonals else SIDE)
+    faces = read(start, SIDE)
     if not with_diagonals:
         return faces, None
-    bodies = read(SIDE, HALF)
-    diagonals = read(SIDE + HALF, PACKED - HALF)
-    return faces, [unpack(b, d[0:1, :]) for b, d in zip(bodies, diagonals)]
+    bodies = read(start + SIDE, HALF)
+    diagonals = read(from_even.shape[0] - EXTRA + slot, 1)
+    return faces, [unpack(body, diagonal) for body, diagonal in zip(bodies, diagonals)]
 
 
 def assemble_kernel(members, has_base, *refs):
@@ -367,8 +377,8 @@
     order = members * SIDE
     cols = lax.axis_size("col")
     devices = lax.axis_size("row") * cols
-    face = shape(slots, SIDE, SIDE)
-    full = shape(slots, SIDE + PACKED, SIDE)
+    face = shape(message_rows(slots, False), SIDE)
+    full = shape(message_rows(slots, True), SIDE)
     own = shape(slots, members, SIDE, SIDE)
     arrow = 2 * members - 1
     part_scratch = pltpu.VMEM((slots, order, order), bf16)

time: 80.2 us -> 79.9 us (level)
  no operation moved by 1% of the time
where the time goes in v7:
time: 79.9 us; the launch traced here: 79.7 us
  Pallas kernels  29.8 us (37%)
  waiting for transfers between devices  26.3 us (33%)
  starting transfers between devices  21.6 us (27%)
  local copies, waits for them, and re-layouts  1.81 us (2%)
    pallas_call x9, Pallas kernels, call(): pl.pallas_call(kernel, out_shape=list(outputs), in_specs=specs, out_specs...  29.8 us
    ppermute x3, waiting for transfers between devices, exchange(): received = [lax.ppermute(over_even, 'col', [(i, i ^ 1) for i in cols])]  14.3 us
    all_to_all x2, waiting for transfers between devices, per_device(): norms = lax.all_to_all(norms, ('row', 'col'), 0, 0, tiled=True)  9.44 us
    all_to_all x2, starting transfers between devices, per_device(): norms = lax.all_to_all(norms, ('row', 'col'), 0, 0, tiled=True)  8.21 us
    ppermute x3, starting transfers between devices, exchange(): received.append(lax.ppermute(over_odd, 'col', odd))  6.31 us
    ppermute x3, starting transfers between devices, exchange(): received = [lax.ppermute(over_even, 'col', [(i, i ^ 1) for i in cols])]  4.4 us
    ppermute x6, starting transfers between devices, exchange(): lax.ppermute(to_partner, 'row', [(i, i ^ place) for i in rows])  2.72 us
    ppermute x3, waiting for transfers between devices, exchange(): received.append(lax.ppermute(over_odd, 'col', odd))  2.11 us
  transfers between devices with their start and end apart: 14, of which 7 were waited for; matrix products, arithmetic and copies ran while one was open for 1% of the time, Pallas kernels for 7%

profile of v7, /device:TPU:0, one launch (start us, length us, event | category | flops | bytes accessed | tf_op | source)
XLA Modules:
  0.0 79.7 jit_solution(2860125380098341705)
XLA Ops:
  0.0 1.0 %copy-done = f32[2,4,128,128]{3,2,1,0:T(8,128)S(1)} copy-done((f32[2,4,128,128]{3,2,1,0:T(8,128)S(1)}, f32[2,4,128,128]{3,2,1,0:T(8,128)}, u32[]{:S(2)}) %copy-start) | copy-done | bytes 524312
  1.0 0.2 pack.1
  1.2 3.0 %collective-permute-start = (f32[392,128]{1,0:T(8,128)S(1)}, f32[392,128]{1,0:T(8,128)S(1)}, u32[]{:S(2)}, u32[]{:S(2)}) collective-permute-start(f32[392,128]{1,0:T(8,128)S(1)} %get-tuple-element.22), channel_id=1, source_target_pairs={{0,1},{1,0},{2,3},{3,2},{4,5},{5,4},{6,7},{7,6},{8,9},{9,8},{10,11... | collective-permute-start | bytes 602120 | tf_op jit(solution)/shard_map/ppermute | solution.py:341
  4.3 3.5 %collective-permute-start.1 = (f32[392,128]{1,0:T(8,128)S(1)}, f32[392,128]{1,0:T(8,128)S(1)}, u32[]{:S(2)}, u32[]{:S(2)}) collective-permute-start(f32[392,128]{1,0:T(8,128)S(1)} %get-tuple-element.23), channel_id=1, source_target_pairs={{0,7},{1,2},{2,1},{3,4},{4,3},{5,6},{6,5},{7,0},{8,15},{9,10},{10,... | collective-permute-start | bytes 602120 | tf_op jit(solution)/shard_map/ppermute | solution.py:342
  7.8 1.5 %collective-permute-start.3 = (f32[392,128]{1,0:T(8,128)S(1)}, f32[392,128]{1,0:T(8,128)S(1)}, u32[]{:S(2)}, u32[]{:S(2)}) collective-permute-start(f32[392,128]{1,0:T(8,128)S(1)} %get-tuple-element.24), channel_id=1, source_target_pairs={{0,16},{8,24},{16,0},{24,8},{1,17},{9,25},{17,1},{25,9},{2,18},{10... | collective-permute-start | bytes 602120 | tf_op jit(solution)/shard_map/ppermute | solution.py:345
  9.3 0.8 copy.3.lists
  10.1 1.1 %links.1.refs_0_ = f32[10,128]{1,0:T(8,128)S(1)} custom-call(s32[64,4]{1,0:T(8,128)S(1)} %copy.3.lists), custom_call_target="tpu_custom_call" | custom-call | bytes 6144 | tf_op jit(solution)/shard_map/links/pallas_call | solution.py:363
  11.2 2.4 %collective-permute-done.refs_2_ = f32[392,128]{1,0:T(8,128)S(1)} collective-permute-done((f32[392,128]{1,0:T(8,128)S(1)}, f32[392,128]{1,0:T(8,128)S(1)}, u32[]{:S(2)}, u32[]{:S(2)}) %collective-permute-start) | collective-permute-done | bytes 200736 | tf_op jit(solution)/shard_map/ppermute | solution.py:341
  13.5 0.0 collective-permute-done.1.refs_3_
  13.5 0.4 collective-permute-done.3.refs_5_
  14.0 2.1 %assemble.2 = (f32[32,1,128]{2,1,0:T(1,128)}, f32[2,7,128,128]{3,2,1,0:T(8,128)S(1)}) custom-call(f32[10,128]{1,0:T(8,128)S(1)} %links.1.refs_0_, f32[2,4,128,128]{3,2,1,0:T(8,128)S(1)} %get-tuple-element.21.refs_1_, f32[392,128]{1,0:T(8,128)S(1)} %collective-permute-done.refs_2_, f32[392,128]{1,0:T(8,128)S(1)} %collective-permute-done.1.refs_3_, ...), custom_call_target="tpu_custom_call" | custom-call | flops 1207959552 | bytes 2266112 | tf_op jit(solution)/shard_map/assemble/pallas_call | solution.py:363
  16.1 5.7 %all-to-all-start = ((f32[32,1,128]{2,1,0:T(1,128)}), f32[32,1,128]{2,1,0:T(1,128)S(1)}, u32[]{:S(2)}, u32[]{:S(2)}) async-start(f32[32,1,128]{2,1,0:T(1,128)} %get-tuple-element.25), calls=%async_computation | async-start | bytes 32768 | tf_op jit(solution)/shard_map/all_to_all | solution.py:409
  21.7 2.3 %cube.2.source.refs_2_ = f32[2,17,128,128]{3,2,1,0:T(8,128)S(1)} custom-call(f32[2,7,128,128]{3,2,1,0:T(8,128)S(1)} %get-tuple-element.26.blocks), custom_call_target="tpu_custom_call" | custom-call | flops 2415919104 | bytes 3145728 | tf_op jit(solution)/shard_map/cube/pallas_call | solution.py:363
  24.1 4.7 %all-to-all-done.norms = f32[32,1,128]{2,1,0:T(1,128)S(1)} async-done(((f32[32,1,128]{2,1,0:T(1,128)}), f32[32,1,128]{2,1,0:T(1,128)S(1)}, u32[]{:S(2)}, u32[]{:S(2)}) %all-to-all-start) | async-done | bytes 16416 | tf_op jit(solution)/shard_map/all_to_all | solution.py:409
  28.8 9.3 %sign.2 = (f32[2,4,128,128]{3,2,1,0:T(8,128)S(1)}, f32[392,128]{1,0:T(8,128)S(1)}, f32[392,128]{1,0:T(8,128)S(1)}, f32[392,128]{1,0:T(8,128)S(1)}) custom-call(f32[32,1,128]{2,1,0:T(1,128)S(1)} %all-to-all-done.norms, f32[2,17,128,128]{3,2,1,0:T(8,128)S(1)} %cube.2.source.refs_2_), custom_call_target="tpu_custom_call" | custom-call | flops 9663676416 | bytes 3371008 | tf_op jit(solution)/shard_map/sign/pallas_call | solution.py:363
  38.1 0.7 collective-permute-start.4
  38.7 1.4 %collective-permute-start.5 = (f32[392,128]{1,0:T(8,128)S(1)}, f32[392,128]{1,0:T(8,128)S(1)}, u32[]{:S(2)}, u32[]{:S(2)}) collective-permute-start(f32[392,128]{1,0:T(8,128)S(1)} %get-tuple-element.29), channel_id=1, source_target_pairs={{0,7},{1,2},{2,1},{3,4},{4,3},{5,6},{6,5},{7,0},{8,15},{9,10},{10,... | collective-permute-start | bytes 602120 | tf_op jit(solution)/shard_map/ppermute | solution.py:342
  40.1 0.6 collective-permute-start.7
  40.7 0.0 collective-permute-start.6
  40.7 8.4 %collective-permute-done.4.refs_3_ = f32[392,128]{1,0:T(8,128)S(1)} collective-permute-done((f32[392,128]{1,0:T(8,128)S(1)}, f32[392,128]{1,0:T(8,128)S(1)}, u32[]{:S(2)}, u32[]{:S(2)}) %collective-permute-start.4) | collective-permute-done | bytes 200736 | tf_op jit(solution)/shard_map/ppermute | solution.py:341
  49.2 0.0 collective-permute-done.5.refs_4_
  49.2 2.3 %assemble.3 = (f32[32,1,128]{2,1,0:T(1,128)}, f32[2,7,128,128]{3,2,1,0:T(8,128)S(1)}) custom-call(f32[10,128]{1,0:T(8,128)S(1)} %links.1.refs_0_, f32[2,4,128,128]{3,2,1,0:T(8,128)S(1)} %get-tuple-element.27.refs_1_, f32[2,17,128,128]{3,2,1,0:T(8,128)S(1)} %cube.2.source.refs_2_, f32[392,128]{1,0:T(8,128)S(1)} %collective-permute-done.4.refs_3_, ...), custom_call_target="tpu_custom_call" | custom-call | flops 1207959552 | bytes 4494336 | tf_op jit(solution)/shard_map/assemble/pallas_call | solution.py:363
  51.5 2.5 %all-to-all-start.1 = ((f32[32,1,128]{2,1,0:T(1,128)}), f32[32,1,128]{2,1,0:T(1,128)S(1)}, u32[]{:S(2)}, u32[]{:S(2)}) async-start(f32[32,1,128]{2,1,0:T(1,128)} %get-tuple-element.31), calls=%async_computation.1 | async-start | bytes 32768 | tf_op jit(solution)/shard_map/all_to_all | solution.py:409
  54.1 2.3 %cube.3.source = f32[2,17,128,128]{3,2,1,0:T(8,128)S(1)} custom-call(f32[2,7,128,128]{3,2,1,0:T(8,128)S(1)} %get-tuple-element.32.blocks), custom_call_target="tpu_custom_call" | custom-call | flops 2415919104 | bytes 3145728 | tf_op jit(solution)/shard_map/cube/pallas_call | solution.py:363
  56.4 4.7 %all-to-all-done.1.norms = f32[32,1,128]{2,1,0:T(1,128)S(1)} async-done(((f32[32,1,128]{2,1,0:T(1,128)}), f32[32,1,128]{2,1,0:T(1,128)S(1)}, u32[]{:S(2)}, u32[]{:S(2)}) %all-to-all-start.1) | async-done | bytes 16416 | tf_op jit(solution)/shard_map/all_to_all | solution.py:409
  61.1 9.2 %sign.3 = (f32[2,4,128,128]{3,2,1,0:T(8,128)S(1)}, f32[256,128]{1,0:T(8,128)S(1)}, f32[256,128]{1,0:T(8,128)S(1)}, f32[256,128]{1,0:T(8,128)S(1)}) custom-call(f32[32,1,128]{2,1,0:T(1,128)S(1)} %all-to-all-done.1.norms, f32[2,17,128,128]{3,2,1,0:T(8,128)S(1)} %cube.3.source), custom_call_target="tpu_custom_call" | custom-call | flops 9663676416 | bytes 3162112 | tf_op jit(solution)/shard_map/sign/pallas_call | solution.py:363
  70.3 0.7 collective-permute-start.8
  71.0 1.4 %collective-permute-start.9 = (f32[256,128]{1,0:T(8,128)S(1)}, f32[256,128]{1,0:T(8,128)S(1)}, u32[]{:S(2)}, u32[]{:S(2)}) collective-permute-start(f32[256,128]{1,0:T(8,128)S(1)} %get-tuple-element.35), channel_id=1, source_target_pairs={{0,7},{1,2},{2,1},{3,4},{4,3},{5,6},{6,5},{7,0},{8,15},{9,10},{10,... | collective-permute-start | bytes 393224 | tf_op jit(solution)/shard_map/ppermute | solution.py:342
  72.4 0.6 collective-permute-start.11
  73.0 3.6 %collective-permute-done.8.refs_2_ = f32[256,128]{1,0:T(8,128)S(1)} collective-permute-done((f32[256,128]{1,0:T(8,128)S(1)}, f32[256,128]{1,0:T(8,128)S(1)}, u32[]{:S(2)}, u32[]{:S(2)}) %collective-permute-start.8) | collective-permute-done | bytes 131104 | tf_op jit(solution)/shard_map/ppermute | solution.py:341
  76.6 2.1 %collective-permute-done.9.refs_3_ = f32[256,128]{1,0:T(8,128)S(1)} collective-permute-done((f32[256,128]{1,0:T(8,128)S(1)}, f32[256,128]{1,0:T(8,128)S(1)}, u32[]{:S(2)}, u32[]{:S(2)}) %collective-permute-start.9) | collective-permute-done | bytes 131104 | tf_op jit(solution)/shard_map/ppermute | solution.py:342
  78.7 1.0 %density.1 = f32[2,4,128,128]{3,2,1,0:T(8,128)} custom-call(f32[10,128]{1,0:T(8,128)S(1)} %links.1.refs_0_, f32[2,4,128,128]{3,2,1,0:T(8,128)S(1)} %get-tuple-element.33.refs_1_, f32[256,128]{1,0:T(8,128)S(1)} %collective-permute-done.8.refs_2_, f32[256,128]{1,0:T(8,128)S(1)} %collective-permute-done.9.refs_3_, ...), custom_call_target="tpu_custom_call" | custom-call | bytes 1577984 | tf_op jit(solution)/shard_map/density/pallas_call | solution.py:363
  (8 shorter events, 0.0 us)
Async XLA Ops:
  0.0 1.0 %copy-start = (f32[2,4,128,128]{3,2,1,0:T(8,128)S(1)}, f32[2,4,128,128]{3,2,1,0:T(8,128)}, u32[]{:S(2)}) copy-start(f32[2,4,128,128]{3,2,1,0:T(8,128)} %own.1) | copy-start | bytes 1572868
  1.2 12.3 %collective-permute-start = (f32[392,128]{1,0:T(8,128)S(1)}, f32[392,128]{1,0:T(8,128)S(1)}, u32[]{:S(2)}, u32[]{:S(2)}) collective-permute-start(f32[392,128]{1,0:T(8,128)S(1)} %get-tuple-element.22), channel_id=1, source_target_pairs={{0,1},{1,0},{2,3},{3,2},{4,5},{5,4},{6,7},{7,6},{8,9},{9,8},{10,11... | collective-permute-start | bytes 602120 | tf_op jit(solution)/shard_map/ppermute | solution.py:341
  4.3 9.3 %collective-permute-start.1 = (f32[392,128]{1,0:T(8,128)S(1)}, f32[392,128]{1,0:T(8,128)S(1)}, u32[]{:S(2)}, u32[]{:S(2)}) collective-permute-start(f32[392,128]{1,0:T(8,128)S(1)} %get-tuple-element.23), channel_id=1, source_target_pairs={{0,7},{1,2},{2,1},{3,4},{4,3},{5,6},{6,5},{7,0},{8,15},{9,10},{10,... | collective-permute-start | bytes 602120 | tf_op jit(solution)/shard_map/ppermute | solution.py:342
  7.8 6.2 %collective-permute-start.3 = (f32[392,128]{1,0:T(8,128)S(1)}, f32[392,128]{1,0:T(8,128)S(1)}, u32[]{:S(2)}, u32[]{:S(2)}) collective-permute-start(f32[392,128]{1,0:T(8,128)S(1)} %get-tuple-element.24), channel_id=1, source_target_pairs={{0,16},{8,24},{16,0},{24,8},{1,17},{9,25},{17,1},{25,9},{2,18},{10... | collective-permute-start | bytes 602120 | tf_op jit(solution)/shard_map/ppermute | solution.py:345
  9.3 4.7 %collective-permute-start.2 = (f32[392,128]{1,0:T(8,128)S(1)}, f32[392,128]{1,0:T(8,128)S(1)}, u32[]{:S(2)}, u32[]{:S(2)}) collective-permute-start(f32[392,128]{1,0:T(8,128)S(1)} %get-tuple-element.24), channel_id=1, source_target_pairs={{0,8},{8,0},{16,24},{24,16},{1,9},{9,1},{17,25},{25,17},{2,10},{10... | collective-permute-start | bytes 602120 | tf_op jit(solution)/shard_map/ppermute | solution.py:345
  16.1 12.7 %all-to-all-start = ((f32[32,1,128]{2,1,0:T(1,128)}), f32[32,1,128]{2,1,0:T(1,128)S(1)}, u32[]{:S(2)}, u32[]{:S(2)}) async-start(f32[32,1,128]{2,1,0:T(1,128)} %get-tuple-element.25), calls=%async_computation | async-start | bytes 32768 | tf_op jit(solution)/shard_map/all_to_all | solution.py:409
  38.1 11.1 %collective-permute-start.4 = (f32[392,128]{1,0:T(8,128)S(1)}, f32[392,128]{1,0:T(8,128)S(1)}, u32[]{:S(2)}, u32[]{:S(2)}) collective-permute-start(f32[392,128]{1,0:T(8,128)S(1)} %get-tuple-element.28), channel_id=1, source_target_pairs={{0,1},{1,0},{2,3},{3,2},{4,5},{5,4},{6,7},{7,6},{8,9},{9,8},{10,11... | collective-permute-start | bytes 602120 | tf_op jit(solution)/shard_map/ppermute | solution.py:341
  38.7 10.4 %collective-permute-start.5 = (f32[392,128]{1,0:T(8,128)S(1)}, f32[392,128]{1,0:T(8,128)S(1)}, u32[]{:S(2)}, u32[]{:S(2)}) collective-permute-start(f32[392,128]{1,0:T(8,128)S(1)} %get-tuple-element.29), channel_id=1, source_target_pairs={{0,7},{1,2},{2,1},{3,4},{4,3},{5,6},{6,5},{7,0},{8,15},{9,10},{10,... | collective-permute-start | bytes 602120 | tf_op jit(solution)/shard_map/ppermute | solution.py:342
  40.1 9.0 %collective-permute-start.7 = (f32[392,128]{1,0:T(8,128)S(1)}, f32[392,128]{1,0:T(8,128)S(1)}, u32[]{:S(2)}, u32[]{:S(2)}) collective-permute-start(f32[392,128]{1,0:T(8,128)S(1)} %get-tuple-element.30), channel_id=1, source_target_pairs={{0,16},{8,24},{16,0},{24,8},{1,17},{9,25},{17,1},{25,9},{2,18},{10... | collective-permute-start | bytes 602120 | tf_op jit(solution)/shard_map/ppermute | solution.py:345
  40.7 8.4 %collective-permute-start.6 = (f32[392,128]{1,0:T(8,128)S(1)}, f32[392,128]{1,0:T(8,128)S(1)}, u32[]{:S(2)}, u32[]{:S(2)}) collective-permute-start(f32[392,128]{1,0:T(8,128)S(1)} %get-tuple-element.30), channel_id=1, source_target_pairs={{0,8},{8,0},{16,24},{24,16},{1,9},{9,1},{17,25},{25,17},{2,10},{10... | collective-permute-start | bytes 602120 | tf_op jit(solution)/shard_map/ppermute | solution.py:345
  51.5 9.6 %all-to-all-start.1 = ((f32[32,1,128]{2,1,0:T(1,128)}), f32[32,1,128]{2,1,0:T(1,128)S(1)}, u32[]{:S(2)}, u32[]{:S(2)}) async-start(f32[32,1,128]{2,1,0:T(1,128)} %get-tuple-element.31), calls=%async_computation.1 | async-start | bytes 32768 | tf_op jit(solution)/shard_map/all_to_all | solution.py:409
  70.3 6.2 %collective-permute-start.8 = (f32[256,128]{1,0:T(8,128)S(1)}, f32[256,128]{1,0:T(8,128)S(1)}, u32[]{:S(2)}, u32[]{:S(2)}) collective-permute-start(f32[256,128]{1,0:T(8,128)S(1)} %get-tuple-element.34), channel_id=1, source_target_pairs={{0,1},{1,0},{2,3},{3,2},{4,5},{5,4},{6,7},{7,6},{8,9},{9,8},{10,11... | collective-permute-start | bytes 393224 | tf_op jit(solution)/shard_map/ppermute | solution.py:341
  71.0 7.7 %collective-permute-start.9 = (f32[256,128]{1,0:T(8,128)S(1)}, f32[256,128]{1,0:T(8,128)S(1)}, u32[]{:S(2)}, u32[]{:S(2)}) collective-permute-start(f32[256,128]{1,0:T(8,128)S(1)} %get-tuple-element.35), channel_id=1, source_target_pairs={{0,7},{1,2},{2,1},{3,4},{4,3},{5,6},{6,5},{7,0},{8,15},{9,10},{10,... | collective-permute-start | bytes 393224 | tf_op jit(solution)/shard_map/ppermute | solution.py:342
  72.4 6.3 %collective-permute-start.11 = (f32[256,128]{1,0:T(8,128)S(1)}, f32[256,128]{1,0:T(8,128)S(1)}, u32[]{:S(2)}, u32[]{:S(2)}) collective-permute-start(f32[256,128]{1,0:T(8,128)S(1)} %get-tuple-element.36), channel_id=1, source_target_pairs={{0,16},{8,24},{16,0},{24,8},{1,17},{9,25},{17,1},{25,9},{2,18},{10... | collective-permute-start | bytes 393224 | tf_op jit(solution)/shard_map/ppermute | solution.py:345
  73.0 5.7 %collective-permute-start.10 = (f32[256,128]{1,0:T(8,128)S(1)}, f32[256,128]{1,0:T(8,128)S(1)}, u32[]{:S(2)}, u32[]{:S(2)}) collective-permute-start(f32[256,128]{1,0:T(8,128)S(1)} %get-tuple-element.36), channel_id=1, source_target_pairs={{0,8},{8,0},{16,24},{24,16},{1,9},{9,1},{17,25},{25,17},{2,10},{10... | collective-permute-start | bytes 393224 | tf_op jit(solution)/shard_map/ppermute | solution.py:345

commit v8 on v7

--- a/solution.py
+++ b/solution.py
@@ -66,8 +66,7 @@
 
 
 def square_blocks(high, low, mixed):
-    for first in range(0, high.shape[0] // SIDE, 2):
-        mixed[:, span(first, 2)] = dot(high[...], low[:, span(first, 2)])
+    mixed[...] = dot(high[...], low[...])
     for rows, cols in STRIPS:
         strip = dot(block_rows(high, rows), block_columns(high, cols))
         for row, col, block in blocks_of(strip, rows, cols):
@@ -219,7 +218,8 @@
         parts += [present[k] * (half[slot, k] + 0.5 * turned(faces[k - 1])) for k in range(1, members)]
         parts += [present[k] * diagonals[k - 1] for k in range(1, members)]
         if has_base:
-            parts = [part + base[slot, place] for place, part in enumerate(parts)]
+            for place in range(half.shape[1], len(parts)):
+                parts[place] = parts[place] + base[slot, place]
         for place, part in enumerate(parts):
             blocks[slot, place] = part
         store_arrow((s_high, s_low), slot, parts)
@@ -316,9 +316,9 @@
             parts.append(turned(0.25 * outer[slot][:, k * SIDE : (k + 1) * SIDE] - 0.75 * stored))
         parts[0] = symmetric(parts[0]) + eye
         fill_all(targets, slot, parts[1:], None if last else pack(parts[0]))
-        own[slot, 0] = parts[0]
-        for k in range(1, members):
-            own[slot, k] = 0.5 * parts[k]
+        for k in range(members):
+            part = 0.5 * parts[k] if k else parts[0]
+            own[slot, k] = part if last else part + source[slot, k]
 
 
 def density_kernel(members, *refs):

time: 79.9 us -> 79.8 us (level)
  no operation moved by 1% of the time
where the time goes in v8:
time: 79.8 us; the launch traced here: 79.6 us
  Pallas kernels  29.8 us (37%)
  waiting for transfers between devices  26.3 us (33%)
  starting transfers between devices  21.6 us (27%)
  local copies, waits for them, and re-layouts  1.81 us (2%)
    pallas_call x9, Pallas kernels, call(): pl.pallas_call(kernel, out_shape=list(outputs), in_specs=specs, out_specs...  29.8 us
    ppermute x3, waiting for transfers between devices, exchange(): received = [lax.ppermute(over_even, 'col', [(i, i ^ 1) for i in cols])]  14.3 us
    all_to_all x2, waiting for transfers between devices, per_device(): norms = lax.all_to_all(norms, ('row', 'col'), 0, 0, tiled=True)  9.43 us
    all_to_all x2, starting transfers between devices, per_device(): norms = lax.all_to_all(norms, ('row', 'col'), 0, 0, tiled=True)  8.21 us
    ppermute x3, starting transfers between devices, exchange(): received.append(lax.ppermute(over_odd, 'col', odd))  6.31 us
    ppermute x3, starting transfers between devices, exchange(): received = [lax.ppermute(over_even, 'col', [(i, i ^ 1) for i in cols])]  4.39 us
    ppermute x6, starting transfers between devices, exchange(): lax.ppermute(to_partner, 'row', [(i, i ^ place) for i in rows])  2.72 us
    ppermute x3, waiting for transfers between devices, exchange(): received.append(lax.ppermute(over_odd, 'col', odd))  2.11 us
  transfers between devices with their start and end apart: 14, of which 7 were waited for; matrix products, arithmetic and copies ran while one was open for 1% of the time, Pallas kernels for 7%

profile of v8, /device:TPU:0, one launch (start us, length us, event | category | flops | bytes accessed | tf_op | source)
XLA Modules:
  0.0 79.6 jit_solution(4352292239954550495)
XLA Ops:
  0.0 1.0 %copy-done = f32[2,4,128,128]{3,2,1,0:T(8,128)S(1)} copy-done((f32[2,4,128,128]{3,2,1,0:T(8,128)S(1)}, f32[2,4,128,128]{3,2,1,0:T(8,128)}, u32[]{:S(2)}) %copy-start) | copy-done | bytes 524312
  1.0 0.2 pack.1
  1.2 3.0 %collective-permute-start = (f32[392,128]{1,0:T(8,128)S(1)}, f32[392,128]{1,0:T(8,128)S(1)}, u32[]{:S(2)}, u32[]{:S(2)}) collective-permute-start(f32[392,128]{1,0:T(8,128)S(1)} %get-tuple-element.22), channel_id=1, source_target_pairs={{0,1},{1,0},{2,3},{3,2},{4,5},{5,4},{6,7},{7,6},{8,9},{9,8},{10,11... | collective-permute-start | bytes 602120 | tf_op jit(solution)/shard_map/ppermute | solution.py:341
  4.3 3.5 %collective-permute-start.1 = (f32[392,128]{1,0:T(8,128)S(1)}, f32[392,128]{1,0:T(8,128)S(1)}, u32[]{:S(2)}, u32[]{:S(2)}) collective-permute-start(f32[392,128]{1,0:T(8,128)S(1)} %get-tuple-element.23), channel_id=1, source_target_pairs={{0,7},{1,2},{2,1},{3,4},{4,3},{5,6},{6,5},{7,0},{8,15},{9,10},{10,... | collective-permute-start | bytes 602120 | tf_op jit(solution)/shard_map/ppermute | solution.py:342
  7.8 1.5 %collective-permute-start.3 = (f32[392,128]{1,0:T(8,128)S(1)}, f32[392,128]{1,0:T(8,128)S(1)}, u32[]{:S(2)}, u32[]{:S(2)}) collective-permute-start(f32[392,128]{1,0:T(8,128)S(1)} %get-tuple-element.24), channel_id=1, source_target_pairs={{0,16},{8,24},{16,0},{24,8},{1,17},{9,25},{17,1},{25,9},{2,18},{10... | collective-permute-start | bytes 602120 | tf_op jit(solution)/shard_map/ppermute | solution.py:345
  9.3 0.8 copy.3.lists
  10.1 1.1 %links.1.refs_0_ = f32[10,128]{1,0:T(8,128)S(1)} custom-call(s32[64,4]{1,0:T(8,128)S(1)} %copy.3.lists), custom_call_target="tpu_custom_call" | custom-call | bytes 6144 | tf_op jit(solution)/shard_map/links/pallas_call | solution.py:363
  11.2 2.4 %collective-permute-done.refs_2_ = f32[392,128]{1,0:T(8,128)S(1)} collective-permute-done((f32[392,128]{1,0:T(8,128)S(1)}, f32[392,128]{1,0:T(8,128)S(1)}, u32[]{:S(2)}, u32[]{:S(2)}) %collective-permute-start) | collective-permute-done | bytes 200736 | tf_op jit(solution)/shard_map/ppermute | solution.py:341
  13.5 0.0 collective-permute-done.1.refs_3_
  13.5 0.4 collective-permute-done.3.refs_5_
  14.0 2.1 %assemble.2 = (f32[32,1,128]{2,1,0:T(1,128)}, f32[2,7,128,128]{3,2,1,0:T(8,128)S(1)}) custom-call(f32[10,128]{1,0:T(8,128)S(1)} %links.1.refs_0_, f32[2,4,128,128]{3,2,1,0:T(8,128)S(1)} %get-tuple-element.21.refs_1_, f32[392,128]{1,0:T(8,128)S(1)} %collective-permute-done.refs_2_, f32[392,128]{1,0:T(8,128)S(1)} %collective-permute-done.1.refs_3_, ...), custom_call_target="tpu_custom_call" | custom-call | flops 1207959552 | bytes 2266112 | tf_op jit(solution)/shard_map/assemble/pallas_call | solution.py:363
  16.1 5.7 %all-to-all-start = ((f32[32,1,128]{2,1,0:T(1,128)}), f32[32,1,128]{2,1,0:T(1,128)S(1)}, u32[]{:S(2)}, u32[]{:S(2)}) async-start(f32[32,1,128]{2,1,0:T(1,128)} %get-tuple-element.25), calls=%async_computation | async-start | bytes 32768 | tf_op jit(solution)/shard_map/all_to_all | solution.py:409
  21.7 2.3 %cube.2.source.refs_2_ = f32[2,17,128,128]{3,2,1,0:T(8,128)S(1)} custom-call(f32[2,7,128,128]{3,2,1,0:T(8,128)S(1)} %get-tuple-element.26.blocks), custom_call_target="tpu_custom_call" | custom-call | flops 2415919104 | bytes 3145728 | tf_op jit(solution)/shard_map/cube/pallas_call | solution.py:363
  24.1 4.7 %all-to-all-done.norms = f32[32,1,128]{2,1,0:T(1,128)S(1)} async-done(((f32[32,1,128]{2,1,0:T(1,128)}), f32[32,1,128]{2,1,0:T(1,128)S(1)}, u32[]{:S(2)}, u32[]{:S(2)}) %all-to-all-start) | async-done | bytes 16416 | tf_op jit(solution)/shard_map/all_to_all | solution.py:409
  28.8 9.3 %sign.2 = (f32[2,4,128,128]{3,2,1,0:T(8,128)S(1)}, f32[392,128]{1,0:T(8,128)S(1)}, f32[392,128]{1,0:T(8,128)S(1)}, f32[392,128]{1,0:T(8,128)S(1)}) custom-call(f32[32,1,128]{2,1,0:T(1,128)S(1)} %all-to-all-done.norms, f32[2,17,128,128]{3,2,1,0:T(8,128)S(1)} %cube.2.source.refs_2_), custom_call_target="tpu_custom_call" | custom-call | flops 9663676416 | bytes 3371008 | tf_op jit(solution)/shard_map/sign/pallas_call | solution.py:363
  38.0 0.7 collective-permute-start.4
  38.7 1.4 %collective-permute-start.5 = (f32[392,128]{1,0:T(8,128)S(1)}, f32[392,128]{1,0:T(8,128)S(1)}, u32[]{:S(2)}, u32[]{:S(2)}) collective-permute-start(f32[392,128]{1,0:T(8,128)S(1)} %get-tuple-element.29), channel_id=1, source_target_pairs={{0,7},{1,2},{2,1},{3,4},{4,3},{5,6},{6,5},{7,0},{8,15},{9,10},{10,... | collective-permute-start | bytes 602120 | tf_op jit(solution)/shard_map/ppermute | solution.py:342
  40.1 0.6 collective-permute-start.7
  40.7 8.4 %collective-permute-done.4.refs_3_ = f32[392,128]{1,0:T(8,128)S(1)} collective-permute-done((f32[392,128]{1,0:T(8,128)S(1)}, f32[392,128]{1,0:T(8,128)S(1)}, u32[]{:S(2)}, u32[]{:S(2)}) %collective-permute-start.4) | collective-permute-done | bytes 200736 | tf_op jit(solution)/shard_map/ppermute | solution.py:341
  49.2 2.3 %assemble.3 = (f32[32,1,128]{2,1,0:T(1,128)}, f32[2,7,128,128]{3,2,1,0:T(8,128)S(1)}) custom-call(f32[10,128]{1,0:T(8,128)S(1)} %links.1.refs_0_, f32[2,4,128,128]{3,2,1,0:T(8,128)S(1)} %get-tuple-element.27.refs_1_, f32[2,17,128,128]{3,2,1,0:T(8,128)S(1)} %cube.2.source.refs_2_, f32[392,128]{1,0:T(8,128)S(1)} %collective-permute-done.4.refs_3_, ...), custom_call_target="tpu_custom_call" | custom-call | flops 1207959552 | bytes 4494336 | tf_op jit(solution)/shard_map/assemble/pallas_call | solution.py:363
  51.5 2.5 %all-to-all-start.1 = ((f32[32,1,128]{2,1,0:T(1,128)}), f32[32,1,128]{2,1,0:T(1,128)S(1)}, u32[]{:S(2)}, u32[]{:S(2)}) async-start(f32[32,1,128]{2,1,0:T(1,128)} %get-tuple-element.31), calls=%async_computation.1 | async-start | bytes 32768 | tf_op jit(solution)/shard_map/all_to_all | solution.py:409
  54.0 2.3 %cube.3.source = f32[2,17,128,128]{3,2,1,0:T(8,128)S(1)} custom-call(f32[2,7,128,128]{3,2,1,0:T(8,128)S(1)} %get-tuple-element.32.blocks), custom_call_target="tpu_custom_call" | custom-call | flops 2415919104 | bytes 3145728 | tf_op jit(solution)/shard_map/cube/pallas_call | solution.py:363
  56.3 4.7 %all-to-all-done.1.norms = f32[32,1,128]{2,1,0:T(1,128)S(1)} async-done(((f32[32,1,128]{2,1,0:T(1,128)}), f32[32,1,128]{2,1,0:T(1,128)S(1)}, u32[]{:S(2)}, u32[]{:S(2)}) %all-to-all-start.1) | async-done | bytes 16416 | tf_op jit(solution)/shard_map/all_to_all | solution.py:409
  61.1 9.2 %sign.3 = (f32[2,4,128,128]{3,2,1,0:T(8,128)S(1)}, f32[256,128]{1,0:T(8,128)S(1)}, f32[256,128]{1,0:T(8,128)S(1)}, f32[256,128]{1,0:T(8,128)S(1)}) custom-call(f32[32,1,128]{2,1,0:T(1,128)S(1)} %all-to-all-done.1.norms, f32[2,17,128,128]{3,2,1,0:T(8,128)S(1)} %cube.3.source), custom_call_target="tpu_custom_call" | custom-call | flops 9663676416 | bytes 3162112 | tf_op jit(solution)/shard_map/sign/pallas_call | solution.py:363
  70.3 0.7 collective-permute-start.8
  71.0 1.4 %collective-permute-start.9 = (f32[256,128]{1,0:T(8,128)S(1)}, f32[256,128]{1,0:T(8,128)S(1)}, u32[]{:S(2)}, u32[]{:S(2)}) collective-permute-start(f32[256,128]{1,0:T(8,128)S(1)} %get-tuple-element.35), channel_id=1, source_target_pairs={{0,7},{1,2},{2,1},{3,4},{4,3},{5,6},{6,5},{7,0},{8,15},{9,10},{10,... | collective-permute-start | bytes 393224 | tf_op jit(solution)/shard_map/ppermute | solution.py:342
  72.3 0.6 collective-permute-start.11
  73.0 0.0 collective-permute-start.10
  73.0 3.6 %collective-permute-done.8.refs_2_ = f32[256,128]{1,0:T(8,128)S(1)} collective-permute-done((f32[256,128]{1,0:T(8,128)S(1)}, f32[256,128]{1,0:T(8,128)S(1)}, u32[]{:S(2)}, u32[]{:S(2)}) %collective-permute-start.8) | collective-permute-done | bytes 131104 | tf_op jit(solution)/shard_map/ppermute | solution.py:341
  76.5 2.1 %collective-permute-done.9.refs_3_ = f32[256,128]{1,0:T(8,128)S(1)} collective-permute-done((f32[256,128]{1,0:T(8,128)S(1)}, f32[256,128]{1,0:T(8,128)S(1)}, u32[]{:S(2)}, u32[]{:S(2)}) %collective-permute-start.9) | collective-permute-done | bytes 131104 | tf_op jit(solution)/shard_map/ppermute | solution.py:342
  78.6 0.0 collective-permute-done.11.refs_5_
  78.6 1.0 %density.1 = f32[2,4,128,128]{3,2,1,0:T(8,128)} custom-call(f32[10,128]{1,0:T(8,128)S(1)} %links.1.refs_0_, f32[2,4,128,128]{3,2,1,0:T(8,128)S(1)} %get-tuple-element.33.refs_1_, f32[256,128]{1,0:T(8,128)S(1)} %collective-permute-done.8.refs_2_, f32[256,128]{1,0:T(8,128)S(1)} %collective-permute-done.9.refs_3_, ...), custom_call_target="tpu_custom_call" | custom-call | bytes 1577984 | tf_op jit(solution)/shard_map/density/pallas_call | solution.py:363
  (8 shorter events, 0.0 us)
Async XLA Ops:
  0.0 1.0 %copy-start = (f32[2,4,128,128]{3,2,1,0:T(8,128)S(1)}, f32[2,4,128,128]{3,2,1,0:T(8,128)}, u32[]{:S(2)}) copy-start(f32[2,4,128,128]{3,2,1,0:T(8,128)} %own.1) | copy-start | bytes 1572868
  1.2 12.3 %collective-permute-start = (f32[392,128]{1,0:T(8,128)S(1)}, f32[392,128]{1,0:T(8,128)S(1)}, u32[]{:S(2)}, u32[]{:S(2)}) collective-permute-start(f32[392,128]{1,0:T(8,128)S(1)} %get-tuple-element.22), channel_id=1, source_target_pairs={{0,1},{1,0},{2,3},{3,2},{4,5},{5,4},{6,7},{7,6},{8,9},{9,8},{10,11... | collective-permute-start | bytes 602120 | tf_op jit(solution)/shard_map/ppermute | solution.py:341
  4.3 9.3 %collective-permute-start.1 = (f32[392,128]{1,0:T(8,128)S(1)}, f32[392,128]{1,0:T(8,128)S(1)}, u32[]{:S(2)}, u32[]{:S(2)}) collective-permute-start(f32[392,128]{1,0:T(8,128)S(1)} %get-tuple-element.23), channel_id=1, source_target_pairs={{0,7},{1,2},{2,1},{3,4},{4,3},{5,6},{6,5},{7,0},{8,15},{9,10},{10,... | collective-permute-start | bytes 602120 | tf_op jit(solution)/shard_map/ppermute | solution.py:342
  7.8 6.2 %collective-permute-start.3 = (f32[392,128]{1,0:T(8,128)S(1)}, f32[392,128]{1,0:T(8,128)S(1)}, u32[]{:S(2)}, u32[]{:S(2)}) collective-permute-start(f32[392,128]{1,0:T(8,128)S(1)} %get-tuple-element.24), channel_id=1, source_target_pairs={{0,16},{8,24},{16,0},{24,8},{1,17},{9,25},{17,1},{25,9},{2,18},{10... | collective-permute-start | bytes 602120 | tf_op jit(solution)/shard_map/ppermute | solution.py:345
  9.3 4.7 %collective-permute-start.2 = (f32[392,128]{1,0:T(8,128)S(1)}, f32[392,128]{1,0:T(8,128)S(1)}, u32[]{:S(2)}, u32[]{:S(2)}) collective-permute-start(f32[392,128]{1,0:T(8,128)S(1)} %get-tuple-element.24), channel_id=1, source_target_pairs={{0,8},{8,0},{16,24},{24,16},{1,9},{9,1},{17,25},{25,17},{2,10},{10... | collective-permute-start | bytes 602120 | tf_op jit(solution)/shard_map/ppermute | solution.py:345
  16.1 12.7 %all-to-all-start = ((f32[32,1,128]{2,1,0:T(1,128)}), f32[32,1,128]{2,1,0:T(1,128)S(1)}, u32[]{:S(2)}, u32[]{:S(2)}) async-start(f32[32,1,128]{2,1,0:T(1,128)} %get-tuple-element.25), calls=%async_computation | async-start | bytes 32768 | tf_op jit(solution)/shard_map/all_to_all | solution.py:409
  38.0 11.1 %collective-permute-start.4 = (f32[392,128]{1,0:T(8,128)S(1)}, f32[392,128]{1,0:T(8,128)S(1)}, u32[]{:S(2)}, u32[]{:S(2)}) collective-permute-start(f32[392,128]{1,0:T(8,128)S(1)} %get-tuple-element.28), channel_id=1, source_target_pairs={{0,1},{1,0},{2,3},{3,2},{4,5},{5,4},{6,7},{7,6},{8,9},{9,8},{10,11... | collective-permute-start | bytes 602120 | tf_op jit(solution)/shard_map/ppermute | solution.py:341
  38.7 10.4 %collective-permute-start.5 = (f32[392,128]{1,0:T(8,128)S(1)}, f32[392,128]{1,0:T(8,128)S(1)}, u32[]{:S(2)}, u32[]{:S(2)}) collective-permute-start(f32[392,128]{1,0:T(8,128)S(1)} %get-tuple-element.29), channel_id=1, source_target_pairs={{0,7},{1,2},{2,1},{3,4},{4,3},{5,6},{6,5},{7,0},{8,15},{9,10},{10,... | collective-permute-start | bytes 602120 | tf_op jit(solution)/shard_map/ppermute | solution.py:342
  40.1 9.0 %collective-permute-start.7 = (f32[392,128]{1,0:T(8,128)S(1)}, f32[392,128]{1,0:T(8,128)S(1)}, u32[]{:S(2)}, u32[]{:S(2)}) collective-permute-start(f32[392,128]{1,0:T(8,128)S(1)} %get-tuple-element.30), channel_id=1, source_target_pairs={{0,16},{8,24},{16,0},{24,8},{1,17},{9,25},{17,1},{25,9},{2,18},{10... | collective-permute-start | bytes 602120 | tf_op jit(solution)/shard_map/ppermute | solution.py:345
  40.7 8.4 %collective-permute-start.6 = (f32[392,128]{1,0:T(8,128)S(1)}, f32[392,128]{1,0:T(8,128)S(1)}, u32[]{:S(2)}, u32[]{:S(2)}) collective-permute-start(f32[392,128]{1,0:T(8,128)S(1)} %get-tuple-element.30), channel_id=1, source_target_pairs={{0,8},{8,0},{16,24},{24,16},{1,9},{9,1},{17,25},{25,17},{2,10},{10... | collective-permute-start | bytes 602120 | tf_op jit(solution)/shard_map/ppermute | solution.py:345
  51.5 9.6 %all-to-all-start.1 = ((f32[32,1,128]{2,1,0:T(1,128)}), f32[32,1,128]{2,1,0:T(1,128)S(1)}, u32[]{:S(2)}, u32[]{:S(2)}) async-start(f32[32,1,128]{2,1,0:T(1,128)} %get-tuple-element.31), calls=%async_computation.1 | async-start | bytes 32768 | tf_op jit(solution)/shard_map/all_to_all | solution.py:409
  70.3 6.2 %collective-permute-start.8 = (f32[256,128]{1,0:T(8,128)S(1)}, f32[256,128]{1,0:T(8,128)S(1)}, u32[]{:S(2)}, u32[]{:S(2)}) collective-permute-start(f32[256,128]{1,0:T(8,128)S(1)} %get-tuple-element.34), channel_id=1, source_target_pairs={{0,1},{1,0},{2,3},{3,2},{4,5},{5,4},{6,7},{7,6},{8,9},{9,8},{10,11... | collective-permute-start | bytes 393224 | tf_op jit(solution)/shard_map/ppermute | solution.py:341
  71.0 7.7 %collective-permute-start.9 = (f32[256,128]{1,0:T(8,128)S(1)}, f32[256,128]{1,0:T(8,128)S(1)}, u32[]{:S(2)}, u32[]{:S(2)}) collective-permute-start(f32[256,128]{1,0:T(8,128)S(1)} %get-tuple-element.35), channel_id=1, source_target_pairs={{0,7},{1,2},{2,1},{3,4},{4,3},{5,6},{6,5},{7,0},{8,15},{9,10},{10,... | collective-permute-start | bytes 393224 | tf_op jit(solution)/shard_map/ppermute | solution.py:342
  72.3 6.3 %collective-permute-start.11 = (f32[256,128]{1,0:T(8,128)S(1)}, f32[256,128]{1,0:T(8,128)S(1)}, u32[]{:S(2)}, u32[]{:S(2)}) collective-permute-start(f32[256,128]{1,0:T(8,128)S(1)} %get-tuple-element.36), channel_id=1, source_target_pairs={{0,16},{8,24},{16,0},{24,8},{1,17},{9,25},{17,1},{25,9},{2,18},{10... | collective-permute-start | bytes 393224 | tf_op jit(solution)/shard_map/ppermute | solution.py:345
  73.0 5.7 %collective-permute-start.10 = (f32[256,128]{1,0:T(8,128)S(1)}, f32[256,128]{1,0:T(8,128)S(1)}, u32[]{:S(2)}, u32[]{:S(2)}) collective-permute-start(f32[256,128]{1,0:T(8,128)S(1)} %get-tuple-element.36), channel_id=1, source_target_pairs={{0,8},{8,0},{16,24},{24,16},{1,9},{9,1},{17,25},{25,17},{2,10},{10... | collective-permute-start | bytes 393224 | tf_op jit(solution)/shard_map/ppermute | solution.py:345

commit v9 on v7

--- a/solution.py
+++ b/solution.py
@@ -38,7 +38,7 @@
     return pl.ds(first * SIDE, count * SIDE)
 
 
-STRIPS = (((0,), (0, 1)), ((1, 3), (1, 2)), ((2,), (2, 0)), ((3,), (3, 0)))
+STRIPS = (((1, 3), (1, 2)), ((0,), (0, 1)), ((2,), (2, 0)), ((3,), (3, 0)))
 PLACES = tuple((row, col) for rows, cols in STRIPS for row in rows for col in cols)
 
 

time: 79.9 us -> 79.9 us (level)
  no operation moved by 1% of the time
where the time goes in v9:
time: 79.9 us; the launch traced here: 79.7 us
  Pallas kernels  29.8 us (37%)
  waiting for transfers between devices  26.3 us (33%)
  starting transfers between devices  21.6 us (27%)
  local copies, waits for them, and re-layouts  1.81 us (2%)
    pallas_call x9, Pallas kernels, call(): pl.pallas_call(kernel, out_shape=list(outputs), in_specs=specs, out_specs...  29.8 us
    ppermute x3, waiting for transfers between devices, exchange(): received = [lax.ppermute(over_even, 'col', [(i, i ^ 1) for i in cols])]  14.3 us
    all_to_all x2, waiting for transfers between devices, per_device(): norms = lax.all_to_all(norms, ('row', 'col'), 0, 0, tiled=True)  9.44 us
    all_to_all x2, starting transfers between devices, per_device(): norms = lax.all_to_all(norms, ('row', 'col'), 0, 0, tiled=True)  8.21 us
    ppermute x3, starting transfers between devices, exchange(): received.append(lax.ppermute(over_odd, 'col', odd))  6.31 us
    ppermute x3, starting transfers between devices, exchange(): received = [lax.ppermute(over_even, 'col', [(i, i ^ 1) for i in cols])]  4.4 us
    ppermute x6, starting transfers between devices, exchange(): lax.ppermute(to_partner, 'row', [(i, i ^ place) for i in rows])  2.72 us
    ppermute x3, waiting for transfers between devices, exchange(): received.append(lax.ppermute(over_odd, 'col', odd))  2.11 us
  transfers between devices with their start and end apart: 14, of which 7 were waited for; matrix products, arithmetic and copies ran while one was open for 1% of the time, Pallas kernels for 7%

profile of v9, /device:TPU:0, one launch (start us, length us, event | category | flops | bytes accessed | tf_op | source)
XLA Modules:
  0.0 79.7 jit_solution(12006709792354373290)
XLA Ops:
  0.0 1.0 %copy-done = f32[2,4,128,128]{3,2,1,0:T(8,128)S(1)} copy-done((f32[2,4,128,128]{3,2,1,0:T(8,128)S(1)}, f32[2,4,128,128]{3,2,1,0:T(8,128)}, u32[]{:S(2)}) %copy-start) | copy-done | bytes 524312
  1.0 0.2 pack.1
  1.2 3.0 %collective-permute-start = (f32[392,128]{1,0:T(8,128)S(1)}, f32[392,128]{1,0:T(8,128)S(1)}, u32[]{:S(2)}, u32[]{:S(2)}) collective-permute-start(f32[392,128]{1,0:T(8,128)S(1)} %get-tuple-element.22), channel_id=1, source_target_pairs={{0,1},{1,0},{2,3},{3,2},{4,5},{5,4},{6,7},{7,6},{8,9},{9,8},{10,11... | collective-permute-start | bytes 602120 | tf_op jit(solution)/shard_map/ppermute | solution.py:341
  4.3 3.5 %collective-permute-start.1 = (f32[392,128]{1,0:T(8,128)S(1)}, f32[392,128]{1,0:T(8,128)S(1)}, u32[]{:S(2)}, u32[]{:S(2)}) collective-permute-start(f32[392,128]{1,0:T(8,128)S(1)} %get-tuple-element.23), channel_id=1, source_target_pairs={{0,7},{1,2},{2,1},{3,4},{4,3},{5,6},{6,5},{7,0},{8,15},{9,10},{10,... | collective-permute-start | bytes 602120 | tf_op jit(solution)/shard_map/ppermute | solution.py:342
  7.8 1.5 %collective-permute-start.3 = (f32[392,128]{1,0:T(8,128)S(1)}, f32[392,128]{1,0:T(8,128)S(1)}, u32[]{:S(2)}, u32[]{:S(2)}) collective-permute-start(f32[392,128]{1,0:T(8,128)S(1)} %get-tuple-element.24), channel_id=1, source_target_pairs={{0,16},{8,24},{16,0},{24,8},{1,17},{9,25},{17,1},{25,9},{2,18},{10... | collective-permute-start | bytes 602120 | tf_op jit(solution)/shard_map/ppermute | solution.py:345
  9.3 0.8 copy.3.lists
  10.1 1.1 %links.1.refs_0_ = f32[10,128]{1,0:T(8,128)S(1)} custom-call(s32[64,4]{1,0:T(8,128)S(1)} %copy.3.lists), custom_call_target="tpu_custom_call" | custom-call | bytes 6144 | tf_op jit(solution)/shard_map/links/pallas_call | solution.py:363
  11.2 2.4 %collective-permute-done.refs_2_ = f32[392,128]{1,0:T(8,128)S(1)} collective-permute-done((f32[392,128]{1,0:T(8,128)S(1)}, f32[392,128]{1,0:T(8,128)S(1)}, u32[]{:S(2)}, u32[]{:S(2)}) %collective-permute-start) | collective-permute-done | bytes 200736 | tf_op jit(solution)/shard_map/ppermute | solution.py:341
  13.5 0.0 collective-permute-done.1.refs_3_
  13.5 0.4 collective-permute-done.3.refs_5_
  14.0 2.1 %assemble.2 = (f32[32,1,128]{2,1,0:T(1,128)}, f32[2,7,128,128]{3,2,1,0:T(8,128)S(1)}) custom-call(f32[10,128]{1,0:T(8,128)S(1)} %links.1.refs_0_, f32[2,4,128,128]{3,2,1,0:T(8,128)S(1)} %get-tuple-element.21.refs_1_, f32[392,128]{1,0:T(8,128)S(1)} %collective-permute-done.refs_2_, f32[392,128]{1,0:T(8,128)S(1)} %collective-permute-done.1.refs_3_, ...), custom_call_target="tpu_custom_call" | custom-call | flops 1207959552 | bytes 2266112 | tf_op jit(solution)/shard_map/assemble/pallas_call | solution.py:363
  16.1 5.7 %all-to-all-start = ((f32[32,1,128]{2,1,0:T(1,128)}), f32[32,1,128]{2,1,0:T(1,128)S(1)}, u32[]{:S(2)}, u32[]{:S(2)}) async-start(f32[32,1,128]{2,1,0:T(1,128)} %get-tuple-element.25), calls=%async_computation | async-start | bytes 32768 | tf_op jit(solution)/shard_map/all_to_all | solution.py:409
  21.7 2.3 %cube.2.source.refs_2_ = f32[2,17,128,128]{3,2,1,0:T(8,128)S(1)} custom-call(f32[2,7,128,128]{3,2,1,0:T(8,128)S(1)} %get-tuple-element.26.blocks), custom_call_target="tpu_custom_call" | custom-call | flops 2415919104 | bytes 3145728 | tf_op jit(solution)/shard_map/cube/pallas_call | solution.py:363
  24.0 4.7 %all-to-all-done.norms = f32[32,1,128]{2,1,0:T(1,128)S(1)} async-done(((f32[32,1,128]{2,1,0:T(1,128)}), f32[32,1,128]{2,1,0:T(1,128)S(1)}, u32[]{:S(2)}, u32[]{:S(2)}) %all-to-all-start) | async-done | bytes 16416 | tf_op jit(solution)/shard_map/all_to_all | solution.py:409
  28.8 9.2 %sign.2 = (f32[2,4,128,128]{3,2,1,0:T(8,128)S(1)}, f32[392,128]{1,0:T(8,128)S(1)}, f32[392,128]{1,0:T(8,128)S(1)}, f32[392,128]{1,0:T(8,128)S(1)}) custom-call(f32[32,1,128]{2,1,0:T(1,128)S(1)} %all-to-all-done.norms, f32[2,17,128,128]{3,2,1,0:T(8,128)S(1)} %cube.2.source.refs_2_), custom_call_target="tpu_custom_call" | custom-call | flops 9663676416 | bytes 3371008 | tf_op jit(solution)/shard_map/sign/pallas_call | solution.py:363
  38.0 0.7 collective-permute-start.4
  38.7 1.4 %collective-permute-start.5 = (f32[392,128]{1,0:T(8,128)S(1)}, f32[392,128]{1,0:T(8,128)S(1)}, u32[]{:S(2)}, u32[]{:S(2)}) collective-permute-start(f32[392,128]{1,0:T(8,128)S(1)} %get-tuple-element.29), channel_id=1, source_target_pairs={{0,7},{1,2},{2,1},{3,4},{4,3},{5,6},{6,5},{7,0},{8,15},{9,10},{10,... | collective-permute-start | bytes 602120 | tf_op jit(solution)/shard_map/ppermute | solution.py:342
  40.1 0.6 collective-permute-start.7
  40.7 8.4 %collective-permute-done.4.refs_3_ = f32[392,128]{1,0:T(8,128)S(1)} collective-permute-done((f32[392,128]{1,0:T(8,128)S(1)}, f32[392,128]{1,0:T(8,128)S(1)}, u32[]{:S(2)}, u32[]{:S(2)}) %collective-permute-start.4) | collective-permute-done | bytes 200736 | tf_op jit(solution)/shard_map/ppermute | solution.py:341
  49.1 0.0 collective-permute-done.5.refs_4_
  49.1 0.0 collective-permute-done.7.refs_6_
  49.1 2.3 %assemble.3 = (f32[32,1,128]{2,1,0:T(1,128)}, f32[2,7,128,128]{3,2,1,0:T(8,128)S(1)}) custom-call(f32[10,128]{1,0:T(8,128)S(1)} %links.1.refs_0_, f32[2,4,128,128]{3,2,1,0:T(8,128)S(1)} %get-tuple-element.27.refs_1_, f32[2,17,128,128]{3,2,1,0:T(8,128)S(1)} %cube.2.source.refs_2_, f32[392,128]{1,0:T(8,128)S(1)} %collective-permute-done.4.refs_3_, ...), custom_call_target="tpu_custom_call" | custom-call | flops 1207959552 | bytes 4494336 | tf_op jit(solution)/shard_map/assemble/pallas_call | solution.py:363
  51.4 2.5 %all-to-all-start.1 = ((f32[32,1,128]{2,1,0:T(1,128)}), f32[32,1,128]{2,1,0:T(1,128)S(1)}, u32[]{:S(2)}, u32[]{:S(2)}) async-start(f32[32,1,128]{2,1,0:T(1,128)} %get-tuple-element.31), calls=%async_computation.1 | async-start | bytes 32768 | tf_op jit(solution)/shard_map/all_to_all | solution.py:409
  54.0 2.3 %cube.3.source = f32[2,17,128,128]{3,2,1,0:T(8,128)S(1)} custom-call(f32[2,7,128,128]{3,2,1,0:T(8,128)S(1)} %get-tuple-element.32.blocks), custom_call_target="tpu_custom_call" | custom-call | flops 2415919104 | bytes 3145728 | tf_op jit(solution)/shard_map/cube/pallas_call | solution.py:363
  56.3 4.7 %all-to-all-done.1.norms = f32[32,1,128]{2,1,0:T(1,128)S(1)} async-done(((f32[32,1,128]{2,1,0:T(1,128)}), f32[32,1,128]{2,1,0:T(1,128)S(1)}, u32[]{:S(2)}, u32[]{:S(2)}) %all-to-all-start.1) | async-done | bytes 16416 | tf_op jit(solution)/shard_map/all_to_all | solution.py:409
  61.0 9.3 %sign.3 = (f32[2,4,128,128]{3,2,1,0:T(8,128)S(1)}, f32[256,128]{1,0:T(8,128)S(1)}, f32[256,128]{1,0:T(8,128)S(1)}, f32[256,128]{1,0:T(8,128)S(1)}) custom-call(f32[32,1,128]{2,1,0:T(1,128)S(1)} %all-to-all-done.1.norms, f32[2,17,128,128]{3,2,1,0:T(8,128)S(1)} %cube.3.source), custom_call_target="tpu_custom_call" | custom-call | flops 9663676416 | bytes 3162112 | tf_op jit(solution)/shard_map/sign/pallas_call | solution.py:363
  70.3 0.7 collective-permute-start.8
  71.0 1.4 %collective-permute-start.9 = (f32[256,128]{1,0:T(8,128)S(1)}, f32[256,128]{1,0:T(8,128)S(1)}, u32[]{:S(2)}, u32[]{:S(2)}) collective-permute-start(f32[256,128]{1,0:T(8,128)S(1)} %get-tuple-element.35), channel_id=1, source_target_pairs={{0,7},{1,2},{2,1},{3,4},{4,3},{5,6},{6,5},{7,0},{8,15},{9,10},{10,... | collective-permute-start | bytes 393224 | tf_op jit(solution)/shard_map/ppermute | solution.py:342
  72.4 0.6 collective-permute-start.11
  73.0 3.6 %collective-permute-done.8.refs_2_ = f32[256,128]{1,0:T(8,128)S(1)} collective-permute-done((f32[256,128]{1,0:T(8,128)S(1)}, f32[256,128]{1,0:T(8,128)S(1)}, u32[]{:S(2)}, u32[]{:S(2)}) %collective-permute-start.8) | collective-permute-done | bytes 131104 | tf_op jit(solution)/shard_map/ppermute | solution.py:341
  76.6 2.1 %collective-permute-done.9.refs_3_ = f32[256,128]{1,0:T(8,128)S(1)} collective-permute-done((f32[256,128]{1,0:T(8,128)S(1)}, f32[256,128]{1,0:T(8,128)S(1)}, u32[]{:S(2)}, u32[]{:S(2)}) %collective-permute-start.9) | collective-permute-done | bytes 131104 | tf_op jit(solution)/shard_map/ppermute | solution.py:342
  78.7 1.0 %density.1 = f32[2,4,128,128]{3,2,1,0:T(8,128)} custom-call(f32[10,128]{1,0:T(8,128)S(1)} %links.1.refs_0_, f32[2,4,128,128]{3,2,1,0:T(8,128)S(1)} %get-tuple-element.33.refs_1_, f32[256,128]{1,0:T(8,128)S(1)} %collective-permute-done.8.refs_2_, f32[256,128]{1,0:T(8,128)S(1)} %collective-permute-done.9.refs_3_, ...), custom_call_target="tpu_custom_call" | custom-call | bytes 1577984 | tf_op jit(solution)/shard_map/density/pallas_call | solution.py:363
  (8 shorter events, 0.0 us)
Async XLA Ops:
  0.0 1.0 %copy-start = (f32[2,4,128,128]{3,2,1,0:T(8,128)S(1)}, f32[2,4,128,128]{3,2,1,0:T(8,128)}, u32[]{:S(2)}) copy-start(f32[2,4,128,128]{3,2,1,0:T(8,128)} %own.1) | copy-start | bytes 1572868
  1.2 12.3 %collective-permute-start = (f32[392,128]{1,0:T(8,128)S(1)}, f32[392,128]{1,0:T(8,128)S(1)}, u32[]{:S(2)}, u32[]{:S(2)}) collective-permute-start(f32[392,128]{1,0:T(8,128)S(1)} %get-tuple-element.22), channel_id=1, source_target_pairs={{0,1},{1,0},{2,3},{3,2},{4,5},{5,4},{6,7},{7,6},{8,9},{9,8},{10,11... | collective-permute-start | bytes 602120 | tf_op jit(solution)/shard_map/ppermute | solution.py:341
  4.3 9.3 %collective-permute-start.1 = (f32[392,128]{1,0:T(8,128)S(1)}, f32[392,128]{1,0:T(8,128)S(1)}, u32[]{:S(2)}, u32[]{:S(2)}) collective-permute-start(f32[392,128]{1,0:T(8,128)S(1)} %get-tuple-element.23), channel_id=1, source_target_pairs={{0,7},{1,2},{2,1},{3,4},{4,3},{5,6},{6,5},{7,0},{8,15},{9,10},{10,... | collective-permute-start | bytes 602120 | tf_op jit(solution)/shard_map/ppermute | solution.py:342
  7.8 6.2 %collective-permute-start.3 = (f32[392,128]{1,0:T(8,128)S(1)}, f32[392,128]{1,0:T(8,128)S(1)}, u32[]{:S(2)}, u32[]{:S(2)}) collective-permute-start(f32[392,128]{1,0:T(8,128)S(1)} %get-tuple-element.24), channel_id=1, source_target_pairs={{0,16},{8,24},{16,0},{24,8},{1,17},{9,25},{17,1},{25,9},{2,18},{10... | collective-permute-start | bytes 602120 | tf_op jit(solution)/shard_map/ppermute | solution.py:345
  9.3 4.7 %collective-permute-start.2 = (f32[392,128]{1,0:T(8,128)S(1)}, f32[392,128]{1,0:T(8,128)S(1)}, u32[]{:S(2)}, u32[]{:S(2)}) collective-permute-start(f32[392,128]{1,0:T(8,128)S(1)} %get-tuple-element.24), channel_id=1, source_target_pairs={{0,8},{8,0},{16,24},{24,16},{1,9},{9,1},{17,25},{25,17},{2,10},{10... | collective-permute-start | bytes 602120 | tf_op jit(solution)/shard_map/ppermute | solution.py:345
  16.1 12.7 %all-to-all-start = ((f32[32,1,128]{2,1,0:T(1,128)}), f32[32,1,128]{2,1,0:T(1,128)S(1)}, u32[]{:S(2)}, u32[]{:S(2)}) async-start(f32[32,1,128]{2,1,0:T(1,128)} %get-tuple-element.25), calls=%async_computation | async-start | bytes 32768 | tf_op jit(solution)/shard_map/all_to_all | solution.py:409
  38.0 11.1 %collective-permute-start.4 = (f32[392,128]{1,0:T(8,128)S(1)}, f32[392,128]{1,0:T(8,128)S(1)}, u32[]{:S(2)}, u32[]{:S(2)}) collective-permute-start(f32[392,128]{1,0:T(8,128)S(1)} %get-tuple-element.28), channel_id=1, source_target_pairs={{0,1},{1,0},{2,3},{3,2},{4,5},{5,4},{6,7},{7,6},{8,9},{9,8},{10,11... | collective-permute-start | bytes 602120 | tf_op jit(solution)/shard_map/ppermute | solution.py:341
  38.7 10.4 %collective-permute-start.5 = (f32[392,128]{1,0:T(8,128)S(1)}, f32[392,128]{1,0:T(8,128)S(1)}, u32[]{:S(2)}, u32[]{:S(2)}) collective-permute-start(f32[392,128]{1,0:T(8,128)S(1)} %get-tuple-element.29), channel_id=1, source_target_pairs={{0,7},{1,2},{2,1},{3,4},{4,3},{5,6},{6,5},{7,0},{8,15},{9,10},{10,... | collective-permute-start | bytes 602120 | tf_op jit(solution)/shard_map/ppermute | solution.py:342
  40.1 9.0 %collective-permute-start.7 = (f32[392,128]{1,0:T(8,128)S(1)}, f32[392,128]{1,0:T(8,128)S(1)}, u32[]{:S(2)}, u32[]{:S(2)}) collective-permute-start(f32[392,128]{1,0:T(8,128)S(1)} %get-tuple-element.30), channel_id=1, source_target_pairs={{0,16},{8,24},{16,0},{24,8},{1,17},{9,25},{17,1},{25,9},{2,18},{10... | collective-permute-start | bytes 602120 | tf_op jit(solution)/shard_map/ppermute | solution.py:345
  40.7 8.4 %collective-permute-start.6 = (f32[392,128]{1,0:T(8,128)S(1)}, f32[392,128]{1,0:T(8,128)S(1)}, u32[]{:S(2)}, u32[]{:S(2)}) collective-permute-start(f32[392,128]{1,0:T(8,128)S(1)} %get-tuple-element.30), channel_id=1, source_target_pairs={{0,8},{8,0},{16,24},{24,16},{1,9},{9,1},{17,25},{25,17},{2,10},{10... | collective-permute-start | bytes 602120 | tf_op jit(solution)/shard_map/ppermute | solution.py:345
  51.4 9.6 %all-to-all-start.1 = ((f32[32,1,128]{2,1,0:T(1,128)}), f32[32,1,128]{2,1,0:T(1,128)S(1)}, u32[]{:S(2)}, u32[]{:S(2)}) async-start(f32[32,1,128]{2,1,0:T(1,128)} %get-tuple-element.31), calls=%async_computation.1 | async-start | bytes 32768 | tf_op jit(solution)/shard_map/all_to_all | solution.py:409
  70.3 6.2 %collective-permute-start.8 = (f32[256,128]{1,0:T(8,128)S(1)}, f32[256,128]{1,0:T(8,128)S(1)}, u32[]{:S(2)}, u32[]{:S(2)}) collective-permute-start(f32[256,128]{1,0:T(8,128)S(1)} %get-tuple-element.34), channel_id=1, source_target_pairs={{0,1},{1,0},{2,3},{3,2},{4,5},{5,4},{6,7},{7,6},{8,9},{9,8},{10,11... | collective-permute-start | bytes 393224 | tf_op jit(solution)/shard_map/ppermute | solution.py:341
  71.0 7.7 %collective-permute-start.9 = (f32[256,128]{1,0:T(8,128)S(1)}, f32[256,128]{1,0:T(8,128)S(1)}, u32[]{:S(2)}, u32[]{:S(2)}) collective-permute-start(f32[256,128]{1,0:T(8,128)S(1)} %get-tuple-element.35), channel_id=1, source_target_pairs={{0,7},{1,2},{2,1},{3,4},{4,3},{5,6},{6,5},{7,0},{8,15},{9,10},{10,... | collective-permute-start | bytes 393224 | tf_op jit(solution)/shard_map/ppermute | solution.py:342
  72.4 6.3 %collective-permute-start.11 = (f32[256,128]{1,0:T(8,128)S(1)}, f32[256,128]{1,0:T(8,128)S(1)}, u32[]{:S(2)}, u32[]{:S(2)}) collective-permute-start(f32[256,128]{1,0:T(8,128)S(1)} %get-tuple-element.36), channel_id=1, source_target_pairs={{0,16},{8,24},{16,0},{24,8},{1,17},{9,25},{17,1},{25,9},{2,18},{10... | collective-permute-start | bytes 393224 | tf_op jit(solution)/shard_map/ppermute | solution.py:345
  73.0 5.7 %collective-permute-start.10 = (f32[256,128]{1,0:T(8,128)S(1)}, f32[256,128]{1,0:T(8,128)S(1)}, u32[]{:S(2)}, u32[]{:S(2)}) collective-permute-start(f32[256,128]{1,0:T(8,128)S(1)} %get-tuple-element.36), channel_id=1, source_target_pairs={{0,8},{8,0},{16,24},{24,16},{1,9},{9,1},{17,25},{25,17},{2,10},{10... | collective-permute-start | bytes 393224 | tf_op jit(solution)/shard_map/ppermute | solution.py:345
